TPU v7x, 32 devices: a whole 2x2x4 slice. The times are simulated.
32 devices in a mesh: blk: 32 (over z, y, x, core).
Axes of the slice: x: 2, y: 2, z: 4, core: 2. Of those that a mesh axis runs over, the one named last changes fastest.
Arguments:
- traces: bfloat16 [4096, 144, 128], P('blk')
- bands: int32 [64], replicated, may hold values from 0 to 7, never falling along the last dimension, each value on 1 to 16 neighbouring positions
Outputs:
- cross_spectra: bfloat16 [4096, 2, 2, 64, 128], P('blk')
Inputs may be any that keep to these rules, and one draw needn't show every extreme that they name: `bands`: band numbers never fall along the bins; every band holds 1 to 16 bins and one holds exactly 16.
All inputs are finite; a program needn't handle non-finite values.
Results may differ from a plain program's by a relative error of at most 0.024.
Values may be sent and summed in bfloat16 or wider, within the bound.
No kernel may reach another device: no remote copies, remote signals or barrier semaphores. Data moves between devices by JAX's collectives and lax.ppermute only.
A program may use at most 128 MiB of HBM per device.

v0:
```python
import math

import jax
import jax.numpy as jnp
from jax import lax
from jax.sharding import PartitionSpec as P

HW = 16
RAM_HALF = 64
ROUNDS = 2


epsilon = 1e-05
floor_power = 0.25


def with_halo(cells, sides, width):
    for axis, dim in sides:
        count = lax.axis_size(axis)
        ends = count - 1
        head = lax.slice_in_dim(cells, 0, width, axis=dim)
        tail = lax.slice_in_dim(cells, cells.shape[dim] - width, cells.shape[dim], axis=dim)
        cells = jnp.concatenate(
            [
                lax.ppermute(tail, axis, [(i, (i + 1) % count) for i in range(ends)]),
                cells,
                lax.ppermute(head, axis, [((i + 1) % count, i) for i in range(ends)]),
            ],
            axis=dim,
        )
    return cells


def shifted(shard, axis, by):
    count = lax.axis_size(axis)
    return lax.ppermute(shard, axis, [(i, (i + by) % count) for i in range(count)])


def prepare(extended, first_channel, total_channels, bands, halo_width, ram_half):
    channel_count = extended.shape[0] - 2 * halo_width
    ext_rows = extended.shape[0]
    window_count = extended.shape[1]
    samples = extended.shape[2]
    bin_count = samples // 2
    inner = jnp.arange(channel_count, dtype=jnp.int32)
    outer = jnp.arange(ext_rows, dtype=jnp.int32)
    offset = outer[None, :] - inner[:, None]
    outer_position = first_channel - halo_width + outer
    inside = (outer_position >= 0) & (outer_position < total_channels)
    selector = (offset >= 0) & (offset <= 2 * halo_width) & inside[None, :]
    neighbour_count = jnp.sum(selector.astype(jnp.float32), axis=1)
    neighbour_sum = jnp.einsum(
        "ie,ewl->iwl", selector.astype(jnp.bfloat16), extended, preferred_element_type=jnp.float32
    )
    centred = (
        extended[halo_width : halo_width + channel_count].astype(jnp.float32)
        - neighbour_sum / neighbour_count[:, None, None]
    )
    balanced = centred.astype(jnp.bfloat16)
    magnitude = jnp.abs(balanced)
    sample_index = jnp.arange(samples, dtype=jnp.int32)
    ram_band = jnp.abs(sample_index[:, None] - sample_index[None, :]) <= ram_half
    ram_count = jnp.sum(ram_band.astype(jnp.float32), axis=0)
    ram_sum = jnp.einsum(
        "cwl,lm->cwm", magnitude, ram_band.astype(jnp.bfloat16), preferred_element_type=jnp.float32
    )
    envelope = ram_sum / ram_count + epsilon
    normalized = (balanced.astype(jnp.float32) / envelope).astype(jnp.bfloat16)
    frequency = jnp.arange(1, bin_count + 1, dtype=jnp.int32)
    phase_steps = frequency[:, None] * sample_index[None, :] % samples
    phase = 2.0 * math.pi / samples * phase_steps.astype(jnp.float32)
    dft_table = (
        jnp.concatenate([jnp.cos(phase), -jnp.sin(phase)], axis=0) / math.sqrt(samples)
    ).astype(jnp.bfloat16)
    spectra = jnp.einsum("jl,cwl->jwc", dft_table, normalized, preferred_element_type=jnp.float32)
    spectra = spectra.reshape(2, bin_count, window_count, channel_count)
    power_bins = spectra[0] * spectra[0] + spectra[1] * spectra[1]
    same_band = (bands[:, None] == bands[None, :]).astype(jnp.float32)
    band_matrix = same_band / jnp.sum(same_band, axis=1, keepdims=True)
    band_mean = jnp.einsum("fg,gwc->fwc", band_matrix, power_bins, precision=lax.Precision.HIGHEST)
    whiten_scale = lax.rsqrt(jnp.maximum(band_mean, floor_power))
    return (spectra * whiten_scale[None]).astype(jnp.bfloat16)


def correlate(own_block, partner):
    flipped = jnp.stack([jnp.stack([partner[0], partner[1]]), jnp.stack([-partner[1], partner[0]])])
    window_count = own_block.shape[2]
    product = jnp.einsum("kfwc,okfwd->cofd", own_block, flipped, preferred_element_type=jnp.float32)
    return (product / math.sqrt(window_count)).astype(jnp.bfloat16)


def per_device(traces, bands):
    extended = with_halo(traces, (("blk", 0),), HW)
    channel_count = traces.shape[0]
    block_count = lax.axis_size("blk")
    first_channel = lax.axis_index("blk") * channel_count
    own_block = prepare(extended, first_channel, channel_count * block_count, bands, HW, RAM_HALF)
    results = []
    for round_index in range(ROUNDS):
        partner = shifted(own_block, "blk", -(round_index + 1))
        results.append(correlate(own_block, partner))
    return jnp.stack(results, axis=1)


def solution(mesh):
    placed = (P("blk", None, None), P())
    return jax.shard_map(
        per_device,
        mesh=mesh,
        in_specs=placed,
        out_specs=P("blk", None, None, None, None),
        check_vma=False,
    )
```

profile of v0, /device:TPU:1, one launch (start us, length us, event | category | flops | bytes accessed | tf_op | source)
XLA Modules:
  0.0 260.4 jit_solution(7440640829816025525)
XLA Ops:
  0.0 0.0 copy-start.2
  0.0 3.6 %copy.12 = bf16[128,144,128]{2,0,1:T(8,128)(2,1)S(1)} copy(bf16[128,144,128]{2,1,0:T(8,128)(2,1)} %param.2) | data formatting | bytes 9437184 | tf_op args[0]
  3.6 0.0 copy-start
  3.6 2.2 copy-done
  5.8 0.2 fusion.76
  6.0 4.5 %collective-permute-start = (bf16[16,144,128]{2,0,1:T(8,128)(2,1)S(1)}, bf16[16,144,128]{2,0,1:T(8,128)(2,1)S(1)}, u32[]{:S(2)}, u32[]{:S(2)}) collective-permute-start(bf16[16,144,128]{2,0,1:T(8,128)(2,1)S(1)} %get-tuple-element.9), channel_id=1, source_target_pairs={{0,1},{1,2},{2,3},{3,4},{4,5},{5,6},{6,7},{7,8},{8,9},{9,10},{10,1... | collective-permute-start | bytes 1769480 | tf_op jit(solution)/shard_map/ppermute | solution.py:25
  10.5 1.9 collective-permute-start.1
  12.5 0.0 copy-done.2
  12.5 0.2 convert_reduce_fusion.2
  12.7 0.1 convert_reduce_fusion
  12.8 0.2 fusion.63
  13.0 10.6 %collective-permute-done = bf16[16,144,128]{2,0,1:T(8,128)(2,1)S(1)} collective-permute-done((bf16[16,144,128]{2,0,1:T(8,128)(2,1)S(1)}, bf16[16,144,128]{2,0,1:T(8,128)(2,1)S(1)}, u32[]{:S(2)}, u32[]{:S(2)}) %collective-permute-start) | collective-permute-done | bytes 589856 | tf_op jit(solution)/shard_map/ppermute | solution.py:25
  23.6 1.6 collective-permute-done.1
  25.3 7.5 %fusion.9 = f32[128,144,128]{2,0,1:T(8,128)} fusion(bf16[16,144,128]{2,0,1:T(8,128)(2,1)S(1)} %collective-permute-done.1, bf16[128,144,128]{2,0,1:T(8,128)(2,1)} %copy-done, bf16[16,144,128]{2,0,1:T(8,128)(2,1)S(1)} %collective-permute-done, pred[160]{0:T(512)(128)(4,1)S(1)} %compare_and_fusion), kind=kOutput, calls=%fused_computation.16 | convolution fusion | flops 772771840 | bytes 15335584 | tf_op jit(solution)/shard_map/ie,ewl->iwl/dot_general | solution.py:52
  32.8 15.9 %fusion.22 = f32[128,144,128]{0,2,1:T(8,128)} fusion(f32[128]{0:T(128)S(1)} %convert_reduce_fusion.1, f32[128,144,128]{2,0,1:T(8,128)} %fusion.9, f32[128]{0:T(128)S(1)} %convert_reduce_fusion, f32[64,128]{1,0:T(8,128)S(1)} %get-tuple-element.12, f32[64,128]{1,0:T(8,128)S(1)} %get-tuple-element.11, bf16[128,144,128]{2,1,0:T(8,128)(2,1)} %param.2), kind=kOutput, calls=%fused_computation.33 | convolution fusion | flops 1241088000 | bytes 23659520 | tf_op jit(solution)/shard_map/jl,cwl->jwc/dot_general | solution.py:75
  48.7 7.0 %maximum_rsqrt_fusion = f32[64,144,128]{2,0,1:T(8,128)S(1)} fusion(f32[128,144,128]{2,0,1:T(8,128)} %bitcast.57, f32[64]{0:T(128)S(1)} %convert_reduce_fusion.2, s32[64]{0:T(128)S(1)} %copy-done.2), kind=kOutput, calls=%fused_computation.30 | convolution fusion | flops 910700544 | bytes 14157312 | tf_op jit(solution)/shard_map/fg,gwc->fwc/dot_general | solution.py:80
  55.7 2.7 %copy.16 = f32[64,144,128]{2,1,0:T(8,128)S(1)} copy(f32[64,144,128]{2,0,1:T(8,128)S(1)} %maximum_rsqrt_fusion) | data formatting | bytes 9437184 | tf_op jit(solution)/shard_map/rsqrt | solution.py:81
  58.5 12.0 %fusion.6 = bf16[2,64,144,128]{3,2,0,1:T(8,128)(2,1)} fusion(f32[2,64,144,128]{3,1,0,2:T(8,128)} %bitcast.58, f32[64,144,128]{2,1,0:T(8,128)S(1)} %copy.16), kind=kLoop, calls=%fused_computation.8 | loop fusion | flops 4718592 | bytes 18874368 | tf_op jit(solution)/shard_map/convert_element_type | solution.py:82
  70.5 0.0 collective-permute-start.3
  70.5 4.1 %collective-permute-start.2 = (bf16[2,64,144,128]{3,2,0,1:T(8,128)(2,1)}, bf16[2,64,144,128]{3,2,0,1:T(8,128)(2,1)}, u32[]{:S(2)}, u32[]{:S(2)}) collective-permute-start(bf16[2,64,144,128]{3,2,0,1:T(8,128)(2,1)} %fusion.6), channel_id=1, source_target_pairs={{0,31},{1,0},{2,1},{3,2},{4,3},{5,4},{6,5},{7,6},{8,7},{9,8},{10,9... | collective-permute-start | bytes 14155784 | tf_op jit(solution)/shard_map/ppermute | solution.py:36
  74.6 99.6 %collective-permute-done.3 = bf16[2,64,144,128]{3,2,0,1:T(8,128)(2,1)S(1)} collective-permute-done((bf16[2,64,144,128]{3,2,0,1:T(8,128)(2,1)}, bf16[2,64,144,128]{3,2,0,1:T(8,128)(2,1)S(1)}, u32[]{:S(2)}, u32[]{:S(2)}) %collective-permute-start.3) | collective-permute-done | bytes 4718624 | tf_op jit(solution)/shard_map/ppermute | solution.py:36
  174.2 0.0 copy-start.1
  174.2 0.5 slice_negate_fusion
  174.7 1.8 copy-done.1
  176.5 2.6 maximum_bitcast_fusion.1
  179.0 10.7 %fusion.24 = bf16[128,1,2,64,128]{0,4,2,3,1:T(8,128)(2,1)} fusion(bf16[2,64,144,128]{3,2,0,1:T(8,128)(2,1)} %fusion.6, bf16[1,2,64,144,128]{4,3,1,2,0:T(8,128)(2,1)} %maximum_bitcast_fusion.1, bf16[1,2,64,144,128]{4,3,1,2,0:T(8,128)(2,1)} %bitcast.59), kind=kOutput, calls=%fused_computation.35 | convolution fusion | flops 1216872448 | bytes 18350080 | tf_op jit(solution)/shard_map/kfwc,okfwd->cofd/dot_general | solution.py:88
  189.8 34.8 %collective-permute-done.2 = bf16[2,64,144,128]{3,2,0,1:T(8,128)(2,1)} collective-permute-done((bf16[2,64,144,128]{3,2,0,1:T(8,128)(2,1)}, bf16[2,64,144,128]{3,2,0,1:T(8,128)(2,1)}, u32[]{:S(2)}, u32[]{:S(2)}) %collective-permute-start.2) | collective-permute-done | bytes 4718624 | tf_op jit(solution)/shard_map/ppermute | solution.py:36
  224.6 2.8 %slice_negate_fusion.1 = (bf16[1,64,144,128]{3,2,0,1:T(8,128)(2,1)S(1)}, bf16[1,64,144,128]{3,2,0,1:T(8,128)(2,1)S(1)}) fusion(bf16[2,64,144,128]{3,2,0,1:T(8,128)(2,1)} %collective-permute-done.2), kind=kLoop, calls=%fused_computation.37 | loop fusion | flops 1179648 | bytes 9437184 | tf_op jit(solution)/shard_map/neg | solution.py:86
  227.4 2.6 maximum_bitcast_fusion
  230.0 11.1 %fusion.23 = bf16[128,1,2,64,128]{0,4,2,3,1:T(8,128)(2,1)} fusion(bf16[2,64,144,128]{3,2,0,1:T(8,128)(2,1)} %fusion.6, bf16[1,2,64,144,128]{4,3,1,0,2:T(8,128)(2,1)} %maximum_bitcast_fusion, bf16[1,2,64,144,128]{4,3,1,0,2:T(8,128)(2,1)} %bitcast.7), kind=kOutput, calls=%fused_computation.34 | convolution fusion | flops 1216872448 | bytes 18350080 | tf_op jit(solution)/shard_map/kfwc,okfwd->cofd/dot_general | solution.py:88
  241.1 7.5 %pad_maximum_fusion.1 = bf16[128,2,2,64,128]{0,4,2,3,1:T(8,128)(2,1)} fusion(bf16[128,1,2,64,128]{0,4,2,3,1:T(8,128)(2,1)} %fusion.24, bf16[128,1,2,64,128]{0,4,2,3,1:T(8,128)(2,1)} %fusion.23), kind=kLoop, calls=%fused_computation.11 | loop fusion | flops 4194304 | bytes 16777216 | tf_op jit(solution)/shard_map/stack | solution.py:102
  248.5 11.9 %copy.20 = bf16[128,2,2,64,128]{4,3,2,1,0:T(8,128)(2,1)} copy(bf16[128,2,2,64,128]{0,4,2,3,1:T(8,128)(2,1)} %pad_maximum_fusion.1) | data formatting | bytes 16777216 | tf_op jit(solution)/shard_map/stack | solution.py:102
  (3 shorter events, 0.1 us)
Async XLA Ops:
  0.0 12.5 %copy-start.2 = (s32[64]{0:T(128)S(1)}, s32[64]{0:T(128)}, u32[]{:S(2)}) copy-start(s32[64]{0:T(128)} %param.3) | copy-start | bytes 772
  3.6 2.2 copy-start
  6.0 17.6 %collective-permute-start = (bf16[16,144,128]{2,0,1:T(8,128)(2,1)S(1)}, bf16[16,144,128]{2,0,1:T(8,128)(2,1)S(1)}, u32[]{:S(2)}, u32[]{:S(2)}) collective-permute-start(bf16[16,144,128]{2,0,1:T(8,128)(2,1)S(1)} %get-tuple-element.9), channel_id=1, source_target_pairs={{0,1},{1,2},{2,3},{3,4},{4,5},{5,6},{6,7},{7,8},{8,9},{9,10},{10,1... | collective-permute-start | bytes 1769480 | tf_op jit(solution)/shard_map/ppermute | solution.py:25
  10.5 14.8 %collective-permute-start.1 = (bf16[16,144,128]{2,0,1:T(8,128)(2,1)S(1)}, bf16[16,144,128]{2,0,1:T(8,128)(2,1)S(1)}, u32[]{:S(2)}, u32[]{:S(2)}) collective-permute-start(bf16[16,144,128]{2,0,1:T(8,128)(2,1)S(1)} %get-tuple-element.10), channel_id=1, source_target_pairs={{1,0},{2,1},{3,2},{4,3},{5,4},{6,5},{7,6},{8,7},{9,8},{10,9},{11,1... | collective-permute-start | bytes 1769480 | tf_op jit(solution)/shard_map/ppermute | solution.py:27
  70.5 103.7 %collective-permute-start.3 = (bf16[2,64,144,128]{3,2,0,1:T(8,128)(2,1)}, bf16[2,64,144,128]{3,2,0,1:T(8,128)(2,1)S(1)}, u32[]{:S(2)}, u32[]{:S(2)}) collective-permute-start(bf16[2,64,144,128]{3,2,0,1:T(8,128)(2,1)} %fusion.6), channel_id=1, source_target_pairs={{0,30},{1,31},{2,0},{3,1},{4,2},{5,3},{6,4},{7,5},{8,6},{9,7},{10,... | collective-permute-start | bytes 14155784 | tf_op jit(solution)/shard_map/ppermute | solution.py:36
  70.5 154.1 %collective-permute-start.2 = (bf16[2,64,144,128]{3,2,0,1:T(8,128)(2,1)}, bf16[2,64,144,128]{3,2,0,1:T(8,128)(2,1)}, u32[]{:S(2)}, u32[]{:S(2)}) collective-permute-start(bf16[2,64,144,128]{3,2,0,1:T(8,128)(2,1)} %fusion.6), channel_id=1, source_target_pairs={{0,31},{1,0},{2,1},{3,2},{4,3},{5,4},{6,5},{7,6},{8,7},{9,8},{10,9... | collective-permute-start | bytes 14155784 | tf_op jit(solution)/shard_map/ppermute | solution.py:36
  174.2 2.2 copy-start.1
where the time goes:
time: 261 us; the launch traced here: 260 us
  waiting for transfers between devices  147 us (56%)
  matrix products  52.2 us (20%)
  other arithmetic  28.5 us (11%)
  local copies, waits for them, and re-layouts  22.4 us (9%)
  starting transfers between devices  10.5 us (4%)
    ppermute x2, waiting for transfers between devices, shifted(): lax.ppermute(shard, axis, [(i, (i + by) % count) for i in range(count)])  134 us
    dot_general x2, matrix products, correlate(): jnp.einsum('kfwc,okfwd->cofd', own_block, flipped, preferred_element_type...  21.8 us
    dot_general x1, matrix products, prepare(): jnp.einsum('jl,cwl->jwc', dft_table, normalized, preferred_element_type=j...  15.9 us
    convert_element_type x1, other arithmetic, prepare(): return (spectra * whiten_scale[None]).astype(jnp.bfloat16)  12 us
    another operation x1, local copies, waits for them, and re-layouts, per_device(): return jnp.stack(results, axis=1)  11.9 us
    ppermute x1, waiting for transfers between devices, with_halo(): lax.ppermute(tail, axis, [(i, (i + 1) % count) for i in range(ends)])  10.6 us
    unnamed x7, local copies, waits for them, and re-layouts  7.56 us
    dot_general x1, matrix products, prepare(): jnp.einsum('ie,ewl->iwl', selector.astype(jnp.bfloat16), extended, prefer...  7.47 us
  transfers between devices with their start and end apart: 4, of which 4 were waited for; matrix products, arithmetic and copies ran while one was open for 5% of the time, Pallas kernels for 0%

commit v1 on v0

v1 whole, which is shorter than its diff:
```python
import functools
import math

import jax
import jax.numpy as jnp
import ml_dtypes
import numpy as np
from jax import lax
from jax.experimental import pallas as pl
from jax.experimental.pallas import tpu as pltpu
from jax.sharding import PartitionSpec as P

HW = 16
RAM_HALF = 64
ROUNDS = 2
EPSILON = 1e-05
FLOOR = 0.25

STEP = 16
BINS_STEP = 16
GROUP = 16
WINDOW_CHUNKS = (1, 2, 2, 2, 2)


def prepare_kernel(x_ref, lo_ref, hi_ref, sel_ref, inv_ref, ram_ref, raminv_ref, table_ref, band_ref, bandinv_ref,
                   out_ref, ext, wide):
    channels, step, samples = x_ref.shape
    rows = channels * step
    side = HW * step
    ext[0:side, :] = lo_ref[...].astype(jnp.float32).reshape(side, samples)
    ext[side : side + rows, :] = x_ref[...].astype(jnp.float32).reshape(rows, samples)
    ext[side + rows :, :] = hi_ref[...].astype(jnp.float32).reshape(side, samples)
    sel = sel_ref[...]
    inv = inv_ref[...]
    ram = ram_ref[...]
    raminv = raminv_ref[...]
    table = table_ref[...]
    band = band_ref[...]
    bandinv = bandinv_ref[...]
    bins = table.shape[0] // 2
    for start in range(0, step, GROUP):
        group = range(start, start + GROUP)
        around = [ext[pl.ds(w, channels + 2 * HW, stride=step), :] for w in group]
        total = jnp.dot(
            sel, jnp.concatenate([a.astype(jnp.bfloat16) for a in around], axis=1), preferred_element_type=jnp.float32
        )
        balanced = jnp.concatenate(
            [
                (a[HW : HW + channels] - total[:, n * samples : (n + 1) * samples] * inv).astype(jnp.bfloat16)
                for n, a in enumerate(around)
            ],
            axis=0,
        )
        ram_sum = jnp.dot(jnp.abs(balanced), ram, preferred_element_type=jnp.float32)
        envelope = ram_sum * raminv + EPSILON
        normalized = (balanced.astype(jnp.float32) / envelope).astype(jnp.bfloat16)
        spectra = lax.dot_general(table, normalized, (((1,), (1,)), ((), ())), preferred_element_type=jnp.float32)
        re, im = spectra[:bins], spectra[bins:]
        power = re * re + im * im
        first = power.astype(jnp.bfloat16)
        rest = power - first.astype(jnp.float32)
        second = rest.astype(jnp.bfloat16)
        third = (rest - second.astype(jnp.float32)).astype(jnp.bfloat16)
        pieces = jnp.concatenate([first, second, third], axis=0)
        band_sum = jnp.dot(band, pieces, preferred_element_type=jnp.float32)
        for n, w in enumerate(group):
            part = slice(n * channels, (n + 1) * channels)
            scale = lax.rsqrt(jnp.maximum(band_sum[:, part] * bandinv, FLOOR))
            wide[pl.ds(w, bins, stride=step), :] = re[:, part] * scale
            wide[pl.ds(bins * step + w, bins, stride=step), :] = im[:, part] * scale
    out_ref[...] = wide[...].reshape(2, bins, step, channels).astype(out_ref.dtype)


def prepare(traces, lo, hi, first, halo_first, windows, consts):
    channels, _, samples = traces.shape
    bins = samples // 2
    steps = windows // STEP
    base, side = first // STEP, (first - halo_first) // STEP
    whole = lambda a: pl.BlockSpec(a.shape, lambda i: (0,) * a.ndim)
    return pl.pallas_call(
        prepare_kernel,
        grid=(steps,),
        in_specs=[
            pl.BlockSpec((channels, STEP, samples), lambda i: (0, base + i, 0)),
            pl.BlockSpec((HW, STEP, samples), lambda i: (0, side + i, 0)),
            pl.BlockSpec((HW, STEP, samples), lambda i: (0, side + i, 0)),
        ] + [whole(a) for a in consts],
        out_specs=pl.BlockSpec((2, bins, STEP, channels), lambda i: (0, 0, i, 0)),
        out_shape=jax.ShapeDtypeStruct((2, bins, windows, channels), jnp.bfloat16),
        scratch_shapes=[
            pltpu.VMEM(((channels + 2 * HW) * STEP, samples), jnp.float32),
            pltpu.VMEM((2 * bins * STEP, channels), jnp.float32),
        ],
        compiler_params=pltpu.CompilerParams(vmem_limit_bytes=32 * 1024 * 1024),
        cost_estimate=pl.CostEstimate(
            flops=windows * 2 * channels * samples * 1600,
            bytes_accessed=windows * channels * samples * 4,
            transcendentals=0,
        ),
        name="prepare",
    )(traces, lo, hi, *consts)


def correlate_kernel(n_own, n_partner, scale, *refs):
    own = refs[:n_own]
    partner = refs[n_own : n_own + n_partner]
    out_ref, wide = refs[-2:]
    step = own[0].shape[1]
    channels = own[0].shape[3]
    for k in range(step):
        parts = []
        for group in (own, partner):
            for part in range(2):
                pieces = [ref[part, k] for ref in group]
                parts.append(pieces[0] if len(pieces) == 1 else jnp.concatenate(pieces, axis=0))
        a_re, a_im, b_re, b_im = parts
        b = jnp.concatenate([b_re, b_im], axis=1)
        dims = (((0,), (0,)), ((), ()))
        by_re = lax.dot_general(a_re, b, dims, preferred_element_type=jnp.float32)
        by_im = lax.dot_general(a_im, b, dims, preferred_element_type=jnp.float32)
        re = by_re[:, :channels] + by_im[:, channels:]
        im = by_im[:, :channels] - by_re[:, channels:]
        wide[0, pl.ds(k, channels, stride=step), :] = re * scale
        wide[1, pl.ds(k, channels, stride=step), :] = im * scale
    for part in range(2):
        out_ref[:, 0, part] = wide[part].reshape(channels, step, channels).astype(out_ref.dtype)


def correlate(own, partner, round_index, first_bin, bins, total_bins, target=None):
    channels = own[0].shape[3]
    windows = sum(a.shape[2] for a in own)
    steps = bins // BINS_STEP
    base = first_bin // BINS_STEP
    shift = base - (0 if partner[0].shape[1] == total_bins else base)
    specs = [pl.BlockSpec((2, BINS_STEP, a.shape[2], channels), lambda i: (0, base + i, 0, 0)) for a in own]
    specs += [pl.BlockSpec((2, BINS_STEP, a.shape[2], channels), lambda i: (0, shift + i, 0, 0)) for a in partner]
    operands = list(own) + list(partner)
    aliases = {}
    if target is not None:
        specs.append(pl.BlockSpec(memory_space=pl.ANY))
        aliases = {len(operands): 0}
        operands.append(target)
    return pl.pallas_call(
        functools.partial(correlate_kernel, len(own), len(partner), 1.0 / math.sqrt(windows)),
        grid=(steps,),
        in_specs=specs,
        out_specs=pl.BlockSpec((channels, 1, 2, BINS_STEP, channels), lambda i: (0, round_index, 0, base + i, 0)),
        out_shape=jax.ShapeDtypeStruct((channels, ROUNDS, 2, total_bins, channels), jnp.bfloat16),
        scratch_shapes=[pltpu.VMEM((2, channels * BINS_STEP, channels), jnp.float32)],
        input_output_aliases=aliases,
        compiler_params=pltpu.CompilerParams(vmem_limit_bytes=48 * 1024 * 1024),
        cost_estimate=pl.CostEstimate(
            flops=bins * 8 * windows * channels * channels * 4,
            bytes_accessed=bins * channels * (windows * 8 + channels * 4),
            transcendentals=0,
        ),
        name="correlate",
    )(*operands)


def constants(first_channel, total_channels, channels, samples, bands):
    bins = samples // 2
    inner, outer = np.arange(channels), np.arange(channels + 2 * HW)
    offset = outer[None, :] - inner[:, None]
    sel = ((offset >= 0) & (offset <= 2 * HW)).astype(ml_dtypes.bfloat16)
    at = first_channel + jnp.arange(channels, dtype=jnp.int32)
    count = jnp.minimum(at, HW) + jnp.minimum(total_channels - 1 - at, HW) + 1
    inv = jnp.broadcast_to((1.0 / count.astype(jnp.float32))[:, None], (channels, samples))
    sample = np.arange(samples)
    near = np.abs(sample[:, None] - sample[None, :]) <= RAM_HALF
    ram = near.astype(ml_dtypes.bfloat16)
    raminv = (1.0 / near.sum(axis=0, dtype=np.float32)).astype(np.float32)[None, :]
    phase = 2.0 * math.pi / samples * (np.arange(1, bins + 1)[:, None] * sample[None, :] % samples)
    table = (np.concatenate([np.cos(phase), -np.sin(phase)], axis=0) / math.sqrt(samples)).astype(ml_dtypes.bfloat16)
    same = bands[:, None] == bands[None, :]
    size = jnp.sum(same.astype(jnp.float32), axis=1, keepdims=True)
    band = jnp.tile(same.astype(jnp.bfloat16), (1, 3))
    bandinv = jnp.broadcast_to(1.0 / size, (bins, channels))
    return [jnp.asarray(sel), inv, jnp.asarray(ram), jnp.asarray(raminv), jnp.asarray(table), band, bandinv]


def per_device(traces, bands):
    channels, windows, samples = traces.shape
    bins = samples // 2
    count = lax.axis_size("blk")
    ends = count - 1
    up = [(i, i + 1) for i in range(ends)]
    down = [(i + 1, i) for i in range(ends)]
    first_pairs = [((i + 2) % count, i) if i % 2 == 0 else (i, i) for i in range(count)]
    second_pairs = [((i + 2) % count, i) if i % 2 == 1 else (i, i) for i in range(count)]
    swap = [(i ^ 1, i) for i in range(count)]

    starts, sizes, at = [], [], 0
    for n in WINDOW_CHUNKS:
        starts.append(at)
        sizes.append(n * STEP)
        at += n * STEP

    cuts = [(0, sizes[0]), (sizes[0], windows)]
    halos = []
    for a, b in cuts:
        lo = lax.ppermute(traces[channels - HW :, a:b], "blk", up)
        hi = lax.ppermute(traces[:HW, a:b], "blk", down)
        halos.append((lo, hi))
    consts = constants(lax.axis_index("blk") * channels, channels * count, channels, samples, bands)

    own, held, other = [], [], []
    for n, (start, size) in enumerate(zip(starts, sizes)):
        lo, hi = halos[min(n, 1)]
        if own:
            lo, hi, own[-1] = lax.optimization_barrier((lo, hi, own[-1]))
        own.append(prepare(traces, lo, hi, start, cuts[min(n, 1)][0], size, consts))
    for chunk in own:
        held.append(lax.ppermute(chunk, "blk", first_pairs))
    for chunk in held:
        other.append(lax.ppermute(chunk, "blk", swap))
    out = correlate(own, other, 0, 0, bins, bins)
    for first in range(0, bins, BINS_STEP):
        mine = jnp.concatenate([c[:, first : first + BINS_STEP] for c in held], axis=2)
        far = lax.ppermute(mine, "blk", second_pairs)
        out = correlate(own, [far], 1, first, BINS_STEP, bins, out)
    return out


def solution(mesh):
    placed = (P("blk", None, None), P())
    return jax.shard_map(
        per_device,
        mesh=mesh,
        in_specs=placed,
        out_specs=P("blk", None, None, None, None),
        check_vma=False,
    )
```

time: 261 us -> 156 us (0.60)
  waiting for transfers between devices: 147 us -> 33.7 us
  starting transfers between devices: 10.5 us -> 81 us
  matrix products: 52.2 us -> 0 us
  Pallas kernels: 0 us -> 33.8 us
  other arithmetic: 28.5 us -> 0.19 us
  local copies, waits for them, and re-layouts: 22.4 us -> 6.39 us
    ppermute x4 -> x18, waiting for transfers between devices: 147 us -> 33.7 us  [the longest x4 27.6 us: per_device(): far = lax.ppermute(mine, 'blk', second_pairs)]
    ppermute x4 -> x18, starting transfers between devices: 10.5 us -> 81 us  [the longest x5 51.7 us: per_device(): other.append(lax.ppermute(chunk, 'blk', swap))]
    dot_general x5 -> x0, matrix products: 52.2 us -> none  [the longest x2 21.8 us: correlate(): jnp.einsum('kfwc,okfwd->cofd', own_block, flipped, preferred_element_type...]
    pallas_call x0 -> x10, Pallas kernels: none -> 33.8 us  [the longest x5 19 us: correlate(): pl.pallas_call(functools.partial(correlate_kernel, len(own), len(partner)...]
    another operation x3 -> x0, other arithmetic: 12.6 us -> none  [the longest x1 7.46 us: per_device(): return jnp.stack(results, axis=1)]
    convert_element_type x1, other arithmetic: 12 us -> 0.07 us  [constants(): band = jnp.tile(same.astype(jnp.bfloat16), (1, 3))]
    another operation x1 -> x2, local copies, waits for them, and re-layouts: 11.9 us -> 0.1 us  [constants(): band = jnp.tile(same.astype(jnp.bfloat16), (1, 3))]
    unnamed x7 -> x22, local copies, waits for them, and re-layouts: 7.56 us -> 3.8 us
  transfers between devices with their start and end apart: 4 -> 18, of which waited for: 4 -> 5; matrix products, arithmetic and copies ran while one was open for 5% -> 1% of each run, Pallas kernels for 0% -> 14%
where the time goes in v1:
time: 156 us; the launch traced here: 155 us
  starting transfers between devices  81 us (52%)
  Pallas kernels  33.8 us (22%)
  waiting for transfers between devices  33.7 us (22%)
  local copies, waits for them, and re-layouts  6.39 us (4%)
    ppermute x5, starting transfers between devices, per_device(): other.append(lax.ppermute(chunk, 'blk', swap))  51.7 us
    ppermute x4, waiting for transfers between devices, per_device(): far = lax.ppermute(mine, 'blk', second_pairs)  27.6 us
    pallas_call x5, Pallas kernels, correlate(): pl.pallas_call(functools.partial(correlate_kernel, len(own), len(partner)...  19 us
    pallas_call x5, Pallas kernels, prepare(): pl.pallas_call(prepare_kernel, grid=(steps,), in_specs=[pl.BlockSpec((cha...  14.8 us
    ppermute x4, starting transfers between devices, per_device(): far = lax.ppermute(mine, 'blk', second_pairs)  13.6 us
    ppermute x2, starting transfers between devices, per_device(): lo = lax.ppermute(traces[channels - HW:, a:b], 'blk', up)  8.15 us
    ppermute x2, starting transfers between devices, per_device(): hi = lax.ppermute(traces[:HW, a:b], 'blk', down)  3.84 us
    unnamed x22, local copies, waits for them, and re-layouts  3.8 us
  transfers between devices with their start and end apart: 18, of which 5 were waited for; matrix products, arithmetic and copies ran while one was open for 1% of the time, Pallas kernels for 14%

profile of v1, /device:TPU:1, one launch (start us, length us, event | category | flops | bytes accessed | tf_op | source)
XLA Modules:
  0.0 155.4 jit_solution(17661998843357146428)
XLA Ops:
  0.0 0.0 copy-start.4
  0.0 1.3 fusion.2
  1.4 4.5 %collective-permute-start = (bf16[16,128,128]{2,1,0:T(8,128)(2,1)S(1)}, bf16[16,128,128]{2,1,0:T(8,128)(2,1)S(1)}, u32[]{:S(2)}, u32[]{:S(2)}) collective-permute-start(bf16[16,128,128]{2,1,0:T(8,128)(2,1)S(1)} %get-tuple-element.32), channel_id=1, source_target_pairs={{0,1},{1,2},{2,3},{3,4},{4,5},{5,6},{6,7},{7,8},{8,9},{9,10},{10,1... | collective-permute-start | bytes 1572872 | tf_op jit(solution)/shard_map/ppermute | solution.py:202
  5.9 1.9 %collective-permute-start.1 = (bf16[16,128,128]{2,1,0:T(8,128)(2,1)S(1)}, bf16[16,128,128]{2,1,0:T(8,128)(2,1)S(1)}, u32[]{:S(2)}, u32[]{:S(2)}) collective-permute-start(bf16[16,128,128]{2,1,0:T(8,128)(2,1)S(1)} %get-tuple-element.31), channel_id=1, source_target_pairs={{1,0},{2,1},{3,2},{4,3},{5,4},{6,5},{7,6},{8,7},{9,8},{10,9},{11,1... | collective-permute-start | bytes 1572872 | tf_op jit(solution)/shard_map/ppermute | solution.py:203
  7.8 0.9 fusion.1
  8.7 3.6 %collective-permute-start.2 = (bf16[16,16,128]{2,1,0:T(8,128)(2,1)S(1)}, bf16[16,16,128]{2,1,0:T(8,128)(2,1)S(1)}, u32[]{:S(2)}, u32[]{:S(2)}) collective-permute-start(bf16[16,16,128]{2,1,0:T(8,128)(2,1)S(1)} %get-tuple-element.30), channel_id=1, source_target_pairs={{0,1},{1,2},{2,3},{3,4},{4,5},{5,6},{6,7},{7,8},{8,9},{9,10},{10,1... | collective-permute-start | bytes 196616 | tf_op jit(solution)/shard_map/ppermute | solution.py:202
  12.3 1.9 %collective-permute-start.3 = (bf16[16,16,128]{2,1,0:T(8,128)(2,1)S(1)}, bf16[16,16,128]{2,1,0:T(8,128)(2,1)S(1)}, u32[]{:S(2)}, u32[]{:S(2)}) collective-permute-start(bf16[16,16,128]{2,1,0:T(8,128)(2,1)S(1)} %get-tuple-element.29), channel_id=1, source_target_pairs={{1,0},{2,1},{3,2},{4,3},{5,4},{6,5},{7,6},{8,7},{9,8},{10,9},{11,1... | collective-permute-start | bytes 196616 | tf_op jit(solution)/shard_map/ppermute | solution.py:203
  14.3 0.1 compare_convert_fusion.1
  14.4 0.1 copy.11.band_ref
  14.5 0.1 fusion
  14.6 3.7 %collective-permute-done.2.lo_ref = bf16[16,16,128]{2,1,0:T(8,128)(2,1)S(1)} collective-permute-done((bf16[16,16,128]{2,1,0:T(8,128)(2,1)S(1)}, bf16[16,16,128]{2,1,0:T(8,128)(2,1)S(1)}, u32[]{:S(2)}, u32[]{:S(2)}) %collective-permute-start.2) | collective-permute-done | bytes 65568 | tf_op jit(solution)/shard_map/ppermute | solution.py:202
  18.3 2.4 %collective-permute-done.3.hi_ref = bf16[16,16,128]{2,1,0:T(8,128)(2,1)S(1)} collective-permute-done((bf16[16,16,128]{2,1,0:T(8,128)(2,1)S(1)}, bf16[16,16,128]{2,1,0:T(8,128)(2,1)S(1)}, u32[]{:S(2)}, u32[]{:S(2)}) %collective-permute-start.3) | collective-permute-done | bytes 65568 | tf_op jit(solution)/shard_map/ppermute | solution.py:203
  20.6 0.1 broadcast_in_dim.4.inv_ref
  20.7 0.1 broadcast_in_dim.5.bandinv_ref
  20.8 0.0 copy-done.3
  20.8 2.3 %copy-done = bf16[128,144,128]{2,1,0:T(8,128)(2,1)S(1)} copy-done((bf16[128,144,128]{2,1,0:T(8,128)(2,1)S(1)}, bf16[128,144,128]{2,1,0:T(8,128)(2,1)}, u32[]{:S(2)}) %copy-start) | copy-done | bytes 4718616
  23.2 1.6 %prepare.5.refs_0_ = bf16[2,64,16,128]{3,2,1,0:T(8,128)(2,1)S(1)} custom-call(bf16[128,144,128]{2,1,0:T(8,128)(2,1)S(1)} %copy-done, bf16[16,16,128]{2,1,0:T(8,128)(2,1)S(1)} %collective-permute-done.2.lo_ref, bf16[16,16,128]{2,1,0:T(8,128)(2,1)S(1)} %collective-permute-done.3.hi_ref, bf16[128,160]{1,0:T(8,128)(2,1)S(1)} %copy-done.1, ...), custom_call_target="tpu_custom_call" | custom-call | flops 838860800 | bytes 1048576 | tf_op jit(solution)/shard_map/prepare/pallas_call | solution.py:80
  24.8 3.3 %prepare.6.refs_1_ = bf16[2,64,32,128]{3,2,1,0:T(8,128)(2,1)S(1)} custom-call(bf16[128,144,128]{2,1,0:T(8,128)(2,1)S(1)} %copy-done, bf16[16,128,128]{2,1,0:T(8,128)(2,1)S(1)} %collective-permute-done.lo_ref, bf16[16,128,128]{2,1,0:T(8,128)(2,1)S(1)} %collective-permute-done.1.hi_ref, bf16[128,160]{1,0:T(8,128)(2,1)S(1)} %copy-done.1, ...), custom_call_target="tpu_custom_call" | custom-call | flops 1677721600 | bytes 2097152 | tf_op jit(solution)/shard_map/prepare/pallas_call | solution.py:80
  28.1 3.3 %prepare.7.refs_2_ = bf16[2,64,32,128]{3,2,1,0:T(8,128)(2,1)S(1)} custom-call(bf16[128,144,128]{2,1,0:T(8,128)(2,1)S(1)} %copy-done, bf16[16,128,128]{2,1,0:T(8,128)(2,1)S(1)} %collective-permute-done.lo_ref, bf16[16,128,128]{2,1,0:T(8,128)(2,1)S(1)} %collective-permute-done.1.hi_ref, bf16[128,160]{1,0:T(8,128)(2,1)S(1)} %copy-done.1, ...), custom_call_target="tpu_custom_call" | custom-call | flops 1677721600 | bytes 2097152 | tf_op jit(solution)/shard_map/prepare/pallas_call | solution.py:80
  31.4 3.3 %prepare.8.refs_3_ = bf16[2,64,32,128]{3,2,1,0:T(8,128)(2,1)S(1)} custom-call(bf16[128,144,128]{2,1,0:T(8,128)(2,1)S(1)} %copy-done, bf16[16,128,128]{2,1,0:T(8,128)(2,1)S(1)} %collective-permute-done.lo_ref, bf16[16,128,128]{2,1,0:T(8,128)(2,1)S(1)} %collective-permute-done.1.hi_ref, bf16[128,160]{1,0:T(8,128)(2,1)S(1)} %copy-done.1, ...), custom_call_target="tpu_custom_call" | custom-call | flops 1677721600 | bytes 2097152 | tf_op jit(solution)/shard_map/prepare/pallas_call | solution.py:80
  34.7 0.7 collective-permute-start.5
  35.5 0.7 collective-permute-start.6
  36.2 0.7 collective-permute-start.7
  36.9 3.3 %prepare.9.refs_4_ = bf16[2,64,32,128]{3,2,1,0:T(8,128)(2,1)S(1)} custom-call(bf16[128,144,128]{2,1,0:T(8,128)(2,1)S(1)} %copy-done, bf16[16,128,128]{2,1,0:T(8,128)(2,1)S(1)} %collective-permute-done.lo_ref, bf16[16,128,128]{2,1,0:T(8,128)(2,1)S(1)} %collective-permute-done.1.hi_ref, bf16[128,160]{1,0:T(8,128)(2,1)S(1)} %copy-done.1, ...), custom_call_target="tpu_custom_call" | custom-call | flops 1677721600 | bytes 2097152 | tf_op jit(solution)/shard_map/prepare/pallas_call | solution.py:80
  40.3 0.7 collective-permute-start.8
  41.0 0.7 collective-permute-start.4
  41.7 50.7 %collective-permute-start.13 = (bf16[2,64,16,128]{3,2,1,0:T(8,128)(2,1)S(1)}, bf16[2,64,16,128]{3,2,1,0:T(8,128)(2,1)S(1)}, u32[]{:S(2)}, u32[]{:S(2)}) collective-permute-start(bf16[2,64,16,128]{3,2,1,0:T(8,128)(2,1)S(1)} %collective-permute-done.4), channel_id=1, source_target_pairs={{1,0},{0,1},{3,2},{2,3},{5,4},{4,5},{7,6},{6,7},{9,8},{8,9},{11,10... | collective-permute-start | bytes 1572872 | tf_op jit(solution)/shard_map/ppermute | solution.py:216
  92.4 0.1 collective-permute-start.14
  92.5 0.5 collective-permute-start.15
  93.0 0.1 collective-permute-start.16
  93.1 0.4 collective-permute-start.17
  93.5 0.1 slice_dynamic-update-slice_fusion.3
  93.7 0.1 slice_dynamic-update-slice_fusion.2
  93.8 0.1 slice_dynamic-update-slice_fusion.1
  94.0 0.1 slice_dynamic-update-slice_fusion
  94.1 7.7 %collective-permute-start.12 = (bf16[2,16,144,128]{3,2,1,0:T(8,128)(2,1)S(1)}, bf16[2,16,144,128]{3,2,1,0:T(8,128)(2,1)S(1)}, u32[]{:S(2)}, u32[]{:S(2)}) collective-permute-start(bf16[2,16,144,128]{3,2,1,0:T(8,128)(2,1)S(1)} %get-tuple-element.33), channel_id=1, source_target_pairs={{0,0},{3,1},{2,2},{5,3},{4,4},{7,5},{6,6},{9,7},{8,8},{11,9},{10,1... | collective-permute-start | bytes 3538952 | tf_op jit(solution)/shard_map/ppermute | solution.py:220
  101.9 1.0 copy-done.6
  102.9 1.9 %collective-permute-start.11 = (bf16[2,16,144,128]{3,2,1,0:T(8,128)(2,1)S(1)}, bf16[2,16,144,128]{3,2,1,0:T(8,128)(2,1)S(1)}, u32[]{:S(2)}, u32[]{:S(2)}) collective-permute-start(bf16[2,16,144,128]{3,2,1,0:T(8,128)(2,1)S(1)} %get-tuple-element.34), channel_id=1, source_target_pairs={{0,0},{3,1},{2,2},{5,3},{4,4},{7,5},{6,6},{9,7},{8,8},{11,9},{10,1... | collective-permute-start | bytes 3538952 | tf_op jit(solution)/shard_map/ppermute | solution.py:220
  104.8 1.9 %collective-permute-start.10 = (bf16[2,16,144,128]{3,2,1,0:T(8,128)(2,1)S(1)}, bf16[2,16,144,128]{3,2,1,0:T(8,128)(2,1)S(1)}, u32[]{:S(2)}, u32[]{:S(2)}) collective-permute-start(bf16[2,16,144,128]{3,2,1,0:T(8,128)(2,1)S(1)} %get-tuple-element.35), channel_id=1, source_target_pairs={{0,0},{3,1},{2,2},{5,3},{4,4},{7,5},{6,6},{9,7},{8,8},{11,9},{10,1... | collective-permute-start | bytes 3538952 | tf_op jit(solution)/shard_map/ppermute | solution.py:220
  106.7 2.1 %collective-permute-start.9 = (bf16[2,16,144,128]{3,2,1,0:T(8,128)(2,1)S(1)}, bf16[2,16,144,128]{3,2,1,0:T(8,128)(2,1)S(1)}, u32[]{:S(2)}, u32[]{:S(2)}) collective-permute-start(bf16[2,16,144,128]{3,2,1,0:T(8,128)(2,1)S(1)} %get-tuple-element.36), channel_id=1, source_target_pairs={{0,0},{3,1},{2,2},{5,3},{4,4},{7,5},{6,6},{9,7},{8,8},{11,9},{10,1... | collective-permute-start | bytes 3538952 | tf_op jit(solution)/shard_map/ppermute | solution.py:220
  108.9 8.8 %correlate.5.refs_6_ = bf16[128,2,2,64,128]{4,3,2,1,0:T(8,128)(2,1)} custom-call(bf16[2,64,16,128]{3,2,1,0:T(8,128)(2,1)S(1)} %prepare.5.refs_0_, bf16[2,64,32,128]{3,2,1,0:T(8,128)(2,1)S(1)} %prepare.6.refs_1_, bf16[2,64,32,128]{3,2,1,0:T(8,128)(2,1)S(1)} %prepare.7.refs_2_, bf16[2,64,32,128]{3,2,1,0:T(8,128)(2,1)S(1)} %prepare.8.refs_3_, ...), custom_call_target="tpu_custom_call" | custom-call | flops 4831838208 | bytes 13631488 | tf_op jit(solution)/shard_map/correlate/pallas_call | solution.py:143
  117.7 2.5 %correlate.6.refs_6_ = bf16[128,2,2,64,128]{4,3,2,1,0:T(8,128)(2,1)} custom-call(bf16[2,64,16,128]{3,2,1,0:T(8,128)(2,1)S(1)} %prepare.5.refs_0_, bf16[2,64,32,128]{3,2,1,0:T(8,128)(2,1)S(1)} %prepare.6.refs_1_, bf16[2,64,32,128]{3,2,1,0:T(8,128)(2,1)S(1)} %prepare.7.refs_2_, ...), custom_call_target="tpu_custom_call", output_to_operand_aliasing={{}: (6, {})} | custom-call | flops 1207959552 | bytes 3407872 | tf_op jit(solution)/shard_map/correlate/pallas_call | solution.py:143
  120.2 7.4 %collective-permute-done.11.refs_5_ = bf16[2,16,144,128]{3,2,1,0:T(8,128)(2,1)S(1)} collective-permute-done((bf16[2,16,144,128]{3,2,1,0:T(8,128)(2,1)S(1)}, bf16[2,16,144,128]{3,2,1,0:T(8,128)(2,1)S(1)}, u32[]{:S(2)}, u32[]{:S(2)}) %collective-permute-start.11) | collective-permute-done | bytes 1179680 | tf_op jit(solution)/shard_map/ppermute | solution.py:220
  127.6 2.5 %correlate.7.refs_6_ = bf16[128,2,2,64,128]{4,3,2,1,0:T(8,128)(2,1)} custom-call(bf16[2,64,16,128]{3,2,1,0:T(8,128)(2,1)S(1)} %prepare.5.refs_0_, bf16[2,64,32,128]{3,2,1,0:T(8,128)(2,1)S(1)} %prepare.6.refs_1_, bf16[2,64,32,128]{3,2,1,0:T(8,128)(2,1)S(1)} %prepare.7.refs_2_, ...), custom_call_target="tpu_custom_call", output_to_operand_aliasing={{}: (6, {})} | custom-call | flops 1207959552 | bytes 3407872 | tf_op jit(solution)/shard_map/correlate/pallas_call | solution.py:143
  130.2 10.1 %collective-permute-done.10.refs_5_ = bf16[2,16,144,128]{3,2,1,0:T(8,128)(2,1)S(1)} collective-permute-done((bf16[2,16,144,128]{3,2,1,0:T(8,128)(2,1)S(1)}, bf16[2,16,144,128]{3,2,1,0:T(8,128)(2,1)S(1)}, u32[]{:S(2)}, u32[]{:S(2)}) %collective-permute-start.10) | collective-permute-done | bytes 1179680 | tf_op jit(solution)/shard_map/ppermute | solution.py:220
  140.3 2.5 %correlate.8.refs_6_ = bf16[128,2,2,64,128]{4,3,2,1,0:T(8,128)(2,1)} custom-call(bf16[2,64,16,128]{3,2,1,0:T(8,128)(2,1)S(1)} %prepare.5.refs_0_, bf16[2,64,32,128]{3,2,1,0:T(8,128)(2,1)S(1)} %prepare.6.refs_1_, bf16[2,64,32,128]{3,2,1,0:T(8,128)(2,1)S(1)} %prepare.7.refs_2_, ...), custom_call_target="tpu_custom_call", output_to_operand_aliasing={{}: (6, {})} | custom-call | flops 1207959552 | bytes 3407872 | tf_op jit(solution)/shard_map/correlate/pallas_call | solution.py:143
  142.8 10.1 %collective-permute-done.9.refs_5_ = bf16[2,16,144,128]{3,2,1,0:T(8,128)(2,1)S(1)} collective-permute-done((bf16[2,16,144,128]{3,2,1,0:T(8,128)(2,1)S(1)}, bf16[2,16,144,128]{3,2,1,0:T(8,128)(2,1)S(1)}, u32[]{:S(2)}, u32[]{:S(2)}) %collective-permute-start.9) | collective-permute-done | bytes 1179680 | tf_op jit(solution)/shard_map/ppermute | solution.py:220
  152.9 2.5 %correlate.9 = bf16[128,2,2,64,128]{4,3,2,1,0:T(8,128)(2,1)} custom-call(bf16[2,64,16,128]{3,2,1,0:T(8,128)(2,1)S(1)} %prepare.5.refs_0_, bf16[2,64,32,128]{3,2,1,0:T(8,128)(2,1)S(1)} %prepare.6.refs_1_, bf16[2,64,32,128]{3,2,1,0:T(8,128)(2,1)S(1)} %prepare.7.refs_2_, bf16[2,64,32,128]{3,2,1,0:T(8,128)(2,1)S(1)} %prepare.8.refs_3_, ...), custom_call_target="tpu_custom_call", output_to_operand_aliasing={{}: (6, {})} | custom-call | flops 1207959552 | bytes 3407872 | tf_op jit(solution)/shard_map/correlate/pallas_call | solution.py:143
  (31 shorter events, 0.1 us)
Async XLA Ops:
  0.0 20.8 %copy-start.1 = (bf16[128,160]{1,0:T(8,128)(2,1)S(1)}, bf16[128,160]{1,0:T(8,128)(2,1)}, u32[]{:S(2)}) copy-start(bf16[128,160]{1,0:T(8,128)(2,1)} %constant.10.clone.sel_ref) | copy-start | bytes 122884
  0.0 20.8 %copy-start.2 = (bf16[128,128]{1,0:T(8,128)(2,1)S(1)}, bf16[128,128]{1,0:T(8,128)(2,1)}, u32[]{:S(2)}) copy-start(bf16[128,128]{1,0:T(8,128)(2,1)} %constant.26.clone.ram_ref) | copy-start | bytes 98308
  0.0 20.8 %copy-start.3 = (bf16[128,128]{1,0:T(8,128)(2,1)S(1)}, bf16[128,128]{1,0:T(8,128)(2,1)}, u32[]{:S(2)}) copy-start(bf16[128,128]{1,0:T(8,128)(2,1)} %constant.28.clone.table_ref) | copy-start | bytes 98308
  0.0 20.8 %copy-start.4 = (f32[1,128]{1,0:T(1,128)S(1)}, f32[1,128]{1,0:T(1,128)}, u32[]{:S(2)}) copy-start(f32[1,128]{1,0:T(1,128)} %constant.27.clone.raminv_ref) | copy-start | bytes 1540
  0.0 14.3 %copy-start.5 = (s32[64]{0:T(128)S(1)}, s32[64]{0:T(128)}, u32[]{:S(2)}) copy-start(s32[64]{0:T(128)} %param.7) | copy-start | bytes 772
  1.4 23.4 %collective-permute-start = (bf16[16,128,128]{2,1,0:T(8,128)(2,1)S(1)}, bf16[16,128,128]{2,1,0:T(8,128)(2,1)S(1)}, u32[]{:S(2)}, u32[]{:S(2)}) collective-permute-start(bf16[16,128,128]{2,1,0:T(8,128)(2,1)S(1)} %get-tuple-element.32), channel_id=1, source_target_pairs={{0,1},{1,2},{2,3},{3,4},{4,5},{5,6},{6,7},{7,8},{8,9},{9,10},{10,1... | collective-permute-start | bytes 1572872 | tf_op jit(solution)/shard_map/ppermute | solution.py:202
  5.9 18.9 %collective-permute-start.1 = (bf16[16,128,128]{2,1,0:T(8,128)(2,1)S(1)}, bf16[16,128,128]{2,1,0:T(8,128)(2,1)S(1)}, u32[]{:S(2)}, u32[]{:S(2)}) collective-permute-start(bf16[16,128,128]{2,1,0:T(8,128)(2,1)S(1)} %get-tuple-element.31), channel_id=1, source_target_pairs={{1,0},{2,1},{3,2},{4,3},{5,4},{6,5},{7,6},{8,7},{9,8},{10,9},{11,1... | collective-permute-start | bytes 1572872 | tf_op jit(solution)/shard_map/ppermute | solution.py:203
  8.7 9.6 %collective-permute-start.2 = (bf16[16,16,128]{2,1,0:T(8,128)(2,1)S(1)}, bf16[16,16,128]{2,1,0:T(8,128)(2,1)S(1)}, u32[]{:S(2)}, u32[]{:S(2)}) collective-permute-start(bf16[16,16,128]{2,1,0:T(8,128)(2,1)S(1)} %get-tuple-element.30), channel_id=1, source_target_pairs={{0,1},{1,2},{2,3},{3,4},{4,5},{5,6},{6,7},{7,8},{8,9},{9,10},{10,1... | collective-permute-start | bytes 196616 | tf_op jit(solution)/shard_map/ppermute | solution.py:202
  12.3 8.3 %collective-permute-start.3 = (bf16[16,16,128]{2,1,0:T(8,128)(2,1)S(1)}, bf16[16,16,128]{2,1,0:T(8,128)(2,1)S(1)}, u32[]{:S(2)}, u32[]{:S(2)}) collective-permute-start(bf16[16,16,128]{2,1,0:T(8,128)(2,1)S(1)} %get-tuple-element.29), channel_id=1, source_target_pairs={{1,0},{2,1},{3,2},{4,3},{5,4},{6,5},{7,6},{8,7},{9,8},{10,9},{11,1... | collective-permute-start | bytes 196616 | tf_op jit(solution)/shard_map/ppermute | solution.py:203
  20.8 2.3 %copy-start = (bf16[128,144,128]{2,1,0:T(8,128)(2,1)S(1)}, bf16[128,144,128]{2,1,0:T(8,128)(2,1)}, u32[]{:S(2)}) copy-start(bf16[128,144,128]{2,1,0:T(8,128)(2,1)} %x_ref.9) | copy-start | bytes 14155780
  34.7 57.7 %collective-permute-start.5 = (bf16[2,64,32,128]{3,2,1,0:T(8,128)(2,1)S(1)}, bf16[2,64,32,128]{3,2,1,0:T(8,128)(2,1)S(1)}, u32[]{:S(2)}, u32[]{:S(2)}) collective-permute-start(bf16[2,64,32,128]{3,2,1,0:T(8,128)(2,1)S(1)} %prepare.6.refs_1_), channel_id=1, source_target_pairs={{2,0},{1,1},{4,2},{3,3},{6,4},{5,5},{8,6},{7,7},{10,8},{9,9},{12,1... | collective-permute-start | bytes 3145736 | tf_op jit(solution)/shard_map/ppermute | solution.py:214
  35.5 57.1 %collective-permute-start.6 = (bf16[2,64,32,128]{3,2,1,0:T(8,128)(2,1)S(1)}, bf16[2,64,32,128]{3,2,1,0:T(8,128)(2,1)S(1)}, u32[]{:S(2)}, u32[]{:S(2)}) collective-permute-start(bf16[2,64,32,128]{3,2,1,0:T(8,128)(2,1)S(1)} %prepare.7.refs_2_), channel_id=1, source_target_pairs={{2,0},{1,1},{4,2},{3,3},{6,4},{5,5},{8,6},{7,7},{10,8},{9,9},{12,1... | collective-permute-start | bytes 3145736 | tf_op jit(solution)/shard_map/ppermute | solution.py:214
  36.2 56.8 %collective-permute-start.7 = (bf16[2,64,32,128]{3,2,1,0:T(8,128)(2,1)S(1)}, bf16[2,64,32,128]{3,2,1,0:T(8,128)(2,1)S(1)}, u32[]{:S(2)}, u32[]{:S(2)}) collective-permute-start(bf16[2,64,32,128]{3,2,1,0:T(8,128)(2,1)S(1)} %prepare.8.refs_3_), channel_id=1, source_target_pairs={{2,0},{1,1},{4,2},{3,3},{6,4},{5,5},{8,6},{7,7},{10,8},{9,9},{12,1... | collective-permute-start | bytes 3145736 | tf_op jit(solution)/shard_map/ppermute | solution.py:214
  40.3 52.8 %collective-permute-start.8 = (bf16[2,64,32,128]{3,2,1,0:T(8,128)(2,1)S(1)}, bf16[2,64,32,128]{3,2,1,0:T(8,128)(2,1)S(1)}, u32[]{:S(2)}, u32[]{:S(2)}) collective-permute-start(bf16[2,64,32,128]{3,2,1,0:T(8,128)(2,1)S(1)} %prepare.9.refs_4_), channel_id=1, source_target_pairs={{2,0},{1,1},{4,2},{3,3},{6,4},{5,5},{8,6},{7,7},{10,8},{9,9},{12,1... | collective-permute-start | bytes 3145736 | tf_op jit(solution)/shard_map/ppermute | solution.py:214
  41.0 0.7 collective-permute-start.4
  41.7 52.4 %collective-permute-start.13 = (bf16[2,64,16,128]{3,2,1,0:T(8,128)(2,1)S(1)}, bf16[2,64,16,128]{3,2,1,0:T(8,128)(2,1)S(1)}, u32[]{:S(2)}, u32[]{:S(2)}) collective-permute-start(bf16[2,64,16,128]{3,2,1,0:T(8,128)(2,1)S(1)} %collective-permute-done.4), channel_id=1, source_target_pairs={{1,0},{0,1},{3,2},{2,3},{5,4},{4,5},{7,6},{6,7},{9,8},{8,9},{11,10... | collective-permute-start | bytes 1572872 | tf_op jit(solution)/shard_map/ppermute | solution.py:216
  92.4 9.4 %collective-permute-start.14 = (bf16[2,64,32,128]{3,2,1,0:T(8,128)(2,1)S(1)}, bf16[2,64,32,128]{3,2,1,0:T(8,128)(2,1)S(1)}, u32[]{:S(2)}, u32[]{:S(2)}) collective-permute-start(bf16[2,64,32,128]{3,2,1,0:T(8,128)(2,1)S(1)} %collective-permute-done.5), channel_id=1, source_target_pairs={{1,0},{0,1},{3,2},{2,3},{5,4},{4,5},{7,6},{6,7},{9,8},{8,9},{11,10... | collective-permute-start | bytes 3145736 | tf_op jit(solution)/shard_map/ppermute | solution.py:216
  92.5 12.2 %collective-permute-start.15 = (bf16[2,64,32,128]{3,2,1,0:T(8,128)(2,1)S(1)}, bf16[2,64,32,128]{3,2,1,0:T(8,128)(2,1)S(1)}, u32[]{:S(2)}, u32[]{:S(2)}) collective-permute-start(bf16[2,64,32,128]{3,2,1,0:T(8,128)(2,1)S(1)} %collective-permute-done.6), channel_id=1, source_target_pairs={{1,0},{0,1},{3,2},{2,3},{5,4},{4,5},{7,6},{6,7},{9,8},{8,9},{11,10... | collective-permute-start | bytes 3145736 | tf_op jit(solution)/shard_map/ppermute | solution.py:216
  93.0 13.7 %collective-permute-start.16 = (bf16[2,64,32,128]{3,2,1,0:T(8,128)(2,1)S(1)}, bf16[2,64,32,128]{3,2,1,0:T(8,128)(2,1)S(1)}, u32[]{:S(2)}, u32[]{:S(2)}) collective-permute-start(bf16[2,64,32,128]{3,2,1,0:T(8,128)(2,1)S(1)} %collective-permute-done.7), channel_id=1, source_target_pairs={{1,0},{0,1},{3,2},{2,3},{5,4},{4,5},{7,6},{6,7},{9,8},{8,9},{11,10... | collective-permute-start | bytes 3145736 | tf_op jit(solution)/shard_map/ppermute | solution.py:216
  93.1 15.8 %collective-permute-start.17 = (bf16[2,64,32,128]{3,2,1,0:T(8,128)(2,1)S(1)}, bf16[2,64,32,128]{3,2,1,0:T(8,128)(2,1)}, u32[]{:S(2)}, u32[]{:S(2)}) collective-permute-start(bf16[2,64,32,128]{3,2,1,0:T(8,128)(2,1)S(1)} %collective-permute-done.8), channel_id=1, source_target_pairs={{1,0},{0,1},{3,2},{2,3},{5,4},{4,5},{7,6},{6,7},{9,8},{8,9},{11,10... | collective-permute-start | bytes 3145736 | tf_op jit(solution)/shard_map/ppermute | solution.py:216
  94.1 23.5 %collective-permute-start.12 = (bf16[2,16,144,128]{3,2,1,0:T(8,128)(2,1)S(1)}, bf16[2,16,144,128]{3,2,1,0:T(8,128)(2,1)S(1)}, u32[]{:S(2)}, u32[]{:S(2)}) collective-permute-start(bf16[2,16,144,128]{3,2,1,0:T(8,128)(2,1)S(1)} %get-tuple-element.33), channel_id=1, source_target_pairs={{0,0},{3,1},{2,2},{5,3},{4,4},{7,5},{6,6},{9,7},{8,8},{11,9},{10,1... | collective-permute-start | bytes 3538952 | tf_op jit(solution)/shard_map/ppermute | solution.py:220
  101.9 1.0 copy-start.6
  102.9 24.8 %collective-permute-start.11 = (bf16[2,16,144,128]{3,2,1,0:T(8,128)(2,1)S(1)}, bf16[2,16,144,128]{3,2,1,0:T(8,128)(2,1)S(1)}, u32[]{:S(2)}, u32[]{:S(2)}) collective-permute-start(bf16[2,16,144,128]{3,2,1,0:T(8,128)(2,1)S(1)} %get-tuple-element.34), channel_id=1, source_target_pairs={{0,0},{3,1},{2,2},{5,3},{4,4},{7,5},{6,6},{9,7},{8,8},{11,9},{10,1... | collective-permute-start | bytes 3538952 | tf_op jit(solution)/shard_map/ppermute | solution.py:220
  104.8 4.1 %copy-start.7 = (bf16[2,64,32,128]{3,2,1,0:T(8,128)(2,1)}, bf16[2,64,32,128]{3,2,1,0:T(8,128)(2,1)S(1)}, u32[]{:S(2)}) copy-start(bf16[2,64,32,128]{3,2,1,0:T(8,128)(2,1)S(1)} %collective-permute-done.15.refs_7_) | copy-start | bytes 3145732
  104.8 35.5 %collective-permute-start.10 = (bf16[2,16,144,128]{3,2,1,0:T(8,128)(2,1)S(1)}, bf16[2,16,144,128]{3,2,1,0:T(8,128)(2,1)S(1)}, u32[]{:S(2)}, u32[]{:S(2)}) collective-permute-start(bf16[2,16,144,128]{3,2,1,0:T(8,128)(2,1)S(1)} %get-tuple-element.35), channel_id=1, source_target_pairs={{0,0},{3,1},{2,2},{5,3},{4,4},{7,5},{6,6},{9,7},{8,8},{11,9},{10,1... | collective-permute-start | bytes 3538952 | tf_op jit(solution)/shard_map/ppermute | solution.py:220
  106.7 2.1 %copy-start.8 = (bf16[2,64,32,128]{3,2,1,0:T(8,128)(2,1)}, bf16[2,64,32,128]{3,2,1,0:T(8,128)(2,1)S(1)}, u32[]{:S(2)}) copy-start(bf16[2,64,32,128]{3,2,1,0:T(8,128)(2,1)S(1)} %collective-permute-done.16.refs_8_) | copy-start | bytes 3145732
  106.7 46.2 %collective-permute-start.9 = (bf16[2,16,144,128]{3,2,1,0:T(8,128)(2,1)S(1)}, bf16[2,16,144,128]{3,2,1,0:T(8,128)(2,1)S(1)}, u32[]{:S(2)}, u32[]{:S(2)}) collective-permute-start(bf16[2,16,144,128]{3,2,1,0:T(8,128)(2,1)S(1)} %get-tuple-element.36), channel_id=1, source_target_pairs={{0,0},{3,1},{2,2},{5,3},{4,4},{7,5},{6,6},{9,7},{8,8},{11,9},{10,1... | collective-permute-start | bytes 3538952 | tf_op jit(solution)/shard_map/ppermute | solution.py:220

commit v2 on v1

v2 whole, which is shorter than its diff:
```python
import functools
import math

import jax
import jax.numpy as jnp
import ml_dtypes
import numpy as np
from jax import lax
from jax.experimental import pallas as pl
from jax.experimental.pallas import tpu as pltpu
from jax.sharding import PartitionSpec as P

HW = 16
RAM_HALF = 64
ROUNDS = 2
EPSILON = 1e-05
FLOOR = 0.25

STEP = 16
BINS_STEP = 16
GROUP = 16
VMEM = 32 * 1024 * 1024
CHUNKS = (2, 2, 2, 2, 1)
TOKEN = 1
FIRST_ROUND_AFTER = 3
AFTER = {2: 0, 3: 1}
HALO_STEPS = 4


def prepare_kernel(odd_ref, x_ref, lo_even, lo_odd, hi_even, hi_odd, sel_ref, inv_ref, ram_ref, raminv_ref,
                   table_ref, band_ref, bandinv_ref, out_ref, ext, wide):
    channels, step, samples = x_ref.shape
    rows = channels * step
    side = HW * step
    odd = odd_ref[0] != 0

    def put(at, ref):
        count = ref.shape[0] * step
        ext[at : at + count, :] = ref[...].astype(jnp.float32).reshape(count, samples)

    @pl.when(odd)
    def _():
        put(0, lo_odd)
        put(side + rows, hi_odd)

    @pl.when(jnp.logical_not(odd))
    def _():
        put(0, lo_even)
        put(side + rows, hi_even)

    put(side, x_ref)
    sel = sel_ref[...]
    inv = inv_ref[...]
    ram = ram_ref[...]
    raminv = raminv_ref[...]
    table = table_ref[...]
    band = band_ref[...]
    bandinv = bandinv_ref[...]
    bins = table.shape[0] // 2
    for start in range(0, step, GROUP):
        group = range(start, start + GROUP)
        around = [ext[pl.ds(w, channels + 2 * HW, stride=step), :] for w in group]
        total = jnp.dot(
            sel, jnp.concatenate([a.astype(jnp.bfloat16) for a in around], axis=1), preferred_element_type=jnp.float32
        )
        balanced = jnp.concatenate(
            [
                (a[HW : HW + channels] - total[:, n * samples : (n + 1) * samples] * inv).astype(jnp.bfloat16)
                for n, a in enumerate(around)
            ],
            axis=0,
        )
        ram_sum = jnp.dot(jnp.abs(balanced), ram, preferred_element_type=jnp.float32)
        envelope = ram_sum * raminv + EPSILON
        normalized = (balanced.astype(jnp.float32) / envelope).astype(jnp.bfloat16)
        spectra = lax.dot_general(table, normalized, (((1,), (1,)), ((), ())), preferred_element_type=jnp.float32)
        re, im = spectra[:bins], spectra[bins:]
        power = re * re + im * im
        first = power.astype(jnp.bfloat16)
        rest = power - first.astype(jnp.float32)
        second = rest.astype(jnp.bfloat16)
        third = (rest - second.astype(jnp.float32)).astype(jnp.bfloat16)
        pieces = jnp.concatenate([first, second, third], axis=0)
        band_sum = jnp.dot(band, pieces, preferred_element_type=jnp.float32)
        for n, w in enumerate(group):
            part = slice(n * channels, (n + 1) * channels)
            scale = lax.rsqrt(jnp.maximum(band_sum[:, part] * bandinv, FLOOR))
            wide[pl.ds(w, bins, stride=step), :] = re[:, part] * scale
            wide[pl.ds(bins * step + w, bins, stride=step), :] = im[:, part] * scale
    out_ref[...] = wide[...].reshape(2, bins, step, channels).astype(out_ref.dtype)


def borders_kernel(early, odd_ref, x_ref, first_ref, rest_ref, inner_ref, sems):
    channels, windows, _ = x_ref.shape
    late = windows - early
    top = channels - HW
    outer = odd_ref[0] * top
    inner = top - outer
    copies = [
        pltpu.make_async_copy(x_ref.at[pl.ds(outer, HW), pl.ds(0, early), :], first_ref, sems.at[0]),
        pltpu.make_async_copy(x_ref.at[pl.ds(inner, HW)], inner_ref, sems.at[1]),
        pltpu.make_async_copy(x_ref.at[pl.ds(outer, HW), pl.ds(early, late), :], rest_ref, sems.at[2]),
    ]
    for copy in copies:
        copy.start()
    for copy in copies:
        copy.wait()


def borders(traces, odd, early):
    _, windows, samples = traces.shape
    shape = lambda n: jax.ShapeDtypeStruct((HW, n, samples), traces.dtype)
    return pl.pallas_call(
        functools.partial(borders_kernel, early),
        in_specs=[pl.BlockSpec(memory_space=pltpu.SMEM), pl.BlockSpec(memory_space=pl.ANY)],
        out_specs=[pl.BlockSpec(memory_space=pltpu.VMEM)] * 3,
        out_shape=[shape(early), shape(windows - early), shape(windows)],
        scratch_shapes=[pltpu.SemaphoreType.DMA((3,))],
        cost_estimate=pl.CostEstimate(flops=1, bytes_accessed=1, transcendentals=0),
        name="borders",
    )(odd, traces)


def prepare(x, odd, halos, first, windows, consts):
    channels, _, samples = x.shape
    bins = samples // 2
    whole = lambda a: pl.BlockSpec(a.shape, lambda i: (0,) * a.ndim)
    part = lambda rows, start: pl.BlockSpec((rows, STEP, samples), lambda i: (0, start // STEP + i, 0))
    return pl.pallas_call(
        prepare_kernel,
        grid=(windows // STEP,),
        in_specs=[pl.BlockSpec(memory_space=pltpu.SMEM), part(channels, first)]
        + [part(HW, start) for _, start in halos]
        + [whole(a) for a in consts],
        out_specs=pl.BlockSpec((2, bins, STEP, channels), lambda i: (0, 0, i, 0)),
        out_shape=jax.ShapeDtypeStruct((2, bins, windows, channels), jnp.bfloat16),
        scratch_shapes=[
            pltpu.VMEM(((channels + 2 * HW) * STEP, samples), jnp.float32),
            pltpu.VMEM((2 * bins * STEP, channels), jnp.float32),
        ],
        compiler_params=pltpu.CompilerParams(vmem_limit_bytes=VMEM),
        cost_estimate=pl.CostEstimate(flops=1, bytes_accessed=1, transcendentals=0),
        name="prepare",
    )(odd, x, *[a for a, _ in halos], *consts)


def correlate_kernel(n_own, n_partner, scale, pick_ref, *refs):
    own = refs[:n_own]
    partner = refs[n_own : n_own + n_partner]
    far = refs[n_own + n_partner] if pick_ref is not None else None
    out_ref, wide = refs[-2:]
    step = own[0].shape[1]
    channels = own[0].shape[3]

    def whole(group, part, k):
        pieces = [ref[part, k] for ref in group]
        return pieces[0] if len(pieces) == 1 else jnp.concatenate(pieces, axis=0)

    def run(partner):
        for k in range(step):
            a_re, a_im = whole(own, 0, k), whole(own, 1, k)
            b = jnp.concatenate([whole(partner, 0, k), whole(partner, 1, k)], axis=1)
            dims = (((0,), (0,)), ((), ()))
            by_re = lax.dot_general(a_re, b, dims, preferred_element_type=jnp.float32)
            by_im = lax.dot_general(a_im, b, dims, preferred_element_type=jnp.float32)
            re = by_re[:, :channels] + by_im[:, channels:]
            im = by_im[:, :channels] - by_re[:, channels:]
            wide[0, pl.ds(k, channels, stride=step), :] = re * scale
            wide[1, pl.ds(k, channels, stride=step), :] = im * scale

    if far is None:
        run(partner)
    else:
        pl.when(pick_ref[0] == 0)(lambda: run(partner))
        pl.when(pick_ref[0] != 0)(lambda: run([far]))
    for part in range(2):
        out_ref[:, 0, part] = wide[part].reshape(channels, step, channels).astype(out_ref.dtype)


def correlate(own, partner, round_index, first_bin, bins, pick=None, far=None, target=None, after=None):
    _, total_bins, _, channels = own[0].shape
    windows = sum(a.shape[2] for a in own)
    steps = bins // BINS_STEP
    base = first_bin // BINS_STEP
    operands = list(own) + list(partner)
    specs = [pl.BlockSpec((2, BINS_STEP, a.shape[2], channels), lambda i: (0, base + i, 0, 0)) for a in operands]
    if far is not None:
        specs.append(pl.BlockSpec((2, BINS_STEP, windows, channels), lambda i: (0, i, 0, 0)))
        operands.append(far)
    kernel = functools.partial(correlate_kernel, len(own), len(partner), 1.0 / math.sqrt(windows))
    if pick is None:
        kernel = functools.partial(kernel, None)
    else:
        specs.insert(0, pl.BlockSpec(memory_space=pltpu.SMEM))
        operands.insert(0, pick)
    aliases = {}
    if target is not None:
        specs.append(pl.BlockSpec(memory_space=pl.ANY))
        aliases = {len(operands): 0}
        operands.append(target)
    if after is not None:
        specs.append(pl.BlockSpec(memory_space=pl.ANY))
        operands.append(after)
    return pl.pallas_call(
        kernel,
        grid=(steps,),
        in_specs=specs,
        out_specs=pl.BlockSpec((channels, 1, 2, BINS_STEP, channels), lambda i: (0, round_index, 0, base + i, 0)),
        out_shape=jax.ShapeDtypeStruct((channels, ROUNDS, 2, total_bins, channels), jnp.bfloat16),
        scratch_shapes=[pltpu.VMEM((2, channels * BINS_STEP, channels), jnp.float32)],
        input_output_aliases=aliases,
        compiler_params=pltpu.CompilerParams(vmem_limit_bytes=VMEM),
        cost_estimate=pl.CostEstimate(flops=1, bytes_accessed=1, transcendentals=0),
        name="correlate",
    )(*operands)


def edges(block, total_channels, channels, samples):
    inner, outer = np.arange(channels), np.arange(channels + 2 * HW)
    offset = outer[None, :] - inner[:, None]
    near = jnp.asarray((offset >= 0) & (offset <= 2 * HW))
    at = block * channels - HW + jnp.asarray(outer, jnp.int32)
    sel = (near & (at >= 0)[None, :] & (at < total_channels)[None, :]).astype(jnp.bfloat16)
    own = block * channels + jnp.asarray(inner, jnp.int32)
    count = jnp.minimum(own, HW) + jnp.minimum(total_channels - 1 - own, HW) + 1
    inv = jnp.broadcast_to((1.0 / count.astype(jnp.float32))[:, None], (channels, samples))
    return [sel, inv]


def tables(channels, samples, bands):
    bins = samples // 2
    sample = np.arange(samples)
    near = np.abs(sample[:, None] - sample[None, :]) <= RAM_HALF
    ram = near.astype(ml_dtypes.bfloat16)
    raminv = (1.0 / near.sum(axis=0, dtype=np.float32)).astype(np.float32)[None, :]
    phase = 2.0 * math.pi / samples * (np.arange(1, bins + 1)[:, None] * sample[None, :] % samples)
    table = (np.concatenate([np.cos(phase), -np.sin(phase)], axis=0) / math.sqrt(samples)).astype(ml_dtypes.bfloat16)
    same = bands[:, None] == bands[None, :]
    size = jnp.sum(same.astype(jnp.float32), axis=1, keepdims=True)
    band = jnp.tile(same.astype(jnp.bfloat16), (1, 3))
    bandinv = jnp.broadcast_to(1.0 / size, (bins, channels))
    return [jnp.asarray(ram), jnp.asarray(raminv), jnp.asarray(table), band, bandinv]


def per_device(traces, bands):
    channels, windows, samples = traces.shape
    bins = samples // 2
    count = lax.axis_size("blk")
    block = lax.axis_index("blk")
    pick = (block % 2).astype(jnp.int32)[None]
    swap = [(i, i ^ 1) for i in range(count)]
    cross = [(i, i + 1 if i % 2 else i - 1) for i in range(1, count - 1)]
    first_pairs = [((i + 2) % count, i) if i % 2 == 0 else (i, i) for i in range(count)]
    second_pairs = [((i + 2) % count, i) for i in range(1, count, 2)]
    early = HALO_STEPS * STEP

    outer_first, outer_rest, inner = borders(traces, pick, early)
    across_first = lax.ppermute(outer_first, "blk", cross)
    beside = lax.ppermute(inner, "blk", swap)
    across_rest = lax.ppermute(outer_rest, "blk", cross)
    consts = edges(block, channels * count, channels, samples) + tables(channels, samples, bands)

    own, held = [], []
    at = 0
    for n, size in enumerate(CHUNKS):
        if n == 1:
            across_first, across_rest, own[0] = lax.optimization_barrier((across_first, across_rest, own[0]))
        elif n > 1:
            across_rest, own[-1], held[n - 2] = lax.optimization_barrier((across_rest, own[-1], held[n - 2]))
        across, skip = (across_first, 0) if at < early else (across_rest, early)
        x, first = (traces[:, : size * STEP], 0) if n == 0 else (traces, at)
        halos = [(across, at - skip), (beside, at), (beside, at), (across, at - skip)]
        own.append(prepare(x, pick, halos, first, size * STEP, consts))
        held.append(lax.ppermute(own[-1], "blk", first_pairs))
        at += size * STEP
    token = lax.ppermute(held[TOKEN][0, 0, :STEP], "blk", swap)
    far = []
    for first in range(0, bins, BINS_STEP):
        mine = jnp.concatenate([c[:, first : first + BINS_STEP] for c in own], axis=2)
        mine, token = lax.optimization_barrier((mine, token))
        far.append(lax.ppermute(mine, "blk", second_pairs))
    other = []
    for n in range(len(held)):
        if n in AFTER:
            held[n], other[AFTER[n]] = lax.optimization_barrier((held[n], other[AFTER[n]]))
        other.append(lax.ppermute(held[n], "blk", swap))
    out = None
    for n, first in enumerate(range(0, bins, BINS_STEP)):
        if n == FIRST_ROUND_AFTER:
            out = correlate(own, other, 0, 0, bins, target=out)
        out = correlate(own, held, 1, first, BINS_STEP, pick, far[n], out, token)
    return out


def solution(mesh):
    placed = (P("blk", None, None), P())
    return jax.shard_map(
        per_device,
        mesh=mesh,
        in_specs=placed,
        out_specs=P("blk", None, None, None, None),
        check_vma=False,
    )
```

time: 156 us -> 134 us (0.86)
  waiting for transfers between devices: 33.7 us -> 15.8 us
  starting transfers between devices: 81 us -> 77 us
  Pallas kernels: 33.8 us -> 36 us
  local copies, waits for them, and re-layouts: 6.39 us -> 4.61 us
    ppermute x18, waiting for transfers between devices: 33.7 us -> 15.8 us  [the longest x4 10.3 us: per_device(): far.append(lax.ppermute(mine, 'blk', second_pairs))]
    ppermute x18, starting transfers between devices: 81 us -> 77 us  [the longest x5 47.9 us: per_device(): other.append(lax.ppermute(held[n], 'blk', swap))]
    pallas_call x10 -> x11, Pallas kernels: 33.8 us -> 36 us  [the longest x5 18.7 us: correlate(): pl.pallas_call(kernel, grid=(steps,), in_specs=specs, out_specs=pl.BlockS...]
    unnamed x22 -> x16, local copies, waits for them, and re-layouts: 3.8 us -> 2.98 us
  transfers between devices with their start and end apart: 18 -> 18, of which waited for: 5 -> 5; matrix products, arithmetic and copies ran while one was open for 1% -> 2% of each run, Pallas kernels for 14% -> 23%
where the time goes in v2:
time: 134 us
  starting transfers between devices  77 us (57%)
  Pallas kernels  36 us (27%)
  waiting for transfers between devices  15.8 us (12%)
  local copies, waits for them, and re-layouts  4.61 us (3%)
    ppermute x5, starting transfers between devices, per_device(): other.append(lax.ppermute(held[n], 'blk', swap))  47.9 us
    ppermute x4, starting transfers between devices, per_device(): far.append(lax.ppermute(mine, 'blk', second_pairs))  18.9 us
    pallas_call x5, Pallas kernels, correlate(): pl.pallas_call(kernel, grid=(steps,), in_specs=specs, out_specs=pl.BlockS...  18.7 us
    pallas_call x5, Pallas kernels, prepare(): pl.pallas_call(prepare_kernel, grid=(windows // STEP,), in_specs=[pl.Bloc...  15.1 us
    ppermute x4, waiting for transfers between devices, per_device(): far.append(lax.ppermute(mine, 'blk', second_pairs))  10.3 us
    ppermute x1, starting transfers between devices, per_device(): across_first = lax.ppermute(outer_first, 'blk', cross)  4.46 us
    ppermute x5, starting transfers between devices, per_device(): held.append(lax.ppermute(own[-1], 'blk', first_pairs))  3.61 us
    unnamed x16, local copies, waits for them, and re-layouts  2.98 us
  transfers between devices with their start and end apart: 18, of which 5 were waited for; matrix products, arithmetic and copies ran while one was open for 2% of the time, Pallas kernels for 23%

profile of v2, /device:TPU:1, one launch (start us, length us, event | category | flops | bytes accessed | tf_op | source)
XLA Modules:
  0.0 134.0 jit_solution(18379057985221320082)
XLA Ops:
  0.0 2.3 %borders.1 = (bf16[16,64,128]{2,1,0:T(8,128)(2,1)}, bf16[16,80,128]{2,1,0:T(8,128)(2,1)}, bf16[16,144,128]{2,1,0:T(8,128)(2,1)}) custom-call(s32[1]{0:T(128)} %bitcast.odd_ref.pick_ref, bf16[128,144,128]{2,1,0:T(8,128)(2,1)} %x_ref.9), custom_call_target="tpu_custom_call" | custom-call | flops 1 | bytes 1 | tf_op jit(solution)/shard_map/borders/pallas_call | solution.py:113
  2.3 0.1 collective-permute-start.2
  2.4 4.5 %collective-permute-start = (bf16[16,64,128]{2,1,0:T(8,128)(2,1)}, bf16[16,64,128]{2,1,0:T(8,128)(2,1)S(1)}, u32[]{:S(2)}, u32[]{:S(2)}) collective-permute-start(bf16[16,64,128]{2,1,0:T(8,128)(2,1)} %get-tuple-element.32), channel_id=1, source_target_pairs={{1,2},{2,1},{3,4},{4,3},{5,6},{6,5},{7,8},{8,7},{9,10},{10,9},{11,... | collective-permute-start | bytes 786440 | tf_op jit(solution)/shard_map/ppermute | solution.py:258
  6.9 1.9 %collective-permute-start.1 = (bf16[16,80,128]{2,1,0:T(8,128)(2,1)}, bf16[16,80,128]{2,1,0:T(8,128)(2,1)S(1)}, u32[]{:S(2)}, u32[]{:S(2)}) collective-permute-start(bf16[16,80,128]{2,1,0:T(8,128)(2,1)} %get-tuple-element.33), channel_id=1, source_target_pairs={{1,2},{2,1},{3,4},{4,3},{5,6},{6,5},{7,8},{8,7},{9,10},{10,9},{11,... | collective-permute-start | bytes 983048 | tf_op jit(solution)/shard_map/ppermute | solution.py:260
  8.8 0.1 compare_convert_fusion.1
  8.9 0.1 fusion
  9.1 0.0 copy-start.1
  9.1 0.0 copy-start.2
  9.1 0.0 copy-start.3
  9.1 1.3 slice.66.x_ref
  10.5 0.1 copy.13.band_ref
  10.5 2.8 %collective-permute-done.lo_even.hi_odd = bf16[16,64,128]{2,1,0:T(8,128)(2,1)S(1)} collective-permute-done((bf16[16,64,128]{2,1,0:T(8,128)(2,1)}, bf16[16,64,128]{2,1,0:T(8,128)(2,1)S(1)}, u32[]{:S(2)}, u32[]{:S(2)}) %collective-permute-start) | collective-permute-done | bytes 262176 | tf_op jit(solution)/shard_map/ppermute | solution.py:258
  13.3 0.1 broadcast_in_dim.7.inv_ref
  13.4 0.1 broadcast_in_dim.8.bandinv_ref
  13.5 0.0 copy-done.3
  13.5 3.4 %prepare.5.refs_0_ = bf16[2,64,32,128]{3,2,1,0:T(8,128)(2,1)S(1)} custom-call(s32[1]{0:T(128)} %bitcast.odd_ref.pick_ref, bf16[128,32,128]{2,1,0:T(8,128)(2,1)S(1)} %slice.66.x_ref, bf16[16,64,128]{2,1,0:T(8,128)(2,1)S(1)} %collective-permute-done.lo_even.hi_odd, bf16[16,144,128]{2,1,0:T(8,128)(2,1)S(1)} %collective-permute-done.2.lo_odd.hi_even, ...), custom_call_target="tpu_custom_call" | custom-call | flops 1 | bytes 1 | tf_op jit(solution)/shard_map/prepare/pallas_call | solution.py:129
  16.9 0.7 collective-permute-start.3
  17.6 2.7 %collective-permute-done.1.lo_even.hi_odd = bf16[16,80,128]{2,1,0:T(8,128)(2,1)S(1)} collective-permute-done((bf16[16,80,128]{2,1,0:T(8,128)(2,1)}, bf16[16,80,128]{2,1,0:T(8,128)(2,1)S(1)}, u32[]{:S(2)}, u32[]{:S(2)}) %collective-permute-start.1) | collective-permute-done | bytes 327712 | tf_op jit(solution)/shard_map/ppermute | solution.py:260
  20.3 2.3 %copy-done = bf16[128,144,128]{2,1,0:T(8,128)(2,1)S(1)} copy-done((bf16[128,144,128]{2,1,0:T(8,128)(2,1)S(1)}, bf16[128,144,128]{2,1,0:T(8,128)(2,1)}, u32[]{:S(2)}) %copy-start) | copy-done | bytes 4718616
  22.7 3.4 %prepare.6.refs_1_ = bf16[2,64,32,128]{3,2,1,0:T(8,128)(2,1)S(1)} custom-call(s32[1]{0:T(128)} %bitcast.odd_ref.pick_ref, bf16[128,144,128]{2,1,0:T(8,128)(2,1)S(1)} %copy-done, bf16[16,64,128]{2,1,0:T(8,128)(2,1)S(1)} %collective-permute-done.lo_even.hi_odd, bf16[16,144,128]{2,1,0:T(8,128)(2,1)S(1)} %collective-permute-done.2.lo_odd.hi_even, ...), custom_call_target="tpu_custom_call" | custom-call | flops 1 | bytes 1 | tf_op jit(solution)/shard_map/prepare/pallas_call | solution.py:129
  26.0 0.7 collective-permute-start.4
  26.8 3.4 %prepare.7.refs_2_ = bf16[2,64,32,128]{3,2,1,0:T(8,128)(2,1)S(1)} custom-call(s32[1]{0:T(128)} %bitcast.odd_ref.pick_ref, bf16[128,144,128]{2,1,0:T(8,128)(2,1)S(1)} %copy-done, bf16[16,80,128]{2,1,0:T(8,128)(2,1)S(1)} %collective-permute-done.1.lo_even.hi_odd, bf16[16,144,128]{2,1,0:T(8,128)(2,1)S(1)} %collective-permute-done.2.lo_odd.hi_even, ...), custom_call_target="tpu_custom_call" | custom-call | flops 1 | bytes 1 | tf_op jit(solution)/shard_map/prepare/pallas_call | solution.py:129
  30.2 0.7 collective-permute-start.5
  30.9 0.1 slice_dynamic-update-slice_fusion.3
  31.0 20.7 %collective-permute-start.8 = (bf16[2,64,32,128]{3,2,1,0:T(8,128)(2,1)S(1)}, bf16[2,64,32,128]{3,2,1,0:T(8,128)(2,1)S(1)}, u32[]{:S(2)}, u32[]{:S(2)}) collective-permute-start(bf16[2,64,32,128]{3,2,1,0:T(8,128)(2,1)S(1)} %collective-permute-done.4.refs_6_), channel_id=1, source_target_pairs={{0,1},{1,0},{2,3},{3,2},{4,5},{5,4},{6,7},{7,6},{8,9},{9,8},{10,11... | collective-permute-start | bytes 3145736 | tf_op jit(solution)/shard_map/ppermute | solution.py:286
  51.7 0.1 collective-permute-start.10
  51.8 3.4 %prepare.8.refs_3_ = bf16[2,64,32,128]{3,2,1,0:T(8,128)(2,1)S(1)} custom-call(s32[1]{0:T(128)} %bitcast.odd_ref.pick_ref, bf16[128,144,128]{2,1,0:T(8,128)(2,1)S(1)} %copy-done, bf16[16,80,128]{2,1,0:T(8,128)(2,1)S(1)} %collective-permute-done.1.lo_even.hi_odd, bf16[16,144,128]{2,1,0:T(8,128)(2,1)S(1)} %collective-permute-done.2.lo_odd.hi_even, ...), custom_call_target="tpu_custom_call" | custom-call | flops 1 | bytes 1 | tf_op jit(solution)/shard_map/prepare/pallas_call | solution.py:129
  55.1 0.7 collective-permute-start.7
  55.9 0.2 slice_dynamic-update-slice_fusion.2
  56.1 0.2 slice_dynamic-update-slice_fusion.1
  56.3 1.6 %prepare.9.refs_4_ = bf16[2,64,16,128]{3,2,1,0:T(8,128)(2,1)S(1)} custom-call(s32[1]{0:T(128)} %bitcast.odd_ref.pick_ref, bf16[128,144,128]{2,1,0:T(8,128)(2,1)S(1)} %copy-done, bf16[16,80,128]{2,1,0:T(8,128)(2,1)S(1)} %collective-permute-done.1.lo_even.hi_odd, bf16[16,144,128]{2,1,0:T(8,128)(2,1)S(1)} %collective-permute-done.2.lo_odd.hi_even, ...), custom_call_target="tpu_custom_call" | custom-call | flops 1 | bytes 1 | tf_op jit(solution)/shard_map/prepare/pallas_call | solution.py:129
  57.9 0.2 slice_dynamic-update-slice_fusion
  58.0 0.1 slice_dynamic-update-slice_fusion.16
  58.1 7.3 %collective-permute-start.17 = (bf16[2,16,144,128]{3,2,1,0:T(8,128)(2,1)S(1)}, bf16[2,16,144,128]{3,2,1,0:T(8,128)(2,1)S(1)}, u32[]{:S(2)}, u32[]{:S(2)}) collective-permute-start(bf16[2,16,144,128]{3,2,1,0:T(8,128)(2,1)S(1)} %get-tuple-element.57), channel_id=1, source_target_pairs={{3,1},{5,3},{7,5},{9,7},{11,9},{13,11},{15,13},{17,15},{19,17},{21... | collective-permute-start | bytes 3538952 | tf_op jit(solution)/shard_map/ppermute | solution.py:281
  65.5 1.0 collective-permute-start.6
  66.5 7.7 %collective-permute-start.16 = (bf16[2,16,144,128]{3,2,1,0:T(8,128)(2,1)S(1)}, bf16[2,16,144,128]{3,2,1,0:T(8,128)(2,1)S(1)}, u32[]{:S(2)}, u32[]{:S(2)}) collective-permute-start(bf16[2,16,144,128]{3,2,1,0:T(8,128)(2,1)S(1)} %get-tuple-element.56), channel_id=1, source_target_pairs={{3,1},{5,3},{7,5},{9,7},{11,9},{13,11},{15,13},{17,15},{19,17},{21... | collective-permute-start | bytes 3538952 | tf_op jit(solution)/shard_map/ppermute | solution.py:281
  74.2 0.7 collective-permute-start.9
  74.9 1.9 %collective-permute-start.15 = (bf16[2,16,144,128]{3,2,1,0:T(8,128)(2,1)S(1)}, bf16[2,16,144,128]{3,2,1,0:T(8,128)(2,1)S(1)}, u32[]{:S(2)}, u32[]{:S(2)}) collective-permute-start(bf16[2,16,144,128]{3,2,1,0:T(8,128)(2,1)S(1)} %get-tuple-element.55), channel_id=1, source_target_pairs={{3,1},{5,3},{7,5},{9,7},{11,9},{13,11},{15,13},{17,15},{19,17},{21... | collective-permute-start | bytes 3538952 | tf_op jit(solution)/shard_map/ppermute | solution.py:281
  76.9 1.9 %collective-permute-start.11 = (bf16[2,16,144,128]{3,2,1,0:T(8,128)(2,1)S(1)}, bf16[2,16,144,128]{3,2,1,0:T(8,128)(2,1)S(1)}, u32[]{:S(2)}, u32[]{:S(2)}) collective-permute-start(bf16[2,16,144,128]{3,2,1,0:T(8,128)(2,1)S(1)} %get-tuple-element.52), channel_id=1, source_target_pairs={{3,1},{5,3},{7,5},{9,7},{11,9},{13,11},{15,13},{17,15},{19,17},{21... | collective-permute-start | bytes 3538952 | tf_op jit(solution)/shard_map/ppermute | solution.py:281
  78.8 26.2 %collective-permute-start.13 = (bf16[2,64,32,128]{3,2,1,0:T(8,128)(2,1)S(1)}, bf16[2,64,32,128]{3,2,1,0:T(8,128)(2,1)S(1)}, u32[]{:S(2)}, u32[]{:S(2)}) collective-permute-start(bf16[2,64,32,128]{3,2,1,0:T(8,128)(2,1)S(1)} %collective-permute-done.7.refs_8_), channel_id=1, source_target_pairs={{0,1},{1,0},{2,3},{3,2},{4,5},{5,4},{6,7},{7,6},{8,9},{9,8},{10,11... | collective-permute-start | bytes 3145736 | tf_op jit(solution)/shard_map/ppermute | solution.py:286
  105.1 1.0 collective-permute-done.16.refs_10_
  106.1 2.8 %correlate.5.refs_11_ = bf16[128,2,2,64,128]{4,3,2,1,0:T(8,128)(2,1)} custom-call(s32[1]{0:T(128)} %bitcast.odd_ref.pick_ref, bf16[2,64,32,128]{3,2,1,0:T(8,128)(2,1)S(1)} %prepare.5.refs_0_, bf16[2,64,32,128]{3,2,1,0:T(8,128)(2,1)S(1)} %prepare.6.refs_1_, bf16[2,64,32,128]{3,2,1,0:T(8,128)(2,1)S(1)} %prepare.7.refs_2_, ...), custom_call_target="tpu_custom_call" | custom-call | flops 1 | bytes 1 | tf_op jit(solution)/shard_map/correlate/pallas_call | solution.py:204
  108.9 2.7 %correlate.6.refs_11_ = bf16[128,2,2,64,128]{4,3,2,1,0:T(8,128)(2,1)} custom-call(s32[1]{0:T(128)} %bitcast.odd_ref.pick_ref, bf16[2,64,32,128]{3,2,1,0:T(8,128)(2,1)S(1)} %prepare.5.refs_0_, bf16[2,64,32,128]{3,2,1,0:T(8,128)(2,1)S(1)} %prepare.6.refs_1_, bf16[2,64,32,128]{3,2,1,0:T(8,128)(2,1)S(1)} %prepare.7.refs_2_, ...), custom_call_target="tpu_custom_call", output_to_operand_aliasing={{}: (12, {})} | custom-call | flops 1 | bytes 1 | tf_op jit(solution)/shard_map/correlate/pallas_call | solution.py:204
  111.6 7.1 %collective-permute-done.15.refs_10_ = bf16[2,16,144,128]{3,2,1,0:T(8,128)(2,1)S(1)} collective-permute-done((bf16[2,16,144,128]{3,2,1,0:T(8,128)(2,1)S(1)}, bf16[2,16,144,128]{3,2,1,0:T(8,128)(2,1)S(1)}, u32[]{:S(2)}, u32[]{:S(2)}) %collective-permute-start.15) | collective-permute-done | bytes 1179680 | tf_op jit(solution)/shard_map/ppermute | solution.py:281
  118.7 2.7 %correlate.7.refs_10_ = bf16[128,2,2,64,128]{4,3,2,1,0:T(8,128)(2,1)} custom-call(s32[1]{0:T(128)} %bitcast.odd_ref.pick_ref, bf16[2,64,32,128]{3,2,1,0:T(8,128)(2,1)S(1)} %prepare.5.refs_0_, bf16[2,64,32,128]{3,2,1,0:T(8,128)(2,1)S(1)} %prepare.6.refs_1_, bf16[2,64,32,128]{3,2,1,0:T(8,128)(2,1)S(1)} %prepare.7.refs_2_, ...), custom_call_target="tpu_custom_call", output_to_operand_aliasing={{}: (12, {})} | custom-call | flops 1 | bytes 1 | tf_op jit(solution)/shard_map/correlate/pallas_call | solution.py:204
  121.4 7.9 %correlate.8.refs_11_ = bf16[128,2,2,64,128]{4,3,2,1,0:T(8,128)(2,1)} custom-call(bf16[2,64,32,128]{3,2,1,0:T(8,128)(2,1)S(1)} %prepare.5.refs_0_, bf16[2,64,32,128]{3,2,1,0:T(8,128)(2,1)S(1)} %prepare.6.refs_1_, bf16[2,64,32,128]{3,2,1,0:T(8,128)(2,1)S(1)} %prepare.7.refs_2_, ...), custom_call_target="tpu_custom_call", output_to_operand_aliasing={{}: (10, {})} | custom-call | flops 1 | bytes 1 | tf_op jit(solution)/shard_map/correlate/pallas_call | solution.py:204
  129.2 2.1 %collective-permute-done.11.refs_10_ = bf16[2,16,144,128]{3,2,1,0:T(8,128)(2,1)S(1)} collective-permute-done((bf16[2,16,144,128]{3,2,1,0:T(8,128)(2,1)S(1)}, bf16[2,16,144,128]{3,2,1,0:T(8,128)(2,1)S(1)}, u32[]{:S(2)}, u32[]{:S(2)}) %collective-permute-start.11) | collective-permute-done | bytes 1179680 | tf_op jit(solution)/shard_map/ppermute | solution.py:281
  131.4 2.7 %correlate.9 = bf16[128,2,2,64,128]{4,3,2,1,0:T(8,128)(2,1)} custom-call(s32[1]{0:T(128)} %bitcast.odd_ref.pick_ref, bf16[2,64,32,128]{3,2,1,0:T(8,128)(2,1)S(1)} %prepare.5.refs_0_, bf16[2,64,32,128]{3,2,1,0:T(8,128)(2,1)S(1)} %prepare.6.refs_1_, bf16[2,64,32,128]{3,2,1,0:T(8,128)(2,1)S(1)} %prepare.7.refs_2_, ...), custom_call_target="tpu_custom_call", output_to_operand_aliasing={{}: (12, {})} | custom-call | flops 1 | bytes 1 | tf_op jit(solution)/shard_map/correlate/pallas_call | solution.py:204
  (28 shorter events, 0.1 us)
Async XLA Ops:
  0.0 8.8 %copy-start.5 = (s32[64]{0:T(128)S(1)}, s32[64]{0:T(128)}, u32[]{:S(2)}) copy-start(s32[64]{0:T(128)} %param.9) | copy-start | bytes 772
  0.0 9.0 %copy-start.4 = (pred[128,160]{1,0:T(32,128)(4,1)S(1)}, pred[128,160]{1,0:T(32,128)(4,1)}, u32[]{:S(2)}) copy-start(pred[128,160]{1,0:T(32,128)(4,1)} %constant.47.clone) | copy-start | bytes 61444
  2.3 11.1 %collective-permute-start.2 = (bf16[16,144,128]{2,1,0:T(8,128)(2,1)}, bf16[16,144,128]{2,1,0:T(8,128)(2,1)S(1)}, u32[]{:S(2)}, u32[]{:S(2)}) collective-permute-start(bf16[16,144,128]{2,1,0:T(8,128)(2,1)} %get-tuple-element.34), channel_id=1, source_target_pairs={{0,1},{1,0},{2,3},{3,2},{4,5},{5,4},{6,7},{7,6},{8,9},{9,8},{10,11... | collective-permute-start | bytes 1769480 | tf_op jit(solution)/shard_map/ppermute | solution.py:259
  2.4 10.9 %collective-permute-start = (bf16[16,64,128]{2,1,0:T(8,128)(2,1)}, bf16[16,64,128]{2,1,0:T(8,128)(2,1)S(1)}, u32[]{:S(2)}, u32[]{:S(2)}) collective-permute-start(bf16[16,64,128]{2,1,0:T(8,128)(2,1)} %get-tuple-element.32), channel_id=1, source_target_pairs={{1,2},{2,1},{3,4},{4,3},{5,6},{6,5},{7,8},{8,7},{9,10},{10,9},{11,... | collective-permute-start | bytes 786440 | tf_op jit(solution)/shard_map/ppermute | solution.py:258
  6.9 13.4 %collective-permute-start.1 = (bf16[16,80,128]{2,1,0:T(8,128)(2,1)}, bf16[16,80,128]{2,1,0:T(8,128)(2,1)S(1)}, u32[]{:S(2)}, u32[]{:S(2)}) collective-permute-start(bf16[16,80,128]{2,1,0:T(8,128)(2,1)} %get-tuple-element.33), channel_id=1, source_target_pairs={{1,2},{2,1},{3,4},{4,3},{5,6},{6,5},{7,8},{8,7},{9,10},{10,9},{11,... | collective-permute-start | bytes 983048 | tf_op jit(solution)/shard_map/ppermute | solution.py:260
  9.1 4.4 %copy-start.1 = (bf16[128,128]{1,0:T(8,128)(2,1)S(1)}, bf16[128,128]{1,0:T(8,128)(2,1)}, u32[]{:S(2)}) copy-start(bf16[128,128]{1,0:T(8,128)(2,1)} %constant.48.clone.ram_ref) | copy-start | bytes 98308
  9.1 4.4 %copy-start.2 = (bf16[128,128]{1,0:T(8,128)(2,1)S(1)}, bf16[128,128]{1,0:T(8,128)(2,1)}, u32[]{:S(2)}) copy-start(bf16[128,128]{1,0:T(8,128)(2,1)} %constant.50.clone.table_ref) | copy-start | bytes 98308
  9.1 4.4 %copy-start.3 = (f32[1,128]{1,0:T(1,128)S(1)}, f32[1,128]{1,0:T(1,128)}, u32[]{:S(2)}) copy-start(f32[1,128]{1,0:T(1,128)} %constant.49.clone.raminv_ref) | copy-start | bytes 1540
  16.9 9.9 %collective-permute-start.3 = (bf16[2,64,32,128]{3,2,1,0:T(8,128)(2,1)S(1)}, bf16[2,64,32,128]{3,2,1,0:T(8,128)(2,1)S(1)}, u32[]{:S(2)}, u32[]{:S(2)}) collective-permute-start(bf16[2,64,32,128]{3,2,1,0:T(8,128)(2,1)S(1)} %prepare.5.refs_0_), channel_id=1, source_target_pairs={{2,0},{1,1},{4,2},{3,3},{6,4},{5,5},{8,6},{7,7},{10,8},{9,9},{12,1... | collective-permute-start | bytes 3145736 | tf_op jit(solution)/shard_map/ppermute | solution.py:274
  20.3 2.3 %copy-start = (bf16[128,144,128]{2,1,0:T(8,128)(2,1)S(1)}, bf16[128,144,128]{2,1,0:T(8,128)(2,1)}, u32[]{:S(2)}) copy-start(bf16[128,144,128]{2,1,0:T(8,128)(2,1)} %x_ref.9) | copy-start | bytes 14155780
  26.0 5.0 %collective-permute-start.4 = (bf16[2,64,32,128]{3,2,1,0:T(8,128)(2,1)S(1)}, bf16[2,64,32,128]{3,2,1,0:T(8,128)(2,1)S(1)}, u32[]{:S(2)}, u32[]{:S(2)}) collective-permute-start(bf16[2,64,32,128]{3,2,1,0:T(8,128)(2,1)S(1)} %prepare.6.refs_1_), channel_id=1, source_target_pairs={{2,0},{1,1},{4,2},{3,3},{6,4},{5,5},{8,6},{7,7},{10,8},{9,9},{12,1... | collective-permute-start | bytes 3145736 | tf_op jit(solution)/shard_map/ppermute | solution.py:274
  30.2 26.1 %collective-permute-start.5 = (bf16[2,64,32,128]{3,2,1,0:T(8,128)(2,1)S(1)}, bf16[2,64,32,128]{3,2,1,0:T(8,128)(2,1)S(1)}, u32[]{:S(2)}, u32[]{:S(2)}) collective-permute-start(bf16[2,64,32,128]{3,2,1,0:T(8,128)(2,1)S(1)} %prepare.7.refs_2_), channel_id=1, source_target_pairs={{2,0},{1,1},{4,2},{3,3},{6,4},{5,5},{8,6},{7,7},{10,8},{9,9},{12,1... | collective-permute-start | bytes 3145736 | tf_op jit(solution)/shard_map/ppermute | solution.py:274
  31.0 43.9 %collective-permute-start.8 = (bf16[2,64,32,128]{3,2,1,0:T(8,128)(2,1)S(1)}, bf16[2,64,32,128]{3,2,1,0:T(8,128)(2,1)S(1)}, u32[]{:S(2)}, u32[]{:S(2)}) collective-permute-start(bf16[2,64,32,128]{3,2,1,0:T(8,128)(2,1)S(1)} %collective-permute-done.4.refs_6_), channel_id=1, source_target_pairs={{0,1},{1,0},{2,3},{3,2},{4,5},{5,4},{6,7},{7,6},{8,9},{9,8},{10,11... | collective-permute-start | bytes 3145736 | tf_op jit(solution)/shard_map/ppermute | solution.py:286
  51.7 6.5 %collective-permute-start.10 = (bf16[16,128]{1,0:T(8,128)(2,1)S(1)}, bf16[16,128]{1,0:T(8,128)(2,1)S(1)}, u32[]{:S(2)}, u32[]{:S(2)}) collective-permute-start(bf16[16,128]{1,0:T(8,128)(2,1)S(1)} %slice_bitcast_fusion), channel_id=1, source_target_pairs={{0,1},{1,0},{2,3},{3,2},{4,5},{5,4},{6,7},{7,6},{8,9},{9,8},{10,11... | collective-permute-start | bytes 12296 | tf_op jit(solution)/shard_map/ppermute | solution.py:276
  55.1 19.1 %collective-permute-start.7 = (bf16[2,64,32,128]{3,2,1,0:T(8,128)(2,1)S(1)}, bf16[2,64,32,128]{3,2,1,0:T(8,128)(2,1)S(1)}, u32[]{:S(2)}, u32[]{:S(2)}) collective-permute-start(bf16[2,64,32,128]{3,2,1,0:T(8,128)(2,1)S(1)} %prepare.8.refs_3_), channel_id=1, source_target_pairs={{2,0},{1,1},{4,2},{3,3},{6,4},{5,5},{8,6},{7,7},{10,8},{9,9},{12,1... | collective-permute-start | bytes 3145736 | tf_op jit(solution)/shard_map/ppermute | solution.py:274
  58.1 46.9 %collective-permute-start.17 = (bf16[2,16,144,128]{3,2,1,0:T(8,128)(2,1)S(1)}, bf16[2,16,144,128]{3,2,1,0:T(8,128)(2,1)S(1)}, u32[]{:S(2)}, u32[]{:S(2)}) collective-permute-start(bf16[2,16,144,128]{3,2,1,0:T(8,128)(2,1)S(1)} %get-tuple-element.57), channel_id=1, source_target_pairs={{3,1},{5,3},{7,5},{9,7},{11,9},{13,11},{15,13},{17,15},{19,17},{21... | collective-permute-start | bytes 3538952 | tf_op jit(solution)/shard_map/ppermute | solution.py:281
  65.5 11.4 %collective-permute-start.6 = (bf16[2,64,32,128]{3,2,1,0:T(8,128)(2,1)S(1)}, bf16[2,64,32,128]{3,2,1,0:T(8,128)(2,1)S(1)}, u32[]{:S(2)}, u32[]{:S(2)}) collective-permute-start(bf16[2,64,32,128]{3,2,1,0:T(8,128)(2,1)S(1)} %collective-permute-done.3.refs_5_), channel_id=1, source_target_pairs={{0,1},{1,0},{2,3},{3,2},{4,5},{5,4},{6,7},{7,6},{8,9},{9,8},{10,11... | collective-permute-start | bytes 3145736 | tf_op jit(solution)/shard_map/ppermute | solution.py:286
  66.5 39.6 %collective-permute-start.16 = (bf16[2,16,144,128]{3,2,1,0:T(8,128)(2,1)S(1)}, bf16[2,16,144,128]{3,2,1,0:T(8,128)(2,1)S(1)}, u32[]{:S(2)}, u32[]{:S(2)}) collective-permute-start(bf16[2,16,144,128]{3,2,1,0:T(8,128)(2,1)S(1)} %get-tuple-element.56), channel_id=1, source_target_pairs={{3,1},{5,3},{7,5},{9,7},{11,9},{13,11},{15,13},{17,15},{19,17},{21... | collective-permute-start | bytes 3538952 | tf_op jit(solution)/shard_map/ppermute | solution.py:281
  74.2 4.6 %collective-permute-start.9 = (bf16[2,64,16,128]{3,2,1,0:T(8,128)(2,1)S(1)}, bf16[2,64,16,128]{3,2,1,0:T(8,128)(2,1)S(1)}, u32[]{:S(2)}, u32[]{:S(2)}) collective-permute-start(bf16[2,64,16,128]{3,2,1,0:T(8,128)(2,1)S(1)} %prepare.9.refs_4_), channel_id=1, source_target_pairs={{2,0},{1,1},{4,2},{3,3},{6,4},{5,5},{8,6},{7,7},{10,8},{9,9},{12,1... | collective-permute-start | bytes 1572872 | tf_op jit(solution)/shard_map/ppermute | solution.py:274
  74.9 43.8 %collective-permute-start.15 = (bf16[2,16,144,128]{3,2,1,0:T(8,128)(2,1)S(1)}, bf16[2,16,144,128]{3,2,1,0:T(8,128)(2,1)S(1)}, u32[]{:S(2)}, u32[]{:S(2)}) collective-permute-start(bf16[2,16,144,128]{3,2,1,0:T(8,128)(2,1)S(1)} %get-tuple-element.55), channel_id=1, source_target_pairs={{3,1},{5,3},{7,5},{9,7},{11,9},{13,11},{15,13},{17,15},{19,17},{21... | collective-permute-start | bytes 3538952 | tf_op jit(solution)/shard_map/ppermute | solution.py:281
  76.9 54.5 %collective-permute-start.11 = (bf16[2,16,144,128]{3,2,1,0:T(8,128)(2,1)S(1)}, bf16[2,16,144,128]{3,2,1,0:T(8,128)(2,1)S(1)}, u32[]{:S(2)}, u32[]{:S(2)}) collective-permute-start(bf16[2,16,144,128]{3,2,1,0:T(8,128)(2,1)S(1)} %get-tuple-element.52), channel_id=1, source_target_pairs={{3,1},{5,3},{7,5},{9,7},{11,9},{13,11},{15,13},{17,15},{19,17},{21... | collective-permute-start | bytes 3538952 | tf_op jit(solution)/shard_map/ppermute | solution.py:281
  78.8 42.6 %collective-permute-start.13 = (bf16[2,64,32,128]{3,2,1,0:T(8,128)(2,1)S(1)}, bf16[2,64,32,128]{3,2,1,0:T(8,128)(2,1)S(1)}, u32[]{:S(2)}, u32[]{:S(2)}) collective-permute-start(bf16[2,64,32,128]{3,2,1,0:T(8,128)(2,1)S(1)} %collective-permute-done.7.refs_8_), channel_id=1, source_target_pairs={{0,1},{1,0},{2,3},{3,2},{4,5},{5,4},{6,7},{7,6},{8,9},{9,8},{10,11... | collective-permute-start | bytes 3145736 | tf_op jit(solution)/shard_map/ppermute | solution.py:286
  105.0 16.3 %collective-permute-start.12 = (bf16[2,64,32,128]{3,2,1,0:T(8,128)(2,1)S(1)}, bf16[2,64,32,128]{3,2,1,0:T(8,128)(2,1)S(1)}, u32[]{:S(2)}, u32[]{:S(2)}) collective-permute-start(bf16[2,64,32,128]{3,2,1,0:T(8,128)(2,1)S(1)} %collective-permute-done.5.refs_7_), channel_id=1, source_target_pairs={{0,1},{1,0},{2,3},{3,2},{4,5},{5,4},{6,7},{7,6},{8,9},{9,8},{10,11... | collective-permute-start | bytes 3145736 | tf_op jit(solution)/shard_map/ppermute | solution.py:286
  106.1 15.3 %collective-permute-start.14 = (bf16[2,64,16,128]{3,2,1,0:T(8,128)(2,1)S(1)}, bf16[2,64,16,128]{3,2,1,0:T(8,128)(2,1)S(1)}, u32[]{:S(2)}, u32[]{:S(2)}) collective-permute-start(bf16[2,64,16,128]{3,2,1,0:T(8,128)(2,1)S(1)} %collective-permute-done.9.refs_9_), channel_id=1, source_target_pairs={{0,1},{1,0},{2,3},{3,2},{4,5},{5,4},{6,7},{7,6},{8,9},{9,8},{10,11... | collective-permute-start | bytes 1572872 | tf_op jit(solution)/shard_map/ppermute | solution.py:286

commit v3 on v2

--- a/solution.py
+++ b/solution.py
@@ -18,6 +18,7 @@
 
 STEP = 16
 BINS_STEP = 16
+PITCH = 24
 GROUP = 16
 VMEM = 32 * 1024 * 1024
 CHUNKS = (2, 2, 2, 2, 1)
@@ -30,25 +31,25 @@
 def prepare_kernel(odd_ref, x_ref, lo_even, lo_odd, hi_even, hi_odd, sel_ref, inv_ref, ram_ref, raminv_ref,
                    table_ref, band_ref, bandinv_ref, out_ref, ext, wide):
     channels, step, samples = x_ref.shape
-    rows = channels * step
-    side = HW * step
     odd = odd_ref[0] != 0
+    ext_rows = ext.reshape(ext.shape[0] * PITCH, samples)
+    wide_rows = wide.reshape(wide.shape[0] * PITCH, channels)
 
     def put(at, ref):
-        count = ref.shape[0] * step
-        ext[at : at + count, :] = ref[...].astype(jnp.float32).reshape(count, samples)
+        count = ref.shape[0]
+        ext[at : at + count, :step, :] = ref[...].astype(jnp.float32)
 
     @pl.when(odd)
     def _():
         put(0, lo_odd)
-        put(side + rows, hi_odd)
+        put(HW + channels, hi_odd)
 
     @pl.when(jnp.logical_not(odd))
     def _():
         put(0, lo_even)
-        put(side + rows, hi_even)
-
-    put(side, x_ref)
+        put(HW + channels, hi_even)
+
+    put(HW, x_ref)
     sel = sel_ref[...]
     inv = inv_ref[...]
     ram = ram_ref[...]
@@ -59,7 +60,7 @@
     bins = table.shape[0] // 2
     for start in range(0, step, GROUP):
         group = range(start, start + GROUP)
-        around = [ext[pl.ds(w, channels + 2 * HW, stride=step), :] for w in group]
+        around = [ext_rows[pl.ds(w, channels + 2 * HW, stride=PITCH), :] for w in group]
         total = jnp.dot(
             sel, jnp.concatenate([a.astype(jnp.bfloat16) for a in around], axis=1), preferred_element_type=jnp.float32
         )
@@ -85,9 +86,9 @@
         for n, w in enumerate(group):
             part = slice(n * channels, (n + 1) * channels)
             scale = lax.rsqrt(jnp.maximum(band_sum[:, part] * bandinv, FLOOR))
-            wide[pl.ds(w, bins, stride=step), :] = re[:, part] * scale
-            wide[pl.ds(bins * step + w, bins, stride=step), :] = im[:, part] * scale
-    out_ref[...] = wide[...].reshape(2, bins, step, channels).astype(out_ref.dtype)
+            wide_rows[pl.ds(w, bins, stride=PITCH), :] = re[:, part] * scale
+            wide_rows[pl.ds(bins * PITCH + w, bins, stride=PITCH), :] = im[:, part] * scale
+    out_ref[...] = wide[:, :step, :].reshape(2, bins, step, channels).astype(out_ref.dtype)
 
 
 def borders_kernel(early, odd_ref, x_ref, first_ref, rest_ref, inner_ref, sems):
@@ -135,8 +136,8 @@
         out_specs=pl.BlockSpec((2, bins, STEP, channels), lambda i: (0, 0, i, 0)),
         out_shape=jax.ShapeDtypeStruct((2, bins, windows, channels), jnp.bfloat16),
         scratch_shapes=[
-            pltpu.VMEM(((channels + 2 * HW) * STEP, samples), jnp.float32),
-            pltpu.VMEM((2 * bins * STEP, channels), jnp.float32),
+            pltpu.VMEM((channels + 2 * HW, PITCH, samples), jnp.float32),
+            pltpu.VMEM((2 * bins, PITCH, channels), jnp.float32),
         ],
         compiler_params=pltpu.CompilerParams(vmem_limit_bytes=VMEM),
         cost_estimate=pl.CostEstimate(flops=1, bytes_accessed=1, transcendentals=0),
@@ -165,8 +166,8 @@
             by_im = lax.dot_general(a_im, b, dims, preferred_element_type=jnp.float32)
             re = by_re[:, :channels] + by_im[:, channels:]
             im = by_im[:, :channels] - by_re[:, channels:]
-            wide[0, pl.ds(k, channels, stride=step), :] = re * scale
-            wide[1, pl.ds(k, channels, stride=step), :] = im * scale
+            wide[0, pl.ds(k, channels, stride=PITCH), :] = re * scale
+            wide[1, pl.ds(k, channels, stride=PITCH), :] = im * scale
 
     if far is None:
         run(partner)
@@ -174,7 +175,7 @@
         pl.when(pick_ref[0] == 0)(lambda: run(partner))
         pl.when(pick_ref[0] != 0)(lambda: run([far]))
     for part in range(2):
-        out_ref[:, 0, part] = wide[part].reshape(channels, step, channels).astype(out_ref.dtype)
+        out_ref[:, 0, part] = wide[part].reshape(channels, PITCH, channels)[:, :step].astype(out_ref.dtype)
 
 
 def correlate(own, partner, round_index, first_bin, bins, pick=None, far=None, target=None, after=None):
@@ -207,11 +208,82 @@
         in_specs=specs,
         out_specs=pl.BlockSpec((channels, 1, 2, BINS_STEP, channels), lambda i: (0, round_index, 0, base + i, 0)),
         out_shape=jax.ShapeDtypeStruct((channels, ROUNDS, 2, total_bins, channels), jnp.bfloat16),
-        scratch_shapes=[pltpu.VMEM((2, channels * BINS_STEP, channels), jnp.float32)],
+        scratch_shapes=[pltpu.VMEM((2, channels * PITCH, channels), jnp.float32)],
         input_output_aliases=aliases,
         compiler_params=pltpu.CompilerParams(vmem_limit_bytes=VMEM),
         cost_estimate=pl.CostEstimate(flops=1, bytes_accessed=1, transcendentals=0),
         name="correlate",
+    )(*operands)
+
+
+def correlate_chunk_kernel(n_own, n_partner, scale, first_bin, round_index, pick_ref, *refs):
+    own = refs[:n_own]
+    partner = refs[n_own : n_own + n_partner]
+    far = refs[n_own + n_partner]
+    out_ref, wide, done, sems = refs[-4:]
+    _, bins, _, channels = far.shape
+    pitch_rows = wide.reshape(2, channels * PITCH, channels)
+
+    def whole(group, part, k):
+        pieces = [ref[part, k] for ref in group]
+        return pieces[0] if len(pieces) == 1 else jnp.concatenate(pieces, axis=0)
+
+    def run(partner, base):
+        for k in range(bins):
+            a_re, a_im = whole(own, 0, first_bin + k), whole(own, 1, first_bin + k)
+            b = jnp.concatenate([whole(partner, 0, base + k), whole(partner, 1, base + k)], axis=1)
+            dims = (((0,), (0,)), ((), ()))
+            by_re = lax.dot_general(a_re, b, dims, preferred_element_type=jnp.float32)
+            by_im = lax.dot_general(a_im, b, dims, preferred_element_type=jnp.float32)
+            re = by_re[:, :channels] + by_im[:, channels:]
+            im = by_im[:, :channels] - by_re[:, channels:]
+            pitch_rows[0, pl.ds(k, channels, stride=PITCH), :] = re * scale
+            pitch_rows[1, pl.ds(k, channels, stride=PITCH), :] = im * scale
+
+    pl.when(pick_ref[0] == 0)(lambda: run(partner, first_bin))
+    pl.when(pick_ref[0] != 0)(lambda: run([far], 0))
+    copies = []
+    for part in range(2):
+        done[part] = wide[part, :, :bins, :].astype(done.dtype)
+        copies.append(
+            pltpu.make_async_copy(
+                done.at[part], out_ref.at[:, round_index, part, pl.ds(first_bin, bins), :], sems.at[part]
+            )
+        )
+        copies[-1].start()
+    for copy in copies:
+        copy.wait()
+
+
+def correlate_chunk(own, partner, round_index, first_bin, pick, far, target, after):
+    _, bins, windows, channels = far.shape
+    total_bins = own[0].shape[1]
+    operands = [pick, *own, *partner, far]
+    specs = [pl.BlockSpec(memory_space=pltpu.SMEM)]
+    specs += [pl.BlockSpec(memory_space=pltpu.VMEM)] * (len(operands) - 1)
+    aliases = {}
+    if target is not None:
+        aliases = {len(operands): 0}
+        operands.append(target)
+        specs.append(pl.BlockSpec(memory_space=pl.ANY))
+    operands.append(after)
+    specs.append(pl.BlockSpec(memory_space=pl.ANY))
+    return pl.pallas_call(
+        functools.partial(
+            correlate_chunk_kernel, len(own), len(partner), 1.0 / math.sqrt(windows), first_bin, round_index
+        ),
+        in_specs=specs,
+        out_specs=pl.BlockSpec(memory_space=pl.ANY),
+        out_shape=jax.ShapeDtypeStruct((channels, ROUNDS, 2, total_bins, channels), jnp.bfloat16),
+        scratch_shapes=[
+            pltpu.VMEM((2, channels, PITCH, channels), jnp.float32),
+            pltpu.VMEM((2, channels, bins, channels), jnp.bfloat16),
+            pltpu.SemaphoreType.DMA((2,)),
+        ],
+        input_output_aliases=aliases,
+        compiler_params=pltpu.CompilerParams(vmem_limit_bytes=VMEM),
+        cost_estimate=pl.CostEstimate(flops=1, bytes_accessed=1, transcendentals=0),
+        name="correlate_chunk",
     )(*operands)
 
 
@@ -288,7 +360,7 @@
     for n, first in enumerate(range(0, bins, BINS_STEP)):
         if n == FIRST_ROUND_AFTER:
             out = correlate(own, other, 0, 0, bins, target=out)
-        out = correlate(own, held, 1, first, BINS_STEP, pick, far[n], out, token)
+        out = correlate_chunk(own, held, 1, first, pick, far[n], out, token)
     return out
 
 

time: 134 us -> 133 us (level)
  Pallas kernels: 36 us -> 27.9 us
  waiting for transfers between devices: 15.8 us -> 20.5 us
    pallas_call x5 -> x1, Pallas kernels: 18.7 us -> 5.62 us  [correlate(): pl.pallas_call(kernel, grid=(steps,), in_specs=specs, out_specs=pl.BlockS...]
    pallas_call x0 -> x4, Pallas kernels: none -> 7.92 us  [correlate_chunk(): pl.pallas_call(functools.partial(correlate_chunk_kernel, len(own), len(pa...]
    ppermute x4, waiting for transfers between devices: 10.3 us -> 14.3 us  [per_device(): far.append(lax.ppermute(mine, 'blk', second_pairs))]
    pallas_call x5, Pallas kernels: 15.1 us -> 12.1 us  [prepare(): pl.pallas_call(prepare_kernel, grid=(windows // STEP,), in_specs=[pl.Bloc...]
  transfers between devices with their start and end apart: 18 -> 18, of which waited for: 5 -> 5; matrix products, arithmetic and copies ran while one was open for 2% -> 2% of each run, Pallas kernels for 23% -> 18%
where the time goes in v3:
time: 133 us; the launch traced here: 132 us
  starting transfers between devices  78.3 us (59%)
  Pallas kernels  27.9 us (21%)
  waiting for transfers between devices  20.5 us (15%)
  local copies, waits for them, and re-layouts  4.61 us (3%)
    ppermute x5, starting transfers between devices, per_device(): other.append(lax.ppermute(held[n], 'blk', swap))  49 us
    ppermute x4, starting transfers between devices, per_device(): far.append(lax.ppermute(mine, 'blk', second_pairs))  19.2 us
    ppermute x4, waiting for transfers between devices, per_device(): far.append(lax.ppermute(mine, 'blk', second_pairs))  14.3 us
    pallas_call x5, Pallas kernels, prepare(): pl.pallas_call(prepare_kernel, grid=(windows // STEP,), in_specs=[pl.Bloc...  12.1 us
    pallas_call x4, Pallas kernels, correlate_chunk(): pl.pallas_call(functools.partial(correlate_chunk_kernel, len(own), len(pa...  7.92 us
    pallas_call x1, Pallas kernels, correlate(): pl.pallas_call(kernel, grid=(steps,), in_specs=specs, out_specs=pl.BlockS...  5.62 us
    ppermute x1, starting transfers between devices, per_device(): across_first = lax.ppermute(outer_first, 'blk', cross)  4.46 us
    ppermute x5, starting transfers between devices, per_device(): held.append(lax.ppermute(own[-1], 'blk', first_pairs))  3.61 us
  transfers between devices with their start and end apart: 18, of which 5 were waited for; matrix products, arithmetic and copies ran while one was open for 2% of the time, Pallas kernels for 18%

profile of v3, /device:TPU:1, one launch (start us, length us, event | category | flops | bytes accessed | tf_op | source)
XLA Modules:
  0.0 132.1 jit_solution(7911727606892044144)
XLA Ops:
  0.0 2.3 %borders.1 = (bf16[16,64,128]{2,1,0:T(8,128)(2,1)}, bf16[16,80,128]{2,1,0:T(8,128)(2,1)}, bf16[16,144,128]{2,1,0:T(8,128)(2,1)}) custom-call(s32[1]{0:T(128)} %bitcast.odd_ref.pick_ref, bf16[128,144,128]{2,1,0:T(8,128)(2,1)} %x_ref.9), custom_call_target="tpu_custom_call" | custom-call | flops 1 | bytes 1 | tf_op jit(solution)/shard_map/borders/pallas_call | solution.py:114
  2.3 0.1 collective-permute-start.2
  2.4 4.5 %collective-permute-start = (bf16[16,64,128]{2,1,0:T(8,128)(2,1)}, bf16[16,64,128]{2,1,0:T(8,128)(2,1)S(1)}, u32[]{:S(2)}, u32[]{:S(2)}) collective-permute-start(bf16[16,64,128]{2,1,0:T(8,128)(2,1)} %get-tuple-element.32), channel_id=1, source_target_pairs={{1,2},{2,1},{3,4},{4,3},{5,6},{6,5},{7,8},{8,7},{9,10},{10,9},{11,... | collective-permute-start | bytes 786440 | tf_op jit(solution)/shard_map/ppermute | solution.py:330
  6.9 1.9 %collective-permute-start.1 = (bf16[16,80,128]{2,1,0:T(8,128)(2,1)}, bf16[16,80,128]{2,1,0:T(8,128)(2,1)S(1)}, u32[]{:S(2)}, u32[]{:S(2)}) collective-permute-start(bf16[16,80,128]{2,1,0:T(8,128)(2,1)} %get-tuple-element.33), channel_id=1, source_target_pairs={{1,2},{2,1},{3,4},{4,3},{5,6},{6,5},{7,8},{8,7},{9,10},{10,9},{11,... | collective-permute-start | bytes 983048 | tf_op jit(solution)/shard_map/ppermute | solution.py:332
  8.8 0.1 compare_convert_fusion.1
  8.9 0.1 fusion
  9.1 0.0 copy-start.1
  9.1 0.0 copy-start.2
  9.1 0.0 copy-start.3
  9.1 1.3 slice.66.x_ref
  10.5 0.1 copy.13.band_ref
  10.5 2.8 %collective-permute-done.lo_even.hi_odd = bf16[16,64,128]{2,1,0:T(8,128)(2,1)S(1)} collective-permute-done((bf16[16,64,128]{2,1,0:T(8,128)(2,1)}, bf16[16,64,128]{2,1,0:T(8,128)(2,1)S(1)}, u32[]{:S(2)}, u32[]{:S(2)}) %collective-permute-start) | collective-permute-done | bytes 262176 | tf_op jit(solution)/shard_map/ppermute | solution.py:330
  13.3 0.1 broadcast_in_dim.7.inv_ref
  13.4 0.1 broadcast_in_dim.8.bandinv_ref
  13.5 0.0 copy-done.3
  13.5 2.7 %prepare.5.refs_0_ = bf16[2,64,32,128]{3,2,1,0:T(8,128)(2,1)S(1)} custom-call(s32[1]{0:T(128)} %bitcast.odd_ref.pick_ref, bf16[128,32,128]{2,1,0:T(8,128)(2,1)S(1)} %slice.66.x_ref, bf16[16,64,128]{2,1,0:T(8,128)(2,1)S(1)} %collective-permute-done.lo_even.hi_odd, bf16[16,144,128]{2,1,0:T(8,128)(2,1)S(1)} %collective-permute-done.2.lo_odd.hi_even, ...), custom_call_target="tpu_custom_call" | custom-call | flops 1 | bytes 1 | tf_op jit(solution)/shard_map/prepare/pallas_call | solution.py:130
  16.2 0.7 collective-permute-start.3
  17.0 3.4 %collective-permute-done.1.lo_even.hi_odd = bf16[16,80,128]{2,1,0:T(8,128)(2,1)S(1)} collective-permute-done((bf16[16,80,128]{2,1,0:T(8,128)(2,1)}, bf16[16,80,128]{2,1,0:T(8,128)(2,1)S(1)}, u32[]{:S(2)}, u32[]{:S(2)}) %collective-permute-start.1) | collective-permute-done | bytes 327712 | tf_op jit(solution)/shard_map/ppermute | solution.py:332
  20.3 2.3 %copy-done = bf16[128,144,128]{2,1,0:T(8,128)(2,1)S(1)} copy-done((bf16[128,144,128]{2,1,0:T(8,128)(2,1)S(1)}, bf16[128,144,128]{2,1,0:T(8,128)(2,1)}, u32[]{:S(2)}) %copy-start) | copy-done | bytes 4718616
  22.7 2.7 %prepare.6.refs_1_ = bf16[2,64,32,128]{3,2,1,0:T(8,128)(2,1)S(1)} custom-call(s32[1]{0:T(128)} %bitcast.odd_ref.pick_ref, bf16[128,144,128]{2,1,0:T(8,128)(2,1)S(1)} %copy-done, bf16[16,64,128]{2,1,0:T(8,128)(2,1)S(1)} %collective-permute-done.lo_even.hi_odd, bf16[16,144,128]{2,1,0:T(8,128)(2,1)S(1)} %collective-permute-done.2.lo_odd.hi_even, ...), custom_call_target="tpu_custom_call" | custom-call | flops 1 | bytes 1 | tf_op jit(solution)/shard_map/prepare/pallas_call | solution.py:130
  25.4 0.7 collective-permute-start.4
  26.1 2.7 %prepare.7.refs_2_ = bf16[2,64,32,128]{3,2,1,0:T(8,128)(2,1)S(1)} custom-call(s32[1]{0:T(128)} %bitcast.odd_ref.pick_ref, bf16[128,144,128]{2,1,0:T(8,128)(2,1)S(1)} %copy-done, bf16[16,80,128]{2,1,0:T(8,128)(2,1)S(1)} %collective-permute-done.1.lo_even.hi_odd, bf16[16,144,128]{2,1,0:T(8,128)(2,1)S(1)} %collective-permute-done.2.lo_odd.hi_even, ...), custom_call_target="tpu_custom_call" | custom-call | flops 1 | bytes 1 | tf_op jit(solution)/shard_map/prepare/pallas_call | solution.py:130
  28.9 0.7 collective-permute-start.5
  29.6 0.1 slice_dynamic-update-slice_fusion.3
  29.7 21.1 %collective-permute-start.8 = (bf16[2,64,32,128]{3,2,1,0:T(8,128)(2,1)S(1)}, bf16[2,64,32,128]{3,2,1,0:T(8,128)(2,1)S(1)}, u32[]{:S(2)}, u32[]{:S(2)}) collective-permute-start(bf16[2,64,32,128]{3,2,1,0:T(8,128)(2,1)S(1)} %collective-permute-done.4.refs_6_), channel_id=1, source_target_pairs={{0,1},{1,0},{2,3},{3,2},{4,5},{5,4},{6,7},{7,6},{8,9},{9,8},{10,11... | collective-permute-start | bytes 3145736 | tf_op jit(solution)/shard_map/ppermute | solution.py:358
  50.7 2.7 %prepare.8.refs_3_ = bf16[2,64,32,128]{3,2,1,0:T(8,128)(2,1)S(1)} custom-call(s32[1]{0:T(128)} %bitcast.odd_ref.pick_ref, bf16[128,144,128]{2,1,0:T(8,128)(2,1)S(1)} %copy-done, bf16[16,80,128]{2,1,0:T(8,128)(2,1)S(1)} %collective-permute-done.1.lo_even.hi_odd, bf16[16,144,128]{2,1,0:T(8,128)(2,1)S(1)} %collective-permute-done.2.lo_odd.hi_even, ...), custom_call_target="tpu_custom_call" | custom-call | flops 1 | bytes 1 | tf_op jit(solution)/shard_map/prepare/pallas_call | solution.py:130
  53.5 0.7 collective-permute-start.7
  54.2 0.2 slice_dynamic-update-slice_fusion.2
  54.4 0.2 slice_dynamic-update-slice_fusion.1
  54.6 1.3 prepare.9.refs_4_
  55.9 0.2 slice_dynamic-update-slice_fusion
  56.0 0.1 slice_dynamic-update-slice_fusion.16
  56.1 7.7 %collective-permute-start.17 = (bf16[2,16,144,128]{3,2,1,0:T(8,128)(2,1)S(1)}, bf16[2,16,144,128]{3,2,1,0:T(8,128)(2,1)S(1)}, u32[]{:S(2)}, u32[]{:S(2)}) collective-permute-start(bf16[2,16,144,128]{3,2,1,0:T(8,128)(2,1)S(1)} %get-tuple-element.57), channel_id=1, source_target_pairs={{3,1},{5,3},{7,5},{9,7},{11,9},{13,11},{15,13},{17,15},{19,17},{21... | collective-permute-start | bytes 3538952 | tf_op jit(solution)/shard_map/ppermute | solution.py:353
  63.8 1.0 collective-permute-start.6
  64.8 7.7 %collective-permute-start.16 = (bf16[2,16,144,128]{3,2,1,0:T(8,128)(2,1)S(1)}, bf16[2,16,144,128]{3,2,1,0:T(8,128)(2,1)S(1)}, u32[]{:S(2)}, u32[]{:S(2)}) collective-permute-start(bf16[2,16,144,128]{3,2,1,0:T(8,128)(2,1)S(1)} %get-tuple-element.56), channel_id=1, source_target_pairs={{3,1},{5,3},{7,5},{9,7},{11,9},{13,11},{15,13},{17,15},{19,17},{21... | collective-permute-start | bytes 3538952 | tf_op jit(solution)/shard_map/ppermute | solution.py:353
  72.6 0.7 collective-permute-start.9
  73.3 1.9 %collective-permute-start.15 = (bf16[2,16,144,128]{3,2,1,0:T(8,128)(2,1)S(1)}, bf16[2,16,144,128]{3,2,1,0:T(8,128)(2,1)S(1)}, u32[]{:S(2)}, u32[]{:S(2)}) collective-permute-start(bf16[2,16,144,128]{3,2,1,0:T(8,128)(2,1)S(1)} %get-tuple-element.55), channel_id=1, source_target_pairs={{3,1},{5,3},{7,5},{9,7},{11,9},{13,11},{15,13},{17,15},{19,17},{21... | collective-permute-start | bytes 3538952 | tf_op jit(solution)/shard_map/ppermute | solution.py:353
  75.2 1.9 %collective-permute-start.11 = (bf16[2,16,144,128]{3,2,1,0:T(8,128)(2,1)S(1)}, bf16[2,16,144,128]{3,2,1,0:T(8,128)(2,1)S(1)}, u32[]{:S(2)}, u32[]{:S(2)}) collective-permute-start(bf16[2,16,144,128]{3,2,1,0:T(8,128)(2,1)S(1)} %get-tuple-element.52), channel_id=1, source_target_pairs={{3,1},{5,3},{7,5},{9,7},{11,9},{13,11},{15,13},{17,15},{19,17},{21... | collective-permute-start | bytes 3538952 | tf_op jit(solution)/shard_map/ppermute | solution.py:353
  77.1 26.9 %collective-permute-start.13 = (bf16[2,64,32,128]{3,2,1,0:T(8,128)(2,1)S(1)}, bf16[2,64,32,128]{3,2,1,0:T(8,128)(2,1)S(1)}, u32[]{:S(2)}, u32[]{:S(2)}) collective-permute-start(bf16[2,64,32,128]{3,2,1,0:T(8,128)(2,1)S(1)} %collective-permute-done.7.refs_8_), channel_id=1, source_target_pairs={{0,1},{1,0},{2,3},{3,2},{4,5},{5,4},{6,7},{7,6},{8,9},{9,8},{10,11... | collective-permute-start | bytes 3145736 | tf_op jit(solution)/shard_map/ppermute | solution.py:358
  104.0 0.0 collective-permute-start.12
  104.0 0.7 collective-permute-done.16.refs_10_
  104.8 1.9 %correlate_chunk.4.refs_11_ = bf16[128,2,2,64,128]{4,3,2,1,0:T(8,128)(2,1)} custom-call(s32[1]{0:T(128)} %bitcast.odd_ref.pick_ref, bf16[2,64,32,128]{3,2,1,0:T(8,128)(2,1)S(1)} %prepare.5.refs_0_, bf16[2,64,32,128]{3,2,1,0:T(8,128)(2,1)S(1)} %prepare.6.refs_1_, bf16[2,64,32,128]{3,2,1,0:T(8,128)(2,1)S(1)} %prepare.7.refs_2_, ...), custom_call_target="tpu_custom_call" | custom-call | flops 1 | bytes 1 | tf_op jit(solution)/shard_map/correlate_chunk/pallas_call | solution.py:271
  106.7 2.1 %correlate_chunk.5.refs_11_ = bf16[128,2,2,64,128]{4,3,2,1,0:T(8,128)(2,1)} custom-call(s32[1]{0:T(128)} %bitcast.odd_ref.pick_ref, bf16[2,64,32,128]{3,2,1,0:T(8,128)(2,1)S(1)} %prepare.5.refs_0_, bf16[2,64,32,128]{3,2,1,0:T(8,128)(2,1)S(1)} %prepare.6.refs_1_, bf16[2,64,32,128]{3,2,1,0:T(8,128)(2,1)S(1)} %prepare.7.refs_2_, ...), custom_call_target="tpu_custom_call", output_to_operand_aliasing={{}: (12, {})} | custom-call | flops 1 | bytes 1 | tf_op jit(solution)/shard_map/correlate_chunk/pallas_call | solution.py:271
  108.8 8.6 %collective-permute-done.15.refs_10_ = bf16[2,16,144,128]{3,2,1,0:T(8,128)(2,1)S(1)} collective-permute-done((bf16[2,16,144,128]{3,2,1,0:T(8,128)(2,1)S(1)}, bf16[2,16,144,128]{3,2,1,0:T(8,128)(2,1)S(1)}, u32[]{:S(2)}, u32[]{:S(2)}) %collective-permute-start.15) | collective-permute-done | bytes 1179680 | tf_op jit(solution)/shard_map/ppermute | solution.py:353
  117.4 1.9 %correlate_chunk.6.refs_10_ = bf16[128,2,2,64,128]{4,3,2,1,0:T(8,128)(2,1)} custom-call(s32[1]{0:T(128)} %bitcast.odd_ref.pick_ref, bf16[2,64,32,128]{3,2,1,0:T(8,128)(2,1)S(1)} %prepare.5.refs_0_, bf16[2,64,32,128]{3,2,1,0:T(8,128)(2,1)S(1)} %prepare.6.refs_1_, bf16[2,64,32,128]{3,2,1,0:T(8,128)(2,1)S(1)} %prepare.7.refs_2_, ...), custom_call_target="tpu_custom_call", output_to_operand_aliasing={{}: (12, {})} | custom-call | flops 1 | bytes 1 | tf_op jit(solution)/shard_map/correlate_chunk/pallas_call | solution.py:271
  119.4 5.6 %correlate.1.refs_11_ = bf16[128,2,2,64,128]{4,3,2,1,0:T(8,128)(2,1)} custom-call(bf16[2,64,32,128]{3,2,1,0:T(8,128)(2,1)S(1)} %prepare.5.refs_0_, bf16[2,64,32,128]{3,2,1,0:T(8,128)(2,1)S(1)} %prepare.6.refs_1_, bf16[2,64,32,128]{3,2,1,0:T(8,128)(2,1)S(1)} %prepare.7.refs_2_, ...), custom_call_target="tpu_custom_call", output_to_operand_aliasing={{}: (10, {})} | custom-call | flops 1 | bytes 1 | tf_op jit(solution)/shard_map/correlate/pallas_call | solution.py:205
  125.0 5.0 %collective-permute-done.11.refs_10_ = bf16[2,16,144,128]{3,2,1,0:T(8,128)(2,1)S(1)} collective-permute-done((bf16[2,16,144,128]{3,2,1,0:T(8,128)(2,1)S(1)}, bf16[2,16,144,128]{3,2,1,0:T(8,128)(2,1)S(1)}, u32[]{:S(2)}, u32[]{:S(2)}) %collective-permute-start.11) | collective-permute-done | bytes 1179680 | tf_op jit(solution)/shard_map/ppermute | solution.py:353
  130.0 1.9 %correlate_chunk.7 = bf16[128,2,2,64,128]{4,3,2,1,0:T(8,128)(2,1)} custom-call(s32[1]{0:T(128)} %bitcast.odd_ref.pick_ref, bf16[2,64,32,128]{3,2,1,0:T(8,128)(2,1)S(1)} %prepare.5.refs_0_, bf16[2,64,32,128]{3,2,1,0:T(8,128)(2,1)S(1)} %prepare.6.refs_1_, bf16[2,64,32,128]{3,2,1,0:T(8,128)(2,1)S(1)} %prepare.7.refs_2_, ...), custom_call_target="tpu_custom_call", output_to_operand_aliasing={{}: (12, {})} | custom-call | flops 1 | bytes 1 | tf_op jit(solution)/shard_map/correlate_chunk/pallas_call | solution.py:271
  (28 shorter events, 0.1 us)
Async XLA Ops:
  0.0 8.8 %copy-start.5 = (s32[64]{0:T(128)S(1)}, s32[64]{0:T(128)}, u32[]{:S(2)}) copy-start(s32[64]{0:T(128)} %param.9) | copy-start | bytes 772
  0.0 9.0 %copy-start.4 = (pred[128,160]{1,0:T(32,128)(4,1)S(1)}, pred[128,160]{1,0:T(32,128)(4,1)}, u32[]{:S(2)}) copy-start(pred[128,160]{1,0:T(32,128)(4,1)} %constant.47.clone) | copy-start | bytes 61444
  2.3 11.1 %collective-permute-start.2 = (bf16[16,144,128]{2,1,0:T(8,128)(2,1)}, bf16[16,144,128]{2,1,0:T(8,128)(2,1)S(1)}, u32[]{:S(2)}, u32[]{:S(2)}) collective-permute-start(bf16[16,144,128]{2,1,0:T(8,128)(2,1)} %get-tuple-element.34), channel_id=1, source_target_pairs={{0,1},{1,0},{2,3},{3,2},{4,5},{5,4},{6,7},{7,6},{8,9},{9,8},{10,11... | collective-permute-start | bytes 1769480 | tf_op jit(solution)/shard_map/ppermute | solution.py:331
  2.4 10.9 %collective-permute-start = (bf16[16,64,128]{2,1,0:T(8,128)(2,1)}, bf16[16,64,128]{2,1,0:T(8,128)(2,1)S(1)}, u32[]{:S(2)}, u32[]{:S(2)}) collective-permute-start(bf16[16,64,128]{2,1,0:T(8,128)(2,1)} %get-tuple-element.32), channel_id=1, source_target_pairs={{1,2},{2,1},{3,4},{4,3},{5,6},{6,5},{7,8},{8,7},{9,10},{10,9},{11,... | collective-permute-start | bytes 786440 | tf_op jit(solution)/shard_map/ppermute | solution.py:330
  6.9 13.4 %collective-permute-start.1 = (bf16[16,80,128]{2,1,0:T(8,128)(2,1)}, bf16[16,80,128]{2,1,0:T(8,128)(2,1)S(1)}, u32[]{:S(2)}, u32[]{:S(2)}) collective-permute-start(bf16[16,80,128]{2,1,0:T(8,128)(2,1)} %get-tuple-element.33), channel_id=1, source_target_pairs={{1,2},{2,1},{3,4},{4,3},{5,6},{6,5},{7,8},{8,7},{9,10},{10,9},{11,... | collective-permute-start | bytes 983048 | tf_op jit(solution)/shard_map/ppermute | solution.py:332
  9.1 4.4 %copy-start.1 = (bf16[128,128]{1,0:T(8,128)(2,1)S(1)}, bf16[128,128]{1,0:T(8,128)(2,1)}, u32[]{:S(2)}) copy-start(bf16[128,128]{1,0:T(8,128)(2,1)} %constant.48.clone.ram_ref) | copy-start | bytes 98308
  9.1 4.4 %copy-start.2 = (bf16[128,128]{1,0:T(8,128)(2,1)S(1)}, bf16[128,128]{1,0:T(8,128)(2,1)}, u32[]{:S(2)}) copy-start(bf16[128,128]{1,0:T(8,128)(2,1)} %constant.50.clone.table_ref) | copy-start | bytes 98308
  9.1 4.4 %copy-start.3 = (f32[1,128]{1,0:T(1,128)S(1)}, f32[1,128]{1,0:T(1,128)}, u32[]{:S(2)}) copy-start(f32[1,128]{1,0:T(1,128)} %constant.49.clone.raminv_ref) | copy-start | bytes 1540
  16.2 9.9 %collective-permute-start.3 = (bf16[2,64,32,128]{3,2,1,0:T(8,128)(2,1)S(1)}, bf16[2,64,32,128]{3,2,1,0:T(8,128)(2,1)S(1)}, u32[]{:S(2)}, u32[]{:S(2)}) collective-permute-start(bf16[2,64,32,128]{3,2,1,0:T(8,128)(2,1)S(1)} %prepare.5.refs_0_), channel_id=1, source_target_pairs={{2,0},{1,1},{4,2},{3,3},{6,4},{5,5},{8,6},{7,7},{10,8},{9,9},{12,1... | collective-permute-start | bytes 3145736 | tf_op jit(solution)/shard_map/ppermute | solution.py:346
  20.3 2.3 %copy-start = (bf16[128,144,128]{2,1,0:T(8,128)(2,1)S(1)}, bf16[128,144,128]{2,1,0:T(8,128)(2,1)}, u32[]{:S(2)}) copy-start(bf16[128,144,128]{2,1,0:T(8,128)(2,1)} %x_ref.9) | copy-start | bytes 14155780
  25.4 4.3 %collective-permute-start.4 = (bf16[2,64,32,128]{3,2,1,0:T(8,128)(2,1)S(1)}, bf16[2,64,32,128]{3,2,1,0:T(8,128)(2,1)S(1)}, u32[]{:S(2)}, u32[]{:S(2)}) collective-permute-start(bf16[2,64,32,128]{3,2,1,0:T(8,128)(2,1)S(1)} %prepare.6.refs_1_), channel_id=1, source_target_pairs={{2,0},{1,1},{4,2},{3,3},{6,4},{5,5},{8,6},{7,7},{10,8},{9,9},{12,1... | collective-permute-start | bytes 3145736 | tf_op jit(solution)/shard_map/ppermute | solution.py:346
  28.9 25.7 %collective-permute-start.5 = (bf16[2,64,32,128]{3,2,1,0:T(8,128)(2,1)S(1)}, bf16[2,64,32,128]{3,2,1,0:T(8,128)(2,1)S(1)}, u32[]{:S(2)}, u32[]{:S(2)}) collective-permute-start(bf16[2,64,32,128]{3,2,1,0:T(8,128)(2,1)S(1)} %prepare.7.refs_2_), channel_id=1, source_target_pairs={{2,0},{1,1},{4,2},{3,3},{6,4},{5,5},{8,6},{7,7},{10,8},{9,9},{12,1... | collective-permute-start | bytes 3145736 | tf_op jit(solution)/shard_map/ppermute | solution.py:346
  29.7 43.6 %collective-permute-start.8 = (bf16[2,64,32,128]{3,2,1,0:T(8,128)(2,1)S(1)}, bf16[2,64,32,128]{3,2,1,0:T(8,128)(2,1)S(1)}, u32[]{:S(2)}, u32[]{:S(2)}) collective-permute-start(bf16[2,64,32,128]{3,2,1,0:T(8,128)(2,1)S(1)} %collective-permute-done.4.refs_6_), channel_id=1, source_target_pairs={{0,1},{1,0},{2,3},{3,2},{4,5},{5,4},{6,7},{7,6},{8,9},{9,8},{10,11... | collective-permute-start | bytes 3145736 | tf_op jit(solution)/shard_map/ppermute | solution.py:358
  50.7 5.4 %collective-permute-start.10 = (bf16[16,128]{1,0:T(8,128)(2,1)S(1)}, bf16[16,128]{1,0:T(8,128)(2,1)S(1)}, u32[]{:S(2)}, u32[]{:S(2)}) collective-permute-start(bf16[16,128]{1,0:T(8,128)(2,1)S(1)} %slice_bitcast_fusion), channel_id=1, source_target_pairs={{0,1},{1,0},{2,3},{3,2},{4,5},{5,4},{6,7},{7,6},{8,9},{9,8},{10,11... | collective-permute-start | bytes 12296 | tf_op jit(solution)/shard_map/ppermute | solution.py:348
  53.5 19.1 %collective-permute-start.7 = (bf16[2,64,32,128]{3,2,1,0:T(8,128)(2,1)S(1)}, bf16[2,64,32,128]{3,2,1,0:T(8,128)(2,1)S(1)}, u32[]{:S(2)}, u32[]{:S(2)}) collective-permute-start(bf16[2,64,32,128]{3,2,1,0:T(8,128)(2,1)S(1)} %prepare.8.refs_3_), channel_id=1, source_target_pairs={{2,0},{1,1},{4,2},{3,3},{6,4},{5,5},{8,6},{7,7},{10,8},{9,9},{12,1... | collective-permute-start | bytes 3145736 | tf_op jit(solution)/shard_map/ppermute | solution.py:346
  56.1 47.9 %collective-permute-start.17 = (bf16[2,16,144,128]{3,2,1,0:T(8,128)(2,1)S(1)}, bf16[2,16,144,128]{3,2,1,0:T(8,128)(2,1)S(1)}, u32[]{:S(2)}, u32[]{:S(2)}) collective-permute-start(bf16[2,16,144,128]{3,2,1,0:T(8,128)(2,1)S(1)} %get-tuple-element.57), channel_id=1, source_target_pairs={{3,1},{5,3},{7,5},{9,7},{11,9},{13,11},{15,13},{17,15},{19,17},{21... | collective-permute-start | bytes 3538952 | tf_op jit(solution)/shard_map/ppermute | solution.py:353
  63.8 11.4 %collective-permute-start.6 = (bf16[2,64,32,128]{3,2,1,0:T(8,128)(2,1)S(1)}, bf16[2,64,32,128]{3,2,1,0:T(8,128)(2,1)S(1)}, u32[]{:S(2)}, u32[]{:S(2)}) collective-permute-start(bf16[2,64,32,128]{3,2,1,0:T(8,128)(2,1)S(1)} %collective-permute-done.3.refs_5_), channel_id=1, source_target_pairs={{0,1},{1,0},{2,3},{3,2},{4,5},{5,4},{6,7},{7,6},{8,9},{9,8},{10,11... | collective-permute-start | bytes 3145736 | tf_op jit(solution)/shard_map/ppermute | solution.py:358
  64.8 39.9 %collective-permute-start.16 = (bf16[2,16,144,128]{3,2,1,0:T(8,128)(2,1)S(1)}, bf16[2,16,144,128]{3,2,1,0:T(8,128)(2,1)S(1)}, u32[]{:S(2)}, u32[]{:S(2)}) collective-permute-start(bf16[2,16,144,128]{3,2,1,0:T(8,128)(2,1)S(1)} %get-tuple-element.56), channel_id=1, source_target_pairs={{3,1},{5,3},{7,5},{9,7},{11,9},{13,11},{15,13},{17,15},{19,17},{21... | collective-permute-start | bytes 3538952 | tf_op jit(solution)/shard_map/ppermute | solution.py:353
  72.6 4.6 %collective-permute-start.9 = (bf16[2,64,16,128]{3,2,1,0:T(8,128)(2,1)S(1)}, bf16[2,64,16,128]{3,2,1,0:T(8,128)(2,1)S(1)}, u32[]{:S(2)}, u32[]{:S(2)}) collective-permute-start(bf16[2,64,16,128]{3,2,1,0:T(8,128)(2,1)S(1)} %prepare.9.refs_4_), channel_id=1, source_target_pairs={{2,0},{1,1},{4,2},{3,3},{6,4},{5,5},{8,6},{7,7},{10,8},{9,9},{12,1... | collective-permute-start | bytes 1572872 | tf_op jit(solution)/shard_map/ppermute | solution.py:346
  73.3 44.1 %collective-permute-start.15 = (bf16[2,16,144,128]{3,2,1,0:T(8,128)(2,1)S(1)}, bf16[2,16,144,128]{3,2,1,0:T(8,128)(2,1)S(1)}, u32[]{:S(2)}, u32[]{:S(2)}) collective-permute-start(bf16[2,16,144,128]{3,2,1,0:T(8,128)(2,1)S(1)} %get-tuple-element.55), channel_id=1, source_target_pairs={{3,1},{5,3},{7,5},{9,7},{11,9},{13,11},{15,13},{17,15},{19,17},{21... | collective-permute-start | bytes 3538952 | tf_op jit(solution)/shard_map/ppermute | solution.py:353
  75.2 54.8 %collective-permute-start.11 = (bf16[2,16,144,128]{3,2,1,0:T(8,128)(2,1)S(1)}, bf16[2,16,144,128]{3,2,1,0:T(8,128)(2,1)S(1)}, u32[]{:S(2)}, u32[]{:S(2)}) collective-permute-start(bf16[2,16,144,128]{3,2,1,0:T(8,128)(2,1)S(1)} %get-tuple-element.52), channel_id=1, source_target_pairs={{3,1},{5,3},{7,5},{9,7},{11,9},{13,11},{15,13},{17,15},{19,17},{21... | collective-permute-start | bytes 3538952 | tf_op jit(solution)/shard_map/ppermute | solution.py:353
  77.1 42.2 %collective-permute-start.13 = (bf16[2,64,32,128]{3,2,1,0:T(8,128)(2,1)S(1)}, bf16[2,64,32,128]{3,2,1,0:T(8,128)(2,1)S(1)}, u32[]{:S(2)}, u32[]{:S(2)}) collective-permute-start(bf16[2,64,32,128]{3,2,1,0:T(8,128)(2,1)S(1)} %collective-permute-done.7.refs_8_), channel_id=1, source_target_pairs={{0,1},{1,0},{2,3},{3,2},{4,5},{5,4},{6,7},{7,6},{8,9},{9,8},{10,11... | collective-permute-start | bytes 3145736 | tf_op jit(solution)/shard_map/ppermute | solution.py:358
  104.0 15.3 %collective-permute-start.12 = (bf16[2,64,32,128]{3,2,1,0:T(8,128)(2,1)S(1)}, bf16[2,64,32,128]{3,2,1,0:T(8,128)(2,1)S(1)}, u32[]{:S(2)}, u32[]{:S(2)}) collective-permute-start(bf16[2,64,32,128]{3,2,1,0:T(8,128)(2,1)S(1)} %collective-permute-done.5.refs_7_), channel_id=1, source_target_pairs={{0,1},{1,0},{2,3},{3,2},{4,5},{5,4},{6,7},{7,6},{8,9},{9,8},{10,11... | collective-permute-start | bytes 3145736 | tf_op jit(solution)/shard_map/ppermute | solution.py:358
  104.8 14.6 %collective-permute-start.14 = (bf16[2,64,16,128]{3,2,1,0:T(8,128)(2,1)S(1)}, bf16[2,64,16,128]{3,2,1,0:T(8,128)(2,1)S(1)}, u32[]{:S(2)}, u32[]{:S(2)}) collective-permute-start(bf16[2,64,16,128]{3,2,1,0:T(8,128)(2,1)S(1)} %collective-permute-done.9.refs_9_), channel_id=1, source_target_pairs={{0,1},{1,0},{2,3},{3,2},{4,5},{5,4},{6,7},{7,6},{8,9},{9,8},{10,11... | collective-permute-start | bytes 1572872 | tf_op jit(solution)/shard_map/ppermute | solution.py:358

commit v4 on v3

--- a/solution.py
+++ b/solution.py
@@ -28,10 +28,10 @@
 HALO_STEPS = 4
 
 
-def prepare_kernel(odd_ref, x_ref, lo_even, lo_odd, hi_even, hi_odd, sel_ref, inv_ref, ram_ref, raminv_ref,
+def prepare_kernel(x_ref, lo_even, lo_odd, hi_even, hi_odd, sel_ref, inv_ref, ram_ref, raminv_ref,
                    table_ref, band_ref, bandinv_ref, out_ref, ext, wide):
     channels, step, samples = x_ref.shape
-    odd = odd_ref[0] != 0
+    odd = lax.axis_index("blk") % 2 != 0
     ext_rows = ext.reshape(ext.shape[0] * PITCH, samples)
     wide_rows = wide.reshape(wide.shape[0] * PITCH, channels)
 
@@ -91,11 +91,11 @@
     out_ref[...] = wide[:, :step, :].reshape(2, bins, step, channels).astype(out_ref.dtype)
 
 
-def borders_kernel(early, odd_ref, x_ref, first_ref, rest_ref, inner_ref, sems):
+def borders_kernel(early, x_ref, first_ref, rest_ref, inner_ref, sems):
     channels, windows, _ = x_ref.shape
     late = windows - early
     top = channels - HW
-    outer = odd_ref[0] * top
+    outer = lax.axis_index("blk") % 2 * top
     inner = top - outer
     copies = [
         pltpu.make_async_copy(x_ref.at[pl.ds(outer, HW), pl.ds(0, early), :], first_ref, sems.at[0]),
@@ -108,21 +108,21 @@
         copy.wait()
 
 
-def borders(traces, odd, early):
+def borders(traces, early):
     _, windows, samples = traces.shape
     shape = lambda n: jax.ShapeDtypeStruct((HW, n, samples), traces.dtype)
     return pl.pallas_call(
         functools.partial(borders_kernel, early),
-        in_specs=[pl.BlockSpec(memory_space=pltpu.SMEM), pl.BlockSpec(memory_space=pl.ANY)],
+        in_specs=[pl.BlockSpec(memory_space=pl.ANY)],
         out_specs=[pl.BlockSpec(memory_space=pltpu.VMEM)] * 3,
         out_shape=[shape(early), shape(windows - early), shape(windows)],
         scratch_shapes=[pltpu.SemaphoreType.DMA((3,))],
         cost_estimate=pl.CostEstimate(flops=1, bytes_accessed=1, transcendentals=0),
         name="borders",
-    )(odd, traces)
-
-
-def prepare(x, odd, halos, first, windows, consts):
+    )(traces)
+
+
+def prepare(x, halos, first, windows, consts):
     channels, _, samples = x.shape
     bins = samples // 2
     whole = lambda a: pl.BlockSpec(a.shape, lambda i: (0,) * a.ndim)
@@ -130,7 +130,7 @@
     return pl.pallas_call(
         prepare_kernel,
         grid=(windows // STEP,),
-        in_specs=[pl.BlockSpec(memory_space=pltpu.SMEM), part(channels, first)]
+        in_specs=[part(channels, first)]
         + [part(HW, start) for _, start in halos]
         + [whole(a) for a in consts],
         out_specs=pl.BlockSpec((2, bins, STEP, channels), lambda i: (0, 0, i, 0)),
@@ -142,106 +142,65 @@
         compiler_params=pltpu.CompilerParams(vmem_limit_bytes=VMEM),
         cost_estimate=pl.CostEstimate(flops=1, bytes_accessed=1, transcendentals=0),
         name="prepare",
-    )(odd, x, *[a for a, _ in halos], *consts)
-
-
-def correlate_kernel(n_own, n_partner, scale, pick_ref, *refs):
-    own = refs[:n_own]
-    partner = refs[n_own : n_own + n_partner]
-    far = refs[n_own + n_partner] if pick_ref is not None else None
+    )(x, *[a for a, _ in halos], *consts)
+
+
+def correlate_kernel(n_own, scale, *refs):
+    own, partner = refs[:n_own], refs[n_own : 2 * n_own]
     out_ref, wide = refs[-2:]
     step = own[0].shape[1]
     channels = own[0].shape[3]
+    multiply(own, partner, 0, 0, step, scale, wide)
+    for part in range(2):
+        out_ref[:, 0, part] = wide[part, :, :step, :].astype(out_ref.dtype)
+
+
+def multiply(own, partner, first, partner_first, bins, scale, wide):
+    channels = own[0].shape[3]
+    rows = wide.reshape(2, channels * PITCH, channels)
+    dims = (((0,), (0,)), ((), ()))
 
     def whole(group, part, k):
         pieces = [ref[part, k] for ref in group]
         return pieces[0] if len(pieces) == 1 else jnp.concatenate(pieces, axis=0)
 
-    def run(partner):
-        for k in range(step):
-            a_re, a_im = whole(own, 0, k), whole(own, 1, k)
-            b = jnp.concatenate([whole(partner, 0, k), whole(partner, 1, k)], axis=1)
-            dims = (((0,), (0,)), ((), ()))
-            by_re = lax.dot_general(a_re, b, dims, preferred_element_type=jnp.float32)
-            by_im = lax.dot_general(a_im, b, dims, preferred_element_type=jnp.float32)
-            re = by_re[:, :channels] + by_im[:, channels:]
-            im = by_im[:, :channels] - by_re[:, channels:]
-            wide[0, pl.ds(k, channels, stride=PITCH), :] = re * scale
-            wide[1, pl.ds(k, channels, stride=PITCH), :] = im * scale
-
-    if far is None:
-        run(partner)
-    else:
-        pl.when(pick_ref[0] == 0)(lambda: run(partner))
-        pl.when(pick_ref[0] != 0)(lambda: run([far]))
-    for part in range(2):
-        out_ref[:, 0, part] = wide[part].reshape(channels, PITCH, channels)[:, :step].astype(out_ref.dtype)
-
-
-def correlate(own, partner, round_index, first_bin, bins, pick=None, far=None, target=None, after=None):
+    for k in range(bins):
+        a_re, a_im = whole(own, 0, first + k), whole(own, 1, first + k)
+        b = jnp.concatenate([whole(partner, 0, partner_first + k), whole(partner, 1, partner_first + k)], axis=1)
+        by_re = lax.dot_general(a_re, b, dims, preferred_element_type=jnp.float32)
+        by_im = lax.dot_general(a_im, b, dims, preferred_element_type=jnp.float32)
+        re = by_re[:, :channels] + by_im[:, channels:]
+        im = by_im[:, :channels] - by_re[:, channels:]
+        rows[0, pl.ds(k, channels, stride=PITCH), :] = re * scale
+        rows[1, pl.ds(k, channels, stride=PITCH), :] = im * scale
+
+
+def correlate(own, partner, round_index, target):
     _, total_bins, _, channels = own[0].shape
     windows = sum(a.shape[2] for a in own)
-    steps = bins // BINS_STEP
-    base = first_bin // BINS_STEP
-    operands = list(own) + list(partner)
-    specs = [pl.BlockSpec((2, BINS_STEP, a.shape[2], channels), lambda i: (0, base + i, 0, 0)) for a in operands]
-    if far is not None:
-        specs.append(pl.BlockSpec((2, BINS_STEP, windows, channels), lambda i: (0, i, 0, 0)))
-        operands.append(far)
-    kernel = functools.partial(correlate_kernel, len(own), len(partner), 1.0 / math.sqrt(windows))
-    if pick is None:
-        kernel = functools.partial(kernel, None)
-    else:
-        specs.insert(0, pl.BlockSpec(memory_space=pltpu.SMEM))
-        operands.insert(0, pick)
-    aliases = {}
-    if target is not None:
-        specs.append(pl.BlockSpec(memory_space=pl.ANY))
-        aliases = {len(operands): 0}
-        operands.append(target)
-    if after is not None:
-        specs.append(pl.BlockSpec(memory_space=pl.ANY))
-        operands.append(after)
+    operands = [*own, *partner, target]
+    specs = [pl.BlockSpec((2, BINS_STEP, a.shape[2], channels), lambda i: (0, i, 0, 0)) for a in operands[:-1]]
     return pl.pallas_call(
-        kernel,
-        grid=(steps,),
-        in_specs=specs,
-        out_specs=pl.BlockSpec((channels, 1, 2, BINS_STEP, channels), lambda i: (0, round_index, 0, base + i, 0)),
-        out_shape=jax.ShapeDtypeStruct((channels, ROUNDS, 2, total_bins, channels), jnp.bfloat16),
-        scratch_shapes=[pltpu.VMEM((2, channels * PITCH, channels), jnp.float32)],
-        input_output_aliases=aliases,
+        functools.partial(correlate_kernel, len(own), 1.0 / math.sqrt(windows)),
+        grid=(total_bins // BINS_STEP,),
+        in_specs=specs + [pl.BlockSpec(memory_space=pl.ANY)],
+        out_specs=pl.BlockSpec((channels, 1, 2, BINS_STEP, channels), lambda i: (0, round_index, 0, i, 0)),
+        out_shape=jax.ShapeDtypeStruct(target.shape, target.dtype),
+        scratch_shapes=[pltpu.VMEM((2, channels, PITCH, channels), jnp.float32)],
+        input_output_aliases={len(operands) - 1: 0},
         compiler_params=pltpu.CompilerParams(vmem_limit_bytes=VMEM),
         cost_estimate=pl.CostEstimate(flops=1, bytes_accessed=1, transcendentals=0),
         name="correlate",
     )(*operands)
 
 
-def correlate_chunk_kernel(n_own, n_partner, scale, first_bin, round_index, pick_ref, *refs):
-    own = refs[:n_own]
-    partner = refs[n_own : n_own + n_partner]
-    far = refs[n_own + n_partner]
+def correlate_chunk_kernel(n_own, scale, first_bin, round_index, *refs):
+    own, partner, far = refs[:n_own], refs[n_own : 2 * n_own], refs[2 * n_own]
     out_ref, wide, done, sems = refs[-4:]
-    _, bins, _, channels = far.shape
-    pitch_rows = wide.reshape(2, channels * PITCH, channels)
-
-    def whole(group, part, k):
-        pieces = [ref[part, k] for ref in group]
-        return pieces[0] if len(pieces) == 1 else jnp.concatenate(pieces, axis=0)
-
-    def run(partner, base):
-        for k in range(bins):
-            a_re, a_im = whole(own, 0, first_bin + k), whole(own, 1, first_bin + k)
-            b = jnp.concatenate([whole(partner, 0, base + k), whole(partner, 1, base + k)], axis=1)
-            dims = (((0,), (0,)), ((), ()))
-            by_re = lax.dot_general(a_re, b, dims, preferred_element_type=jnp.float32)
-            by_im = lax.dot_general(a_im, b, dims, preferred_element_type=jnp.float32)
-            re = by_re[:, :channels] + by_im[:, channels:]
-            im = by_im[:, :channels] - by_re[:, channels:]
-            pitch_rows[0, pl.ds(k, channels, stride=PITCH), :] = re * scale
-            pitch_rows[1, pl.ds(k, channels, stride=PITCH), :] = im * scale
-
-    pl.when(pick_ref[0] == 0)(lambda: run(partner, first_bin))
-    pl.when(pick_ref[0] != 0)(lambda: run([far], 0))
+    bins = far.shape[1]
+    odd = lax.axis_index("blk") % 2 != 0
+    pl.when(jnp.logical_not(odd))(lambda: multiply(own, partner, first_bin, first_bin, bins, scale, wide))
+    pl.when(odd)(lambda: multiply(own, [far], first_bin, 0, bins, scale, wide))
     copies = []
     for part in range(2):
         done[part] = wide[part, :, :bins, :].astype(done.dtype)
@@ -255,12 +214,11 @@
         copy.wait()
 
 
-def correlate_chunk(own, partner, round_index, first_bin, pick, far, target, after):
+def correlate_chunk(own, partner, round_index, first_bin, far, target, after):
     _, bins, windows, channels = far.shape
     total_bins = own[0].shape[1]
-    operands = [pick, *own, *partner, far]
-    specs = [pl.BlockSpec(memory_space=pltpu.SMEM)]
-    specs += [pl.BlockSpec(memory_space=pltpu.VMEM)] * (len(operands) - 1)
+    operands = [*own, *partner, far]
+    specs = [pl.BlockSpec(memory_space=pltpu.VMEM)] * len(operands)
     aliases = {}
     if target is not None:
         aliases = {len(operands): 0}
@@ -270,7 +228,7 @@
     specs.append(pl.BlockSpec(memory_space=pl.ANY))
     return pl.pallas_call(
         functools.partial(
-            correlate_chunk_kernel, len(own), len(partner), 1.0 / math.sqrt(windows), first_bin, round_index
+            correlate_chunk_kernel, len(own), 1.0 / math.sqrt(windows), first_bin, round_index
         ),
         in_specs=specs,
         out_specs=pl.BlockSpec(memory_space=pl.ANY),
@@ -319,15 +277,15 @@
     bins = samples // 2
     count = lax.axis_size("blk")
     block = lax.axis_index("blk")
-    pick = (block % 2).astype(jnp.int32)[None]
     swap = [(i, i ^ 1) for i in range(count)]
     cross = [(i, i + 1 if i % 2 else i - 1) for i in range(1, count - 1)]
     first_pairs = [((i + 2) % count, i) if i % 2 == 0 else (i, i) for i in range(count)]
     second_pairs = [((i + 2) % count, i) for i in range(1, count, 2)]
     early = HALO_STEPS * STEP
 
-    outer_first, outer_rest, inner = borders(traces, pick, early)
-    across_first = lax.ppermute(outer_first, "blk", cross)
+    outer_first, outer_rest, inner = borders(traces, early)
+    above_first = lax.ppermute(outer_first, "blk", [(i + 1, i) for i in range(1, count - 1, 2)])
+    below_first = lax.ppermute(outer_first, "blk", [(i, i + 1) for i in range(1, count - 1, 2)])
     beside = lax.ppermute(inner, "blk", swap)
     across_rest = lax.ppermute(outer_rest, "blk", cross)
     consts = edges(block, channels * count, channels, samples) + tables(channels, samples, bands)
@@ -336,13 +294,15 @@
     at = 0
     for n, size in enumerate(CHUNKS):
         if n == 1:
-            across_first, across_rest, own[0] = lax.optimization_barrier((across_first, across_rest, own[0]))
+            below_first, across_rest, own[0] = lax.optimization_barrier((below_first, across_rest, own[0]))
         elif n > 1:
             across_rest, own[-1], held[n - 2] = lax.optimization_barrier((across_rest, own[-1], held[n - 2]))
-        across, skip = (across_first, 0) if at < early else (across_rest, early)
+        if at < early:
+            halos = [(below_first, at), (beside, at), (beside, at), (above_first, at)]
+        else:
+            halos = [(across_rest, at - early), (beside, at), (beside, at), (across_rest, at - early)]
         x, first = (traces[:, : size * STEP], 0) if n == 0 else (traces, at)
-        halos = [(across, at - skip), (beside, at), (beside, at), (across, at - skip)]
-        own.append(prepare(x, pick, halos, first, size * STEP, consts))
+        own.append(prepare(x, halos, first, size * STEP, consts))
         held.append(lax.ppermute(own[-1], "blk", first_pairs))
         at += size * STEP
     token = lax.ppermute(held[TOKEN][0, 0, :STEP], "blk", swap)
@@ -359,8 +319,8 @@
     out = None
     for n, first in enumerate(range(0, bins, BINS_STEP)):
         if n == FIRST_ROUND_AFTER:
-            out = correlate(own, other, 0, 0, bins, target=out)
-        out = correlate_chunk(own, held, 1, first, pick, far[n], out, token)
+            out = correlate(own, other, 0, out)
+        out = correlate_chunk(own, held, 1, first, far[n], out, token)
     return out
 
 

time: 133 us -> 130 us (0.977)
    ppermute x5, starting transfers between devices: 49 us -> 44.3 us  [per_device(): other.append(lax.ppermute(held[n], 'blk', swap))]
    ppermute x1, starting transfers between devices: 1.92 us -> 4.28 us  [per_device(): across_rest = lax.ppermute(outer_rest, 'blk', cross)]
    ppermute x1 -> x2, waiting for transfers between devices: 2.79 us -> 0.54 us  [the longest x1 0.54 us: per_device(): lax.ppermute(outer_first, 'blk', [(i + 1, i) for i in range(1, count - 1,...]
    ppermute x1 -> x2, starting transfers between devices: 4.46 us -> 5.81 us  [the longest x1 4.52 us: per_device(): lax.ppermute(outer_first, 'blk', [(i, i + 1) for i in range(1, count - 1,...]
  transfers between devices with their start and end apart: 18 -> 19, of which waited for: 5 -> 5; matrix products, arithmetic and copies ran while one was open for 2% -> 2% of each run, Pallas kernels for 18% -> 18%
where the time goes in v4:
time: 130 us
  starting transfers between devices  77.3 us (59%)
  Pallas kernels  28 us (22%)
  waiting for transfers between devices  19.3 us (15%)
  local copies, waits for them, and re-layouts  4.49 us (3%)
    ppermute x5, starting transfers between devices, per_device(): other.append(lax.ppermute(held[n], 'blk', swap))  44.3 us
    ppermute x4, starting transfers between devices, per_device(): far.append(lax.ppermute(mine, 'blk', second_pairs))  19.2 us
    ppermute x4, waiting for transfers between devices, per_device(): far.append(lax.ppermute(mine, 'blk', second_pairs))  14.2 us
    pallas_call x5, Pallas kernels, prepare(): pl.pallas_call(prepare_kernel, grid=(windows // STEP,), in_specs=[part(ch...  12.2 us
    pallas_call x4, Pallas kernels, correlate_chunk(): pl.pallas_call(functools.partial(correlate_chunk_kernel, len(own), 1.0 /...  7.93 us
    pallas_call x1, Pallas kernels, correlate(): pl.pallas_call(functools.partial(correlate_kernel, len(own), 1.0 / math.s...  5.62 us
    ppermute x1, waiting for transfers between devices, per_device(): across_rest = lax.ppermute(outer_rest, 'blk', cross)  4.59 us
    ppermute x1, starting transfers between devices, per_device(): lax.ppermute(outer_first, 'blk', [(i, i + 1) for i in range(1, count - 1,...  4.52 us
  transfers between devices with their start and end apart: 19, of which 5 were waited for; matrix products, arithmetic and copies ran while one was open for 2% of the time, Pallas kernels for 18%

profile of v4, /device:TPU:1, one launch (start us, length us, event | category | flops | bytes accessed | tf_op | source)
XLA Modules:
  0.0 129.9 jit_solution(16599044131053173826)
XLA Ops:
  0.0 2.3 %borders.1 = (bf16[16,64,128]{2,1,0:T(8,128)(2,1)}, bf16[16,80,128]{2,1,0:T(8,128)(2,1)}, bf16[16,144,128]{2,1,0:T(8,128)(2,1)}) custom-call(bf16[128,144,128]{2,1,0:T(8,128)(2,1)} %x_ref.9), custom_call_target="tpu_custom_call" | custom-call | flops 1 | bytes 1 | tf_op jit(solution)/shard_map/borders/pallas_call | solution.py:114
  2.3 4.5 %collective-permute-start = (bf16[16,64,128]{2,1,0:T(8,128)(2,1)}, bf16[16,64,128]{2,1,0:T(8,128)(2,1)S(1)}, u32[]{:S(2)}, u32[]{:S(2)}) collective-permute-start(bf16[16,64,128]{2,1,0:T(8,128)(2,1)} %get-tuple-element.32), channel_id=1, source_target_pairs={{1,2},{3,4},{5,6},{7,8},{9,10},{11,12},{13,14},{15,16},{17,18},{19... | collective-permute-start | bytes 786440 | tf_op jit(solution)/shard_map/ppermute | solution.py:288
  6.8 1.3 collective-permute-start.3
  8.1 0.1 collective-permute-start.2
  8.2 4.3 %collective-permute-start.1 = (bf16[16,80,128]{2,1,0:T(8,128)(2,1)}, bf16[16,80,128]{2,1,0:T(8,128)(2,1)S(1)}, u32[]{:S(2)}, u32[]{:S(2)}) collective-permute-start(bf16[16,80,128]{2,1,0:T(8,128)(2,1)} %get-tuple-element.33), channel_id=1, source_target_pairs={{1,2},{2,1},{3,4},{4,3},{5,6},{6,5},{7,8},{8,7},{9,10},{10,9},{11,... | collective-permute-start | bytes 983048 | tf_op jit(solution)/shard_map/ppermute | solution.py:290
  12.5 0.1 compare_convert_fusion.1
  12.6 0.1 fusion
  12.7 0.0 copy-start.1
  12.7 0.0 copy-start.2
  12.8 0.0 copy-start.3
  12.8 1.3 %slice.66.x_ref = bf16[128,32,128]{2,1,0:T(8,128)(2,1)S(1)} slice(bf16[128,144,128]{2,1,0:T(8,128)(2,1)} %x_ref.9), slice={[0:128], [0:32], [0:128]} | slice | bytes 2097152 | tf_op jit(solution)/shard_map/slice | solution.py:304
  14.1 0.1 copy.13.band_ref
  14.2 0.5 collective-permute-done.3.hi_odd
  14.8 0.1 broadcast_in_dim.4.inv_ref
  14.9 0.1 broadcast_in_dim.5.bandinv_ref
  14.9 0.0 copy-done.3
  15.0 2.7 %prepare.5.refs_0_ = bf16[2,64,32,128]{3,2,1,0:T(8,128)(2,1)S(1)} custom-call(bf16[128,32,128]{2,1,0:T(8,128)(2,1)S(1)} %slice.66.x_ref, bf16[16,64,128]{2,1,0:T(8,128)(2,1)S(1)} %collective-permute-done.lo_even, bf16[16,144,128]{2,1,0:T(8,128)(2,1)S(1)} %collective-permute-done.2.lo_odd.hi_even, ...), custom_call_target="tpu_custom_call" | custom-call | flops 1 | bytes 1 | tf_op jit(solution)/shard_map/prepare/pallas_call | solution.py:130
  17.7 0.7 collective-permute-start.4
  18.4 4.6 %collective-permute-done.1.lo_even.hi_odd = bf16[16,80,128]{2,1,0:T(8,128)(2,1)S(1)} collective-permute-done((bf16[16,80,128]{2,1,0:T(8,128)(2,1)}, bf16[16,80,128]{2,1,0:T(8,128)(2,1)S(1)}, u32[]{:S(2)}, u32[]{:S(2)}) %collective-permute-start.1) | collective-permute-done | bytes 327712 | tf_op jit(solution)/shard_map/ppermute | solution.py:290
  23.0 2.3 %copy-done = bf16[128,144,128]{2,1,0:T(8,128)(2,1)S(1)} copy-done((bf16[128,144,128]{2,1,0:T(8,128)(2,1)S(1)}, bf16[128,144,128]{2,1,0:T(8,128)(2,1)}, u32[]{:S(2)}) %copy-start) | copy-done | bytes 4718616
  25.4 2.7 %prepare.6.refs_1_ = bf16[2,64,32,128]{3,2,1,0:T(8,128)(2,1)S(1)} custom-call(bf16[128,144,128]{2,1,0:T(8,128)(2,1)S(1)} %copy-done, bf16[16,64,128]{2,1,0:T(8,128)(2,1)S(1)} %collective-permute-done.lo_even, bf16[16,144,128]{2,1,0:T(8,128)(2,1)S(1)} %collective-permute-done.2.lo_odd.hi_even, ...), custom_call_target="tpu_custom_call" | custom-call | flops 1 | bytes 1 | tf_op jit(solution)/shard_map/prepare/pallas_call | solution.py:130
  28.1 0.7 collective-permute-start.5
  28.8 2.7 %prepare.7.refs_2_ = bf16[2,64,32,128]{3,2,1,0:T(8,128)(2,1)S(1)} custom-call(bf16[128,144,128]{2,1,0:T(8,128)(2,1)S(1)} %copy-done, bf16[16,80,128]{2,1,0:T(8,128)(2,1)S(1)} %collective-permute-done.1.lo_even.hi_odd, bf16[16,144,128]{2,1,0:T(8,128)(2,1)S(1)} %collective-permute-done.2.lo_odd.hi_even, ...), custom_call_target="tpu_custom_call" | custom-call | flops 1 | bytes 1 | tf_op jit(solution)/shard_map/prepare/pallas_call | solution.py:130
  31.6 0.7 collective-permute-start.6
  32.3 0.1 slice_dynamic-update-slice_fusion.3
  32.4 16.1 %collective-permute-start.9 = (bf16[2,64,32,128]{3,2,1,0:T(8,128)(2,1)S(1)}, bf16[2,64,32,128]{3,2,1,0:T(8,128)(2,1)S(1)}, u32[]{:S(2)}, u32[]{:S(2)}) collective-permute-start(bf16[2,64,32,128]{3,2,1,0:T(8,128)(2,1)S(1)} %collective-permute-done.5.refs_6_), channel_id=1, source_target_pairs={{0,1},{1,0},{2,3},{3,2},{4,5},{5,4},{6,7},{7,6},{8,9},{9,8},{10,11... | collective-permute-start | bytes 3145736 | tf_op jit(solution)/shard_map/ppermute | solution.py:318
  48.5 2.7 %prepare.8.refs_3_ = bf16[2,64,32,128]{3,2,1,0:T(8,128)(2,1)S(1)} custom-call(bf16[128,144,128]{2,1,0:T(8,128)(2,1)S(1)} %copy-done, bf16[16,80,128]{2,1,0:T(8,128)(2,1)S(1)} %collective-permute-done.1.lo_even.hi_odd, bf16[16,144,128]{2,1,0:T(8,128)(2,1)S(1)} %collective-permute-done.2.lo_odd.hi_even, ...), custom_call_target="tpu_custom_call" | custom-call | flops 1 | bytes 1 | tf_op jit(solution)/shard_map/prepare/pallas_call | solution.py:130
  51.3 0.7 collective-permute-start.8
  52.0 0.1 slice_dynamic-update-slice_fusion.2
  52.1 0.1 slice_dynamic-update-slice_fusion.1
  52.3 1.3 prepare.9.refs_4_
  53.6 0.1 slice_dynamic-update-slice_fusion
  53.7 0.1 slice_dynamic-update-slice_fusion.16
  53.8 7.7 %collective-permute-start.18 = (bf16[2,16,144,128]{3,2,1,0:T(8,128)(2,1)S(1)}, bf16[2,16,144,128]{3,2,1,0:T(8,128)(2,1)S(1)}, u32[]{:S(2)}, u32[]{:S(2)}) collective-permute-start(bf16[2,16,144,128]{3,2,1,0:T(8,128)(2,1)S(1)} %get-tuple-element.57), channel_id=1, source_target_pairs={{3,1},{5,3},{7,5},{9,7},{11,9},{13,11},{15,13},{17,15},{19,17},{21... | collective-permute-start | bytes 3538952 | tf_op jit(solution)/shard_map/ppermute | solution.py:313
  61.5 1.1 collective-permute-start.7
  62.6 7.7 %collective-permute-start.17 = (bf16[2,16,144,128]{3,2,1,0:T(8,128)(2,1)S(1)}, bf16[2,16,144,128]{3,2,1,0:T(8,128)(2,1)S(1)}, u32[]{:S(2)}, u32[]{:S(2)}) collective-permute-start(bf16[2,16,144,128]{3,2,1,0:T(8,128)(2,1)S(1)} %get-tuple-element.56), channel_id=1, source_target_pairs={{3,1},{5,3},{7,5},{9,7},{11,9},{13,11},{15,13},{17,15},{19,17},{21... | collective-permute-start | bytes 3538952 | tf_op jit(solution)/shard_map/ppermute | solution.py:313
  70.3 0.7 collective-permute-start.10
  71.0 1.9 %collective-permute-start.16 = (bf16[2,16,144,128]{3,2,1,0:T(8,128)(2,1)S(1)}, bf16[2,16,144,128]{3,2,1,0:T(8,128)(2,1)S(1)}, u32[]{:S(2)}, u32[]{:S(2)}) collective-permute-start(bf16[2,16,144,128]{3,2,1,0:T(8,128)(2,1)S(1)} %get-tuple-element.55), channel_id=1, source_target_pairs={{3,1},{5,3},{7,5},{9,7},{11,9},{13,11},{15,13},{17,15},{19,17},{21... | collective-permute-start | bytes 3538952 | tf_op jit(solution)/shard_map/ppermute | solution.py:313
  73.0 1.9 %collective-permute-start.12 = (bf16[2,16,144,128]{3,2,1,0:T(8,128)(2,1)S(1)}, bf16[2,16,144,128]{3,2,1,0:T(8,128)(2,1)S(1)}, u32[]{:S(2)}, u32[]{:S(2)}) collective-permute-start(bf16[2,16,144,128]{3,2,1,0:T(8,128)(2,1)S(1)} %get-tuple-element.52), channel_id=1, source_target_pairs={{3,1},{5,3},{7,5},{9,7},{11,9},{13,11},{15,13},{17,15},{19,17},{21... | collective-permute-start | bytes 3538952 | tf_op jit(solution)/shard_map/ppermute | solution.py:313
  74.9 27.1 %collective-permute-start.14 = (bf16[2,64,32,128]{3,2,1,0:T(8,128)(2,1)S(1)}, bf16[2,64,32,128]{3,2,1,0:T(8,128)(2,1)S(1)}, u32[]{:S(2)}, u32[]{:S(2)}) collective-permute-start(bf16[2,64,32,128]{3,2,1,0:T(8,128)(2,1)S(1)} %collective-permute-done.8.refs_8_), channel_id=1, source_target_pairs={{0,1},{1,0},{2,3},{3,2},{4,5},{5,4},{6,7},{7,6},{8,9},{9,8},{10,11... | collective-permute-start | bytes 3145736 | tf_op jit(solution)/shard_map/ppermute | solution.py:318
  102.0 0.6 collective-permute-done.17.refs_10_
  102.6 1.9 %correlate_chunk.4.refs_11_ = bf16[128,2,2,64,128]{4,3,2,1,0:T(8,128)(2,1)} custom-call(bf16[2,64,32,128]{3,2,1,0:T(8,128)(2,1)S(1)} %prepare.5.refs_0_, bf16[2,64,32,128]{3,2,1,0:T(8,128)(2,1)S(1)} %prepare.6.refs_1_, bf16[2,64,32,128]{3,2,1,0:T(8,128)(2,1)S(1)} %prepare.7.refs_2_, bf16[2,64,32,128]{3,2,1,0:T(8,128)(2,1)S(1)} %prepare.8.refs_3_, ...), custom_call_target="tpu_custom_call" | custom-call | flops 1 | bytes 1 | tf_op jit(solution)/shard_map/correlate_chunk/pallas_call | solution.py:229
  104.5 2.1 %correlate_chunk.5.refs_11_ = bf16[128,2,2,64,128]{4,3,2,1,0:T(8,128)(2,1)} custom-call(bf16[2,64,32,128]{3,2,1,0:T(8,128)(2,1)S(1)} %prepare.5.refs_0_, bf16[2,64,32,128]{3,2,1,0:T(8,128)(2,1)S(1)} %prepare.6.refs_1_, bf16[2,64,32,128]{3,2,1,0:T(8,128)(2,1)S(1)} %prepare.7.refs_2_, ...), custom_call_target="tpu_custom_call", output_to_operand_aliasing={{}: (11, {})} | custom-call | flops 1 | bytes 1 | tf_op jit(solution)/shard_map/correlate_chunk/pallas_call | solution.py:229
  106.6 8.6 %collective-permute-done.16.refs_10_ = bf16[2,16,144,128]{3,2,1,0:T(8,128)(2,1)S(1)} collective-permute-done((bf16[2,16,144,128]{3,2,1,0:T(8,128)(2,1)S(1)}, bf16[2,16,144,128]{3,2,1,0:T(8,128)(2,1)S(1)}, u32[]{:S(2)}, u32[]{:S(2)}) %collective-permute-start.16) | collective-permute-done | bytes 1179680 | tf_op jit(solution)/shard_map/ppermute | solution.py:313
  115.2 1.9 %correlate_chunk.6.refs_10_ = bf16[128,2,2,64,128]{4,3,2,1,0:T(8,128)(2,1)} custom-call(bf16[2,64,32,128]{3,2,1,0:T(8,128)(2,1)S(1)} %prepare.5.refs_0_, bf16[2,64,32,128]{3,2,1,0:T(8,128)(2,1)S(1)} %prepare.6.refs_1_, bf16[2,64,32,128]{3,2,1,0:T(8,128)(2,1)S(1)} %prepare.7.refs_2_, ...), custom_call_target="tpu_custom_call", output_to_operand_aliasing={{}: (11, {})} | custom-call | flops 1 | bytes 1 | tf_op jit(solution)/shard_map/correlate_chunk/pallas_call | solution.py:229
  117.2 5.6 %correlate.1.refs_11_ = bf16[128,2,2,64,128]{4,3,2,1,0:T(8,128)(2,1)} custom-call(bf16[2,64,32,128]{3,2,1,0:T(8,128)(2,1)S(1)} %prepare.5.refs_0_, bf16[2,64,32,128]{3,2,1,0:T(8,128)(2,1)S(1)} %prepare.6.refs_1_, bf16[2,64,32,128]{3,2,1,0:T(8,128)(2,1)S(1)} %prepare.7.refs_2_, ...), custom_call_target="tpu_custom_call", output_to_operand_aliasing={{}: (10, {})} | custom-call | flops 1 | bytes 1 | tf_op jit(solution)/shard_map/correlate/pallas_call | solution.py:183
  122.8 5.0 %collective-permute-done.12.refs_10_ = bf16[2,16,144,128]{3,2,1,0:T(8,128)(2,1)S(1)} collective-permute-done((bf16[2,16,144,128]{3,2,1,0:T(8,128)(2,1)S(1)}, bf16[2,16,144,128]{3,2,1,0:T(8,128)(2,1)S(1)}, u32[]{:S(2)}, u32[]{:S(2)}) %collective-permute-start.12) | collective-permute-done | bytes 1179680 | tf_op jit(solution)/shard_map/ppermute | solution.py:313
  127.8 1.9 %correlate_chunk.7 = bf16[128,2,2,64,128]{4,3,2,1,0:T(8,128)(2,1)} custom-call(bf16[2,64,32,128]{3,2,1,0:T(8,128)(2,1)S(1)} %prepare.5.refs_0_, bf16[2,64,32,128]{3,2,1,0:T(8,128)(2,1)S(1)} %prepare.6.refs_1_, bf16[2,64,32,128]{3,2,1,0:T(8,128)(2,1)S(1)} %prepare.7.refs_2_, ...), custom_call_target="tpu_custom_call", output_to_operand_aliasing={{}: (11, {})} | custom-call | flops 1 | bytes 1 | tf_op jit(solution)/shard_map/correlate_chunk/pallas_call | solution.py:229
  (30 shorter events, 0.1 us)
Async XLA Ops:
  0.0 12.7 %copy-start.4 = (pred[128,160]{1,0:T(32,128)(4,1)S(1)}, pred[128,160]{1,0:T(32,128)(4,1)}, u32[]{:S(2)}) copy-start(pred[128,160]{1,0:T(32,128)(4,1)} %constant.36.clone) | copy-start | bytes 61444
  0.0 12.5 %copy-start.5 = (s32[64]{0:T(128)S(1)}, s32[64]{0:T(128)}, u32[]{:S(2)}) copy-start(s32[64]{0:T(128)} %param.9) | copy-start | bytes 772
  2.3 11.9 %collective-permute-start = (bf16[16,64,128]{2,1,0:T(8,128)(2,1)}, bf16[16,64,128]{2,1,0:T(8,128)(2,1)S(1)}, u32[]{:S(2)}, u32[]{:S(2)}) collective-permute-start(bf16[16,64,128]{2,1,0:T(8,128)(2,1)} %get-tuple-element.32), channel_id=1, source_target_pairs={{1,2},{3,4},{5,6},{7,8},{9,10},{11,12},{13,14},{15,16},{17,18},{19... | collective-permute-start | bytes 786440 | tf_op jit(solution)/shard_map/ppermute | solution.py:288
  6.8 8.0 %collective-permute-start.3 = (bf16[16,64,128]{2,1,0:T(8,128)(2,1)}, bf16[16,64,128]{2,1,0:T(8,128)(2,1)S(1)}, u32[]{:S(2)}, u32[]{:S(2)}) collective-permute-start(bf16[16,64,128]{2,1,0:T(8,128)(2,1)} %get-tuple-element.32), channel_id=1, source_target_pairs={{2,1},{4,3},{6,5},{8,7},{10,9},{12,11},{14,13},{16,15},{18,17},{20... | collective-permute-start | bytes 786440 | tf_op jit(solution)/shard_map/ppermute | solution.py:287
  8.1 6.7 %collective-permute-start.2 = (bf16[16,144,128]{2,1,0:T(8,128)(2,1)}, bf16[16,144,128]{2,1,0:T(8,128)(2,1)S(1)}, u32[]{:S(2)}, u32[]{:S(2)}) collective-permute-start(bf16[16,144,128]{2,1,0:T(8,128)(2,1)} %get-tuple-element.34), channel_id=1, source_target_pairs={{0,1},{1,0},{2,3},{3,2},{4,5},{5,4},{6,7},{7,6},{8,9},{9,8},{10,11... | collective-permute-start | bytes 1769480 | tf_op jit(solution)/shard_map/ppermute | solution.py:289
  8.2 14.8 %collective-permute-start.1 = (bf16[16,80,128]{2,1,0:T(8,128)(2,1)}, bf16[16,80,128]{2,1,0:T(8,128)(2,1)S(1)}, u32[]{:S(2)}, u32[]{:S(2)}) collective-permute-start(bf16[16,80,128]{2,1,0:T(8,128)(2,1)} %get-tuple-element.33), channel_id=1, source_target_pairs={{1,2},{2,1},{3,4},{4,3},{5,6},{6,5},{7,8},{8,7},{9,10},{10,9},{11,... | collective-permute-start | bytes 983048 | tf_op jit(solution)/shard_map/ppermute | solution.py:290
  12.7 2.2 %copy-start.1 = (bf16[128,128]{1,0:T(8,128)(2,1)S(1)}, bf16[128,128]{1,0:T(8,128)(2,1)}, u32[]{:S(2)}) copy-start(bf16[128,128]{1,0:T(8,128)(2,1)} %constant.37.clone.ram_ref) | copy-start | bytes 98308
  12.7 2.2 %copy-start.2 = (bf16[128,128]{1,0:T(8,128)(2,1)S(1)}, bf16[128,128]{1,0:T(8,128)(2,1)}, u32[]{:S(2)}) copy-start(bf16[128,128]{1,0:T(8,128)(2,1)} %constant.39.clone.table_ref) | copy-start | bytes 98308
  12.8 2.2 %copy-start.3 = (f32[1,128]{1,0:T(1,128)S(1)}, f32[1,128]{1,0:T(1,128)}, u32[]{:S(2)}) copy-start(f32[1,128]{1,0:T(1,128)} %constant.38.clone.raminv_ref) | copy-start | bytes 1540
  17.7 11.1 %collective-permute-start.4 = (bf16[2,64,32,128]{3,2,1,0:T(8,128)(2,1)S(1)}, bf16[2,64,32,128]{3,2,1,0:T(8,128)(2,1)S(1)}, u32[]{:S(2)}, u32[]{:S(2)}) collective-permute-start(bf16[2,64,32,128]{3,2,1,0:T(8,128)(2,1)S(1)} %prepare.5.refs_0_), channel_id=1, source_target_pairs={{2,0},{1,1},{4,2},{3,3},{6,4},{5,5},{8,6},{7,7},{10,8},{9,9},{12,1... | collective-permute-start | bytes 3145736 | tf_op jit(solution)/shard_map/ppermute | solution.py:306
  23.0 2.3 %copy-start = (bf16[128,144,128]{2,1,0:T(8,128)(2,1)S(1)}, bf16[128,144,128]{2,1,0:T(8,128)(2,1)}, u32[]{:S(2)}) copy-start(bf16[128,144,128]{2,1,0:T(8,128)(2,1)} %x_ref.9) | copy-start | bytes 14155780
  28.1 4.3 %collective-permute-start.5 = (bf16[2,64,32,128]{3,2,1,0:T(8,128)(2,1)S(1)}, bf16[2,64,32,128]{3,2,1,0:T(8,128)(2,1)S(1)}, u32[]{:S(2)}, u32[]{:S(2)}) collective-permute-start(bf16[2,64,32,128]{3,2,1,0:T(8,128)(2,1)S(1)} %prepare.6.refs_1_), channel_id=1, source_target_pairs={{2,0},{1,1},{4,2},{3,3},{6,4},{5,5},{8,6},{7,7},{10,8},{9,9},{12,1... | collective-permute-start | bytes 3145736 | tf_op jit(solution)/shard_map/ppermute | solution.py:306
  31.6 20.7 %collective-permute-start.6 = (bf16[2,64,32,128]{3,2,1,0:T(8,128)(2,1)S(1)}, bf16[2,64,32,128]{3,2,1,0:T(8,128)(2,1)S(1)}, u32[]{:S(2)}, u32[]{:S(2)}) collective-permute-start(bf16[2,64,32,128]{3,2,1,0:T(8,128)(2,1)S(1)} %prepare.7.refs_2_), channel_id=1, source_target_pairs={{2,0},{1,1},{4,2},{3,3},{6,4},{5,5},{8,6},{7,7},{10,8},{9,9},{12,1... | collective-permute-start | bytes 3145736 | tf_op jit(solution)/shard_map/ppermute | solution.py:306
  32.4 38.6 %collective-permute-start.9 = (bf16[2,64,32,128]{3,2,1,0:T(8,128)(2,1)S(1)}, bf16[2,64,32,128]{3,2,1,0:T(8,128)(2,1)S(1)}, u32[]{:S(2)}, u32[]{:S(2)}) collective-permute-start(bf16[2,64,32,128]{3,2,1,0:T(8,128)(2,1)S(1)} %collective-permute-done.5.refs_6_), channel_id=1, source_target_pairs={{0,1},{1,0},{2,3},{3,2},{4,5},{5,4},{6,7},{7,6},{8,9},{9,8},{10,11... | collective-permute-start | bytes 3145736 | tf_op jit(solution)/shard_map/ppermute | solution.py:318
  48.5 5.3 %collective-permute-start.11 = (bf16[16,128]{1,0:T(8,128)(2,1)S(1)}, bf16[16,128]{1,0:T(8,128)(2,1)S(1)}, u32[]{:S(2)}, u32[]{:S(2)}) collective-permute-start(bf16[16,128]{1,0:T(8,128)(2,1)S(1)} %slice_bitcast_fusion), channel_id=1, source_target_pairs={{0,1},{1,0},{2,3},{3,2},{4,5},{5,4},{6,7},{7,6},{8,9},{9,8},{10,11... | collective-permute-start | bytes 12296 | tf_op jit(solution)/shard_map/ppermute | solution.py:308
  51.3 19.0 %collective-permute-start.8 = (bf16[2,64,32,128]{3,2,1,0:T(8,128)(2,1)S(1)}, bf16[2,64,32,128]{3,2,1,0:T(8,128)(2,1)S(1)}, u32[]{:S(2)}, u32[]{:S(2)}) collective-permute-start(bf16[2,64,32,128]{3,2,1,0:T(8,128)(2,1)S(1)} %prepare.8.refs_3_), channel_id=1, source_target_pairs={{2,0},{1,1},{4,2},{3,3},{6,4},{5,5},{8,6},{7,7},{10,8},{9,9},{12,1... | collective-permute-start | bytes 3145736 | tf_op jit(solution)/shard_map/ppermute | solution.py:306
  53.8 48.2 %collective-permute-start.18 = (bf16[2,16,144,128]{3,2,1,0:T(8,128)(2,1)S(1)}, bf16[2,16,144,128]{3,2,1,0:T(8,128)(2,1)S(1)}, u32[]{:S(2)}, u32[]{:S(2)}) collective-permute-start(bf16[2,16,144,128]{3,2,1,0:T(8,128)(2,1)S(1)} %get-tuple-element.57), channel_id=1, source_target_pairs={{3,1},{5,3},{7,5},{9,7},{11,9},{13,11},{15,13},{17,15},{19,17},{21... | collective-permute-start | bytes 3538952 | tf_op jit(solution)/shard_map/ppermute | solution.py:313
  61.5 11.4 %collective-permute-start.7 = (bf16[2,64,32,128]{3,2,1,0:T(8,128)(2,1)S(1)}, bf16[2,64,32,128]{3,2,1,0:T(8,128)(2,1)S(1)}, u32[]{:S(2)}, u32[]{:S(2)}) collective-permute-start(bf16[2,64,32,128]{3,2,1,0:T(8,128)(2,1)S(1)} %collective-permute-done.4.refs_5_), channel_id=1, source_target_pairs={{0,1},{1,0},{2,3},{3,2},{4,5},{5,4},{6,7},{7,6},{8,9},{9,8},{10,11... | collective-permute-start | bytes 3145736 | tf_op jit(solution)/shard_map/ppermute | solution.py:318
  62.6 40.0 %collective-permute-start.17 = (bf16[2,16,144,128]{3,2,1,0:T(8,128)(2,1)S(1)}, bf16[2,16,144,128]{3,2,1,0:T(8,128)(2,1)S(1)}, u32[]{:S(2)}, u32[]{:S(2)}) collective-permute-start(bf16[2,16,144,128]{3,2,1,0:T(8,128)(2,1)S(1)} %get-tuple-element.56), channel_id=1, source_target_pairs={{3,1},{5,3},{7,5},{9,7},{11,9},{13,11},{15,13},{17,15},{19,17},{21... | collective-permute-start | bytes 3538952 | tf_op jit(solution)/shard_map/ppermute | solution.py:313
  70.3 4.6 %collective-permute-start.10 = (bf16[2,64,16,128]{3,2,1,0:T(8,128)(2,1)S(1)}, bf16[2,64,16,128]{3,2,1,0:T(8,128)(2,1)S(1)}, u32[]{:S(2)}, u32[]{:S(2)}) collective-permute-start(bf16[2,64,16,128]{3,2,1,0:T(8,128)(2,1)S(1)} %prepare.9.refs_4_), channel_id=1, source_target_pairs={{2,0},{1,1},{4,2},{3,3},{6,4},{5,5},{8,6},{7,7},{10,8},{9,9},{12,1... | collective-permute-start | bytes 1572872 | tf_op jit(solution)/shard_map/ppermute | solution.py:306
  71.0 44.2 %collective-permute-start.16 = (bf16[2,16,144,128]{3,2,1,0:T(8,128)(2,1)S(1)}, bf16[2,16,144,128]{3,2,1,0:T(8,128)(2,1)S(1)}, u32[]{:S(2)}, u32[]{:S(2)}) collective-permute-start(bf16[2,16,144,128]{3,2,1,0:T(8,128)(2,1)S(1)} %get-tuple-element.55), channel_id=1, source_target_pairs={{3,1},{5,3},{7,5},{9,7},{11,9},{13,11},{15,13},{17,15},{19,17},{21... | collective-permute-start | bytes 3538952 | tf_op jit(solution)/shard_map/ppermute | solution.py:313
  73.0 54.9 %collective-permute-start.12 = (bf16[2,16,144,128]{3,2,1,0:T(8,128)(2,1)S(1)}, bf16[2,16,144,128]{3,2,1,0:T(8,128)(2,1)S(1)}, u32[]{:S(2)}, u32[]{:S(2)}) collective-permute-start(bf16[2,16,144,128]{3,2,1,0:T(8,128)(2,1)S(1)} %get-tuple-element.52), channel_id=1, source_target_pairs={{3,1},{5,3},{7,5},{9,7},{11,9},{13,11},{15,13},{17,15},{19,17},{21... | collective-permute-start | bytes 3538952 | tf_op jit(solution)/shard_map/ppermute | solution.py:313
  74.9 42.2 %collective-permute-start.14 = (bf16[2,64,32,128]{3,2,1,0:T(8,128)(2,1)S(1)}, bf16[2,64,32,128]{3,2,1,0:T(8,128)(2,1)S(1)}, u32[]{:S(2)}, u32[]{:S(2)}) collective-permute-start(bf16[2,64,32,128]{3,2,1,0:T(8,128)(2,1)S(1)} %collective-permute-done.8.refs_8_), channel_id=1, source_target_pairs={{0,1},{1,0},{2,3},{3,2},{4,5},{5,4},{6,7},{7,6},{8,9},{9,8},{10,11... | collective-permute-start | bytes 3145736 | tf_op jit(solution)/shard_map/ppermute | solution.py:318
  102.0 15.2 %collective-permute-start.13 = (bf16[2,64,32,128]{3,2,1,0:T(8,128)(2,1)S(1)}, bf16[2,64,32,128]{3,2,1,0:T(8,128)(2,1)S(1)}, u32[]{:S(2)}, u32[]{:S(2)}) collective-permute-start(bf16[2,64,32,128]{3,2,1,0:T(8,128)(2,1)S(1)} %collective-permute-done.6.refs_7_), channel_id=1, source_target_pairs={{0,1},{1,0},{2,3},{3,2},{4,5},{5,4},{6,7},{7,6},{8,9},{9,8},{10,11... | collective-permute-start | bytes 3145736 | tf_op jit(solution)/shard_map/ppermute | solution.py:318
  102.6 14.6 %collective-permute-start.15 = (bf16[2,64,16,128]{3,2,1,0:T(8,128)(2,1)S(1)}, bf16[2,64,16,128]{3,2,1,0:T(8,128)(2,1)S(1)}, u32[]{:S(2)}, u32[]{:S(2)}) collective-permute-start(bf16[2,64,16,128]{3,2,1,0:T(8,128)(2,1)S(1)} %collective-permute-done.10.refs_9_), channel_id=1, source_target_pairs={{0,1},{1,0},{2,3},{3,2},{4,5},{5,4},{6,7},{7,6},{8,9},{9,8},{10,11... | collective-permute-start | bytes 1572872 | tf_op jit(solution)/shard_map/ppermute | solution.py:318

commit v5 on v4

--- a/solution.py
+++ b/solution.py
@@ -22,34 +22,25 @@
 GROUP = 16
 VMEM = 32 * 1024 * 1024
 CHUNKS = (2, 2, 2, 2, 1)
-TOKEN = 1
+TOKEN = 0
 FIRST_ROUND_AFTER = 3
 AFTER = {2: 0, 3: 1}
 HALO_STEPS = 4
 
 
-def prepare_kernel(x_ref, lo_even, lo_odd, hi_even, hi_odd, sel_ref, inv_ref, ram_ref, raminv_ref,
+def prepare_kernel(begin, offsets, x_ref, lo_even, lo_odd, hi_even, hi_odd, sel_ref, inv_ref, ram_ref, raminv_ref,
                    table_ref, band_ref, bandinv_ref, out_ref, ext, wide):
-    channels, step, samples = x_ref.shape
+    channels, _, samples = x_ref.shape
+    windows = out_ref.shape[2]
+    step = STEP
     odd = lax.axis_index("blk") % 2 != 0
     ext_rows = ext.reshape(ext.shape[0] * PITCH, samples)
     wide_rows = wide.reshape(wide.shape[0] * PITCH, channels)
 
-    def put(at, ref):
+    def put(at, ref, window):
         count = ref.shape[0]
-        ext[at : at + count, :step, :] = ref[...].astype(jnp.float32)
-
-    @pl.when(odd)
-    def _():
-        put(0, lo_odd)
-        put(HW + channels, hi_odd)
-
-    @pl.when(jnp.logical_not(odd))
-    def _():
-        put(0, lo_even)
-        put(HW + channels, hi_even)
-
-    put(HW, x_ref)
+        ext[at : at + count, :step, :] = ref[:, window : window + step, :].astype(jnp.float32)
+
     sel = sel_ref[...]
     inv = inv_ref[...]
     ram = ram_ref[...]
@@ -58,37 +49,50 @@
     band = band_ref[...]
     bandinv = bandinv_ref[...]
     bins = table.shape[0] // 2
-    for start in range(0, step, GROUP):
-        group = range(start, start + GROUP)
-        around = [ext_rows[pl.ds(w, channels + 2 * HW, stride=PITCH), :] for w in group]
-        total = jnp.dot(
-            sel, jnp.concatenate([a.astype(jnp.bfloat16) for a in around], axis=1), preferred_element_type=jnp.float32
-        )
-        balanced = jnp.concatenate(
-            [
-                (a[HW : HW + channels] - total[:, n * samples : (n + 1) * samples] * inv).astype(jnp.bfloat16)
-                for n, a in enumerate(around)
-            ],
-            axis=0,
-        )
-        ram_sum = jnp.dot(jnp.abs(balanced), ram, preferred_element_type=jnp.float32)
-        envelope = ram_sum * raminv + EPSILON
-        normalized = (balanced.astype(jnp.float32) / envelope).astype(jnp.bfloat16)
-        spectra = lax.dot_general(table, normalized, (((1,), (1,)), ((), ())), preferred_element_type=jnp.float32)
-        re, im = spectra[:bins], spectra[bins:]
-        power = re * re + im * im
-        first = power.astype(jnp.bfloat16)
-        rest = power - first.astype(jnp.float32)
-        second = rest.astype(jnp.bfloat16)
-        third = (rest - second.astype(jnp.float32)).astype(jnp.bfloat16)
-        pieces = jnp.concatenate([first, second, third], axis=0)
-        band_sum = jnp.dot(band, pieces, preferred_element_type=jnp.float32)
-        for n, w in enumerate(group):
-            part = slice(n * channels, (n + 1) * channels)
-            scale = lax.rsqrt(jnp.maximum(band_sum[:, part] * bandinv, FLOOR))
-            wide_rows[pl.ds(w, bins, stride=PITCH), :] = re[:, part] * scale
-            wide_rows[pl.ds(bins * PITCH + w, bins, stride=PITCH), :] = im[:, part] * scale
-    out_ref[...] = wide[:, :step, :].reshape(2, bins, step, channels).astype(out_ref.dtype)
+    for done in range(0, windows, step):
+
+        @pl.when(odd)
+        def _():
+            put(0, lo_odd, offsets[1] + done)
+            put(HW + channels, hi_odd, offsets[3] + done)
+
+        @pl.when(jnp.logical_not(odd))
+        def _():
+            put(0, lo_even, offsets[0] + done)
+            put(HW + channels, hi_even, offsets[2] + done)
+
+        put(HW, x_ref, begin + done)
+        for start in range(0, step, GROUP):
+            group = range(start, start + GROUP)
+            around = [ext_rows[pl.ds(w, channels + 2 * HW, stride=PITCH), :] for w in group]
+            total = jnp.dot(
+                sel, jnp.concatenate([a.astype(jnp.bfloat16) for a in around], axis=1), preferred_element_type=jnp.float32
+            )
+            balanced = jnp.concatenate(
+                [
+                    (a[HW : HW + channels] - total[:, n * samples : (n + 1) * samples] * inv).astype(jnp.bfloat16)
+                    for n, a in enumerate(around)
+                ],
+                axis=0,
+            )
+            ram_sum = jnp.dot(jnp.abs(balanced), ram, preferred_element_type=jnp.float32)
+            envelope = ram_sum * raminv + EPSILON
+            normalized = (balanced.astype(jnp.float32) / envelope).astype(jnp.bfloat16)
+            spectra = lax.dot_general(table, normalized, (((1,), (1,)), ((), ())), preferred_element_type=jnp.float32)
+            re, im = spectra[:bins], spectra[bins:]
+            power = re * re + im * im
+            first = power.astype(jnp.bfloat16)
+            rest = power - first.astype(jnp.float32)
+            second = rest.astype(jnp.bfloat16)
+            third = (rest - second.astype(jnp.float32)).astype(jnp.bfloat16)
+            pieces = jnp.concatenate([first, second, third], axis=0)
+            band_sum = jnp.dot(band, pieces, preferred_element_type=jnp.float32)
+            for n, w in enumerate(group):
+                part = slice(n * channels, (n + 1) * channels)
+                scale = lax.rsqrt(jnp.maximum(band_sum[:, part] * bandinv, FLOOR))
+                wide_rows[pl.ds(w, bins, stride=PITCH), :] = re[:, part] * scale
+                wide_rows[pl.ds(bins * PITCH + w, bins, stride=PITCH), :] = im[:, part] * scale
+        out_ref[:, :, done : done + step, :] = wide[:, :step, :].reshape(2, bins, step, channels).astype(out_ref.dtype)
 
 
 def borders_kernel(early, x_ref, first_ref, rest_ref, inner_ref, sems):
@@ -125,15 +129,12 @@
 def prepare(x, halos, first, windows, consts):
     channels, _, samples = x.shape
     bins = samples // 2
-    whole = lambda a: pl.BlockSpec(a.shape, lambda i: (0,) * a.ndim)
-    part = lambda rows, start: pl.BlockSpec((rows, STEP, samples), lambda i: (0, start // STEP + i, 0))
+    operands = [x, *[a for a, _ in halos], *consts]
+    inside = pl.BlockSpec(memory_space=pltpu.VMEM)
     return pl.pallas_call(
-        prepare_kernel,
-        grid=(windows // STEP,),
-        in_specs=[part(channels, first)]
-        + [part(HW, start) for _, start in halos]
-        + [whole(a) for a in consts],
-        out_specs=pl.BlockSpec((2, bins, STEP, channels), lambda i: (0, 0, i, 0)),
+        functools.partial(prepare_kernel, first, [start for _, start in halos]),
+        in_specs=[inside] * len(operands),
+        out_specs=inside,
         out_shape=jax.ShapeDtypeStruct((2, bins, windows, channels), jnp.bfloat16),
         scratch_shapes=[
             pltpu.VMEM((channels + 2 * HW, PITCH, samples), jnp.float32),
@@ -142,7 +143,7 @@
         compiler_params=pltpu.CompilerParams(vmem_limit_bytes=VMEM),
         cost_estimate=pl.CostEstimate(flops=1, bytes_accessed=1, transcendentals=0),
         name="prepare",
-    )(x, *[a for a, _ in halos], *consts)
+    )(*operands)
 
 
 def correlate_kernel(n_own, scale, *refs):

time: 130 us -> 129 us (level)
  waiting for transfers between devices: 19.3 us -> 22 us
  starting transfers between devices: 77.3 us -> 74.8 us
    ppermute x1, starting transfers between devices: 0.01 us -> 16.4 us  [per_device(): token = lax.ppermute(held[TOKEN][0, 0, :STEP], 'blk', swap)]
    ppermute x5, starting transfers between devices: 44.3 us -> 31.6 us  [per_device(): other.append(lax.ppermute(held[n], 'blk', swap))]
    ppermute x4, starting transfers between devices: 19.2 us -> 12.9 us  [per_device(): far.append(lax.ppermute(mine, 'blk', second_pairs))]
    ppermute x4, waiting for transfers between devices: 14.2 us -> 16.5 us  [per_device(): far.append(lax.ppermute(mine, 'blk', second_pairs))]
where the time goes in v5:
time: 129 us
  starting transfers between devices  74.8 us (58%)
  Pallas kernels  26.8 us (21%)
  waiting for transfers between devices  22 us (17%)
  local copies, waits for them, and re-layouts  4.49 us (3%)
    ppermute x5, starting transfers between devices, per_device(): other.append(lax.ppermute(held[n], 'blk', swap))  31.6 us
    ppermute x4, waiting for transfers between devices, per_device(): far.append(lax.ppermute(mine, 'blk', second_pairs))  16.5 us
    ppermute x1, starting transfers between devices, per_device(): token = lax.ppermute(held[TOKEN][0, 0, :STEP], 'blk', swap)  16.4 us
    ppermute x4, starting transfers between devices, per_device(): far.append(lax.ppermute(mine, 'blk', second_pairs))  12.9 us
    pallas_call x5, Pallas kernels, prepare(): pl.pallas_call(functools.partial(prepare_kernel, first, [start for _, sta...  11.1 us
    pallas_call x4, Pallas kernels, correlate_chunk(): pl.pallas_call(functools.partial(correlate_chunk_kernel, len(own), 1.0 /...  7.74 us
    pallas_call x1, Pallas kernels, correlate(): pl.pallas_call(functools.partial(correlate_kernel, len(own), 1.0 / math.s...  5.63 us
    ppermute x1, waiting for transfers between devices, per_device(): across_rest = lax.ppermute(outer_rest, 'blk', cross)  4.89 us
  transfers between devices with their start and end apart: 19, of which 5 were waited for; matrix products, arithmetic and copies ran while one was open for 2% of the time, Pallas kernels for 18%

profile of v5, /device:TPU:1, one launch (start us, length us, event | category | flops | bytes accessed | tf_op | source)
XLA Modules:
  0.0 128.8 jit_solution(4297461715419258102)
XLA Ops:
  0.0 2.3 %borders.1 = (bf16[16,64,128]{2,1,0:T(8,128)(2,1)}, bf16[16,80,128]{2,1,0:T(8,128)(2,1)}, bf16[16,144,128]{2,1,0:T(8,128)(2,1)}) custom-call(bf16[128,144,128]{2,1,0:T(8,128)(2,1)} %x_ref.9), custom_call_target="tpu_custom_call" | custom-call | flops 1 | bytes 1 | tf_op jit(solution)/shard_map/borders/pallas_call | solution.py:118
  2.3 4.5 %collective-permute-start = (bf16[16,64,128]{2,1,0:T(8,128)(2,1)}, bf16[16,64,128]{2,1,0:T(8,128)(2,1)S(1)}, u32[]{:S(2)}, u32[]{:S(2)}) collective-permute-start(bf16[16,64,128]{2,1,0:T(8,128)(2,1)} %get-tuple-element.32), channel_id=1, source_target_pairs={{1,2},{3,4},{5,6},{7,8},{9,10},{11,12},{13,14},{15,16},{17,18},{19... | collective-permute-start | bytes 786440 | tf_op jit(solution)/shard_map/ppermute | solution.py:289
  6.8 1.3 %collective-permute-start.3 = (bf16[16,64,128]{2,1,0:T(8,128)(2,1)}, bf16[16,64,128]{2,1,0:T(8,128)(2,1)S(1)}, u32[]{:S(2)}, u32[]{:S(2)}) collective-permute-start(bf16[16,64,128]{2,1,0:T(8,128)(2,1)} %get-tuple-element.32), channel_id=1, source_target_pairs={{2,1},{4,3},{6,5},{8,7},{10,9},{12,11},{14,13},{16,15},{18,17},{20... | collective-permute-start | bytes 786440 | tf_op jit(solution)/shard_map/ppermute | solution.py:288
  8.1 0.1 collective-permute-start.2
  8.2 4.3 %collective-permute-start.1 = (bf16[16,80,128]{2,1,0:T(8,128)(2,1)}, bf16[16,80,128]{2,1,0:T(8,128)(2,1)S(1)}, u32[]{:S(2)}, u32[]{:S(2)}) collective-permute-start(bf16[16,80,128]{2,1,0:T(8,128)(2,1)} %get-tuple-element.33), channel_id=1, source_target_pairs={{1,2},{2,1},{3,4},{4,3},{5,6},{6,5},{7,8},{8,7},{9,10},{10,9},{11,... | collective-permute-start | bytes 983048 | tf_op jit(solution)/shard_map/ppermute | solution.py:291
  12.5 0.1 compare_convert_fusion.1
  12.6 0.1 fusion
  12.7 0.0 copy-start.1
  12.7 0.0 copy-start.2
  12.8 0.0 copy-start.3
  12.8 1.3 %slice.66.x_ref = bf16[128,32,128]{2,1,0:T(8,128)(2,1)S(1)} slice(bf16[128,144,128]{2,1,0:T(8,128)(2,1)} %x_ref.9), slice={[0:128], [0:32], [0:128]} | slice | bytes 2097152 | tf_op jit(solution)/shard_map/slice | solution.py:305
  14.1 0.1 copy.13.band_ref
  14.2 0.5 collective-permute-done.3.hi_odd
  14.8 0.1 broadcast_in_dim.4.inv_ref
  14.9 0.1 broadcast_in_dim.5.bandinv_ref
  15.0 2.4 %prepare.5.refs_0_ = bf16[2,64,32,128]{3,2,1,0:T(8,128)(2,1)S(1)} custom-call(bf16[128,32,128]{2,1,0:T(8,128)(2,1)S(1)} %slice.66.x_ref, bf16[16,64,128]{2,1,0:T(8,128)(2,1)S(1)} %collective-permute-done.lo_even, bf16[16,144,128]{2,1,0:T(8,128)(2,1)S(1)} %collective-permute-done.2.lo_odd.hi_even, ...), custom_call_target="tpu_custom_call" | custom-call | flops 1 | bytes 1 | tf_op jit(solution)/shard_map/prepare/pallas_call | solution.py:134
  17.4 0.7 collective-permute-start.4
  18.1 4.9 %collective-permute-done.1.lo_even.hi_odd = bf16[16,80,128]{2,1,0:T(8,128)(2,1)S(1)} collective-permute-done((bf16[16,80,128]{2,1,0:T(8,128)(2,1)}, bf16[16,80,128]{2,1,0:T(8,128)(2,1)S(1)}, u32[]{:S(2)}, u32[]{:S(2)}) %collective-permute-start.1) | collective-permute-done | bytes 327712 | tf_op jit(solution)/shard_map/ppermute | solution.py:291
  23.0 2.3 %copy-done = bf16[128,144,128]{2,1,0:T(8,128)(2,1)S(1)} copy-done((bf16[128,144,128]{2,1,0:T(8,128)(2,1)S(1)}, bf16[128,144,128]{2,1,0:T(8,128)(2,1)}, u32[]{:S(2)}) %copy-start) | copy-done | bytes 4718616
  25.4 2.4 %prepare.6.refs_1_ = bf16[2,64,32,128]{3,2,1,0:T(8,128)(2,1)S(1)} custom-call(bf16[128,144,128]{2,1,0:T(8,128)(2,1)S(1)} %copy-done, bf16[16,64,128]{2,1,0:T(8,128)(2,1)S(1)} %collective-permute-done.lo_even, bf16[16,144,128]{2,1,0:T(8,128)(2,1)S(1)} %collective-permute-done.2.lo_odd.hi_even, ...), custom_call_target="tpu_custom_call" | custom-call | flops 1 | bytes 1 | tf_op jit(solution)/shard_map/prepare/pallas_call | solution.py:134
  27.8 0.7 collective-permute-start.5
  28.5 2.4 %prepare.7.refs_2_ = bf16[2,64,32,128]{3,2,1,0:T(8,128)(2,1)S(1)} custom-call(bf16[128,144,128]{2,1,0:T(8,128)(2,1)S(1)} %copy-done, bf16[16,80,128]{2,1,0:T(8,128)(2,1)S(1)} %collective-permute-done.1.lo_even.hi_odd, bf16[16,144,128]{2,1,0:T(8,128)(2,1)S(1)} %collective-permute-done.2.lo_odd.hi_even, ...), custom_call_target="tpu_custom_call" | custom-call | flops 1 | bytes 1 | tf_op jit(solution)/shard_map/prepare/pallas_call | solution.py:134
  31.0 0.7 collective-permute-start.6
  31.7 0.1 slice_dynamic-update-slice_fusion.3
  31.8 16.4 %collective-permute-start.11 = (bf16[16,128]{1,0:T(8,128)(2,1)S(1)}, bf16[16,128]{1,0:T(8,128)(2,1)S(1)}, u32[]{:S(2)}, u32[]{:S(2)}) collective-permute-start(bf16[16,128]{1,0:T(8,128)(2,1)S(1)} %slice_bitcast_fusion), channel_id=1, source_target_pairs={{0,1},{1,0},{2,3},{3,2},{4,5},{5,4},{6,7},{7,6},{8,9},{9,8},{10,11... | collective-permute-start | bytes 12296 | tf_op jit(solution)/shard_map/ppermute | solution.py:309
  48.2 2.4 %prepare.8.refs_3_ = bf16[2,64,32,128]{3,2,1,0:T(8,128)(2,1)S(1)} custom-call(bf16[128,144,128]{2,1,0:T(8,128)(2,1)S(1)} %copy-done, bf16[16,80,128]{2,1,0:T(8,128)(2,1)S(1)} %collective-permute-done.1.lo_even.hi_odd, bf16[16,144,128]{2,1,0:T(8,128)(2,1)S(1)} %collective-permute-done.2.lo_odd.hi_even, ...), custom_call_target="tpu_custom_call" | custom-call | flops 1 | bytes 1 | tf_op jit(solution)/shard_map/prepare/pallas_call | solution.py:134
  50.7 0.7 collective-permute-start.8
  51.4 7.3 %collective-permute-start.9 = (bf16[2,64,32,128]{3,2,1,0:T(8,128)(2,1)S(1)}, bf16[2,64,32,128]{3,2,1,0:T(8,128)(2,1)S(1)}, u32[]{:S(2)}, u32[]{:S(2)}) collective-permute-start(bf16[2,64,32,128]{3,2,1,0:T(8,128)(2,1)S(1)} %collective-permute-done.5.refs_6_), channel_id=1, source_target_pairs={{0,1},{1,0},{2,3},{3,2},{4,5},{5,4},{6,7},{7,6},{8,9},{9,8},{10,11... | collective-permute-start | bytes 3145736 | tf_op jit(solution)/shard_map/ppermute | solution.py:319
  58.7 0.1 slice_dynamic-update-slice_fusion.2
  58.9 0.1 slice_dynamic-update-slice_fusion.1
  59.0 1.4 %prepare.9.refs_4_ = bf16[2,64,16,128]{3,2,1,0:T(8,128)(2,1)S(1)} custom-call(bf16[128,144,128]{2,1,0:T(8,128)(2,1)S(1)} %copy-done, bf16[16,80,128]{2,1,0:T(8,128)(2,1)S(1)} %collective-permute-done.1.lo_even.hi_odd, bf16[16,144,128]{2,1,0:T(8,128)(2,1)S(1)} %collective-permute-done.2.lo_odd.hi_even, ...), custom_call_target="tpu_custom_call" | custom-call | flops 1 | bytes 1 | tf_op jit(solution)/shard_map/prepare/pallas_call | solution.py:134
  60.4 0.1 slice_dynamic-update-slice_fusion
  60.6 0.1 slice_dynamic-update-slice_fusion.16
  60.7 1.9 %collective-permute-start.18 = (bf16[2,16,144,128]{3,2,1,0:T(8,128)(2,1)S(1)}, bf16[2,16,144,128]{3,2,1,0:T(8,128)(2,1)S(1)}, u32[]{:S(2)}, u32[]{:S(2)}) collective-permute-start(bf16[2,16,144,128]{3,2,1,0:T(8,128)(2,1)S(1)} %get-tuple-element.57), channel_id=1, source_target_pairs={{3,1},{5,3},{7,5},{9,7},{11,9},{13,11},{15,13},{17,15},{19,17},{21... | collective-permute-start | bytes 3538952 | tf_op jit(solution)/shard_map/ppermute | solution.py:314
  62.6 0.1 collective-permute-start.7
  62.7 7.2 %collective-permute-start.17 = (bf16[2,16,144,128]{3,2,1,0:T(8,128)(2,1)S(1)}, bf16[2,16,144,128]{3,2,1,0:T(8,128)(2,1)S(1)}, u32[]{:S(2)}, u32[]{:S(2)}) collective-permute-start(bf16[2,16,144,128]{3,2,1,0:T(8,128)(2,1)S(1)} %get-tuple-element.56), channel_id=1, source_target_pairs={{3,1},{5,3},{7,5},{9,7},{11,9},{13,11},{15,13},{17,15},{19,17},{21... | collective-permute-start | bytes 3538952 | tf_op jit(solution)/shard_map/ppermute | solution.py:314
  69.9 0.7 collective-permute-start.10
  70.6 1.9 %collective-permute-start.16 = (bf16[2,16,144,128]{3,2,1,0:T(8,128)(2,1)S(1)}, bf16[2,16,144,128]{3,2,1,0:T(8,128)(2,1)S(1)}, u32[]{:S(2)}, u32[]{:S(2)}) collective-permute-start(bf16[2,16,144,128]{3,2,1,0:T(8,128)(2,1)S(1)} %get-tuple-element.55), channel_id=1, source_target_pairs={{3,1},{5,3},{7,5},{9,7},{11,9},{13,11},{15,13},{17,15},{19,17},{21... | collective-permute-start | bytes 3538952 | tf_op jit(solution)/shard_map/ppermute | solution.py:314
  72.5 1.9 %collective-permute-start.12 = (bf16[2,16,144,128]{3,2,1,0:T(8,128)(2,1)S(1)}, bf16[2,16,144,128]{3,2,1,0:T(8,128)(2,1)S(1)}, u32[]{:S(2)}, u32[]{:S(2)}) collective-permute-start(bf16[2,16,144,128]{3,2,1,0:T(8,128)(2,1)S(1)} %get-tuple-element.52), channel_id=1, source_target_pairs={{3,1},{5,3},{7,5},{9,7},{11,9},{13,11},{15,13},{17,15},{19,17},{21... | collective-permute-start | bytes 3538952 | tf_op jit(solution)/shard_map/ppermute | solution.py:314
  74.5 24.2 %collective-permute-start.14 = (bf16[2,64,32,128]{3,2,1,0:T(8,128)(2,1)S(1)}, bf16[2,64,32,128]{3,2,1,0:T(8,128)(2,1)S(1)}, u32[]{:S(2)}, u32[]{:S(2)}) collective-permute-start(bf16[2,64,32,128]{3,2,1,0:T(8,128)(2,1)S(1)} %collective-permute-done.8.refs_8_), channel_id=1, source_target_pairs={{0,1},{1,0},{2,3},{3,2},{4,5},{5,4},{6,7},{7,6},{8,9},{9,8},{10,11... | collective-permute-start | bytes 3145736 | tf_op jit(solution)/shard_map/ppermute | solution.py:319
  98.7 2.8 %collective-permute-done.17.refs_10_ = bf16[2,16,144,128]{3,2,1,0:T(8,128)(2,1)S(1)} collective-permute-done((bf16[2,16,144,128]{3,2,1,0:T(8,128)(2,1)S(1)}, bf16[2,16,144,128]{3,2,1,0:T(8,128)(2,1)S(1)}, u32[]{:S(2)}, u32[]{:S(2)}) %collective-permute-start.17) | collective-permute-done | bytes 1179680 | tf_op jit(solution)/shard_map/ppermute | solution.py:314
  101.5 1.9 %correlate_chunk.4.refs_11_ = bf16[128,2,2,64,128]{4,3,2,1,0:T(8,128)(2,1)} custom-call(bf16[2,64,32,128]{3,2,1,0:T(8,128)(2,1)S(1)} %prepare.5.refs_0_, bf16[2,64,32,128]{3,2,1,0:T(8,128)(2,1)S(1)} %prepare.6.refs_1_, bf16[2,64,32,128]{3,2,1,0:T(8,128)(2,1)S(1)} %prepare.7.refs_2_, bf16[2,64,32,128]{3,2,1,0:T(8,128)(2,1)S(1)} %prepare.8.refs_3_, ...), custom_call_target="tpu_custom_call" | custom-call | flops 1 | bytes 1 | tf_op jit(solution)/shard_map/correlate_chunk/pallas_call | solution.py:230
  103.4 2.0 %correlate_chunk.5.refs_11_ = bf16[128,2,2,64,128]{4,3,2,1,0:T(8,128)(2,1)} custom-call(bf16[2,64,32,128]{3,2,1,0:T(8,128)(2,1)S(1)} %prepare.5.refs_0_, bf16[2,64,32,128]{3,2,1,0:T(8,128)(2,1)S(1)} %prepare.6.refs_1_, bf16[2,64,32,128]{3,2,1,0:T(8,128)(2,1)S(1)} %prepare.7.refs_2_, ...), custom_call_target="tpu_custom_call", output_to_operand_aliasing={{}: (11, {})} | custom-call | flops 1 | bytes 1 | tf_op jit(solution)/shard_map/correlate_chunk/pallas_call | solution.py:230
  105.4 8.7 %collective-permute-done.16.refs_10_ = bf16[2,16,144,128]{3,2,1,0:T(8,128)(2,1)S(1)} collective-permute-done((bf16[2,16,144,128]{3,2,1,0:T(8,128)(2,1)S(1)}, bf16[2,16,144,128]{3,2,1,0:T(8,128)(2,1)S(1)}, u32[]{:S(2)}, u32[]{:S(2)}) %collective-permute-start.16) | collective-permute-done | bytes 1179680 | tf_op jit(solution)/shard_map/ppermute | solution.py:314
  114.1 1.9 %correlate_chunk.6.refs_10_ = bf16[128,2,2,64,128]{4,3,2,1,0:T(8,128)(2,1)} custom-call(bf16[2,64,32,128]{3,2,1,0:T(8,128)(2,1)S(1)} %prepare.5.refs_0_, bf16[2,64,32,128]{3,2,1,0:T(8,128)(2,1)S(1)} %prepare.6.refs_1_, bf16[2,64,32,128]{3,2,1,0:T(8,128)(2,1)S(1)} %prepare.7.refs_2_, ...), custom_call_target="tpu_custom_call", output_to_operand_aliasing={{}: (11, {})} | custom-call | flops 1 | bytes 1 | tf_op jit(solution)/shard_map/correlate_chunk/pallas_call | solution.py:230
  116.1 5.6 %correlate.1.refs_11_ = bf16[128,2,2,64,128]{4,3,2,1,0:T(8,128)(2,1)} custom-call(bf16[2,64,32,128]{3,2,1,0:T(8,128)(2,1)S(1)} %prepare.5.refs_0_, bf16[2,64,32,128]{3,2,1,0:T(8,128)(2,1)S(1)} %prepare.6.refs_1_, bf16[2,64,32,128]{3,2,1,0:T(8,128)(2,1)S(1)} %prepare.7.refs_2_, ...), custom_call_target="tpu_custom_call", output_to_operand_aliasing={{}: (10, {})} | custom-call | flops 1 | bytes 1 | tf_op jit(solution)/shard_map/correlate/pallas_call | solution.py:184
  121.7 5.0 %collective-permute-done.12.refs_10_ = bf16[2,16,144,128]{3,2,1,0:T(8,128)(2,1)S(1)} collective-permute-done((bf16[2,16,144,128]{3,2,1,0:T(8,128)(2,1)S(1)}, bf16[2,16,144,128]{3,2,1,0:T(8,128)(2,1)S(1)}, u32[]{:S(2)}, u32[]{:S(2)}) %collective-permute-start.12) | collective-permute-done | bytes 1179680 | tf_op jit(solution)/shard_map/ppermute | solution.py:314
  126.7 1.9 %correlate_chunk.7 = bf16[128,2,2,64,128]{4,3,2,1,0:T(8,128)(2,1)} custom-call(bf16[2,64,32,128]{3,2,1,0:T(8,128)(2,1)S(1)} %prepare.5.refs_0_, bf16[2,64,32,128]{3,2,1,0:T(8,128)(2,1)S(1)} %prepare.6.refs_1_, bf16[2,64,32,128]{3,2,1,0:T(8,128)(2,1)S(1)} %prepare.7.refs_2_, ...), custom_call_target="tpu_custom_call", output_to_operand_aliasing={{}: (11, {})} | custom-call | flops 1 | bytes 1 | tf_op jit(solution)/shard_map/correlate_chunk/pallas_call | solution.py:230
  (30 shorter events, 0.1 us)
Async XLA Ops:
  0.0 12.7 %copy-start.4 = (pred[128,160]{1,0:T(32,128)(4,1)S(1)}, pred[128,160]{1,0:T(32,128)(4,1)}, u32[]{:S(2)}) copy-start(pred[128,160]{1,0:T(32,128)(4,1)} %constant.36.clone) | copy-start | bytes 61444
  0.0 12.5 %copy-start.5 = (s32[64]{0:T(128)S(1)}, s32[64]{0:T(128)}, u32[]{:S(2)}) copy-start(s32[64]{0:T(128)} %param.9) | copy-start | bytes 772
  2.3 11.9 %collective-permute-start = (bf16[16,64,128]{2,1,0:T(8,128)(2,1)}, bf16[16,64,128]{2,1,0:T(8,128)(2,1)S(1)}, u32[]{:S(2)}, u32[]{:S(2)}) collective-permute-start(bf16[16,64,128]{2,1,0:T(8,128)(2,1)} %get-tuple-element.32), channel_id=1, source_target_pairs={{1,2},{3,4},{5,6},{7,8},{9,10},{11,12},{13,14},{15,16},{17,18},{19... | collective-permute-start | bytes 786440 | tf_op jit(solution)/shard_map/ppermute | solution.py:289
  6.8 8.0 %collective-permute-start.3 = (bf16[16,64,128]{2,1,0:T(8,128)(2,1)}, bf16[16,64,128]{2,1,0:T(8,128)(2,1)S(1)}, u32[]{:S(2)}, u32[]{:S(2)}) collective-permute-start(bf16[16,64,128]{2,1,0:T(8,128)(2,1)} %get-tuple-element.32), channel_id=1, source_target_pairs={{2,1},{4,3},{6,5},{8,7},{10,9},{12,11},{14,13},{16,15},{18,17},{20... | collective-permute-start | bytes 786440 | tf_op jit(solution)/shard_map/ppermute | solution.py:288
  8.1 6.7 %collective-permute-start.2 = (bf16[16,144,128]{2,1,0:T(8,128)(2,1)}, bf16[16,144,128]{2,1,0:T(8,128)(2,1)S(1)}, u32[]{:S(2)}, u32[]{:S(2)}) collective-permute-start(bf16[16,144,128]{2,1,0:T(8,128)(2,1)} %get-tuple-element.34), channel_id=1, source_target_pairs={{0,1},{1,0},{2,3},{3,2},{4,5},{5,4},{6,7},{7,6},{8,9},{9,8},{10,11... | collective-permute-start | bytes 1769480 | tf_op jit(solution)/shard_map/ppermute | solution.py:290
  8.2 14.8 %collective-permute-start.1 = (bf16[16,80,128]{2,1,0:T(8,128)(2,1)}, bf16[16,80,128]{2,1,0:T(8,128)(2,1)S(1)}, u32[]{:S(2)}, u32[]{:S(2)}) collective-permute-start(bf16[16,80,128]{2,1,0:T(8,128)(2,1)} %get-tuple-element.33), channel_id=1, source_target_pairs={{1,2},{2,1},{3,4},{4,3},{5,6},{6,5},{7,8},{8,7},{9,10},{10,9},{11,... | collective-permute-start | bytes 983048 | tf_op jit(solution)/shard_map/ppermute | solution.py:291
  12.7 2.2 %copy-start.1 = (bf16[128,128]{1,0:T(8,128)(2,1)S(1)}, bf16[128,128]{1,0:T(8,128)(2,1)}, u32[]{:S(2)}) copy-start(bf16[128,128]{1,0:T(8,128)(2,1)} %constant.37.clone.ram_ref) | copy-start | bytes 98308
  12.7 2.2 %copy-start.2 = (bf16[128,128]{1,0:T(8,128)(2,1)S(1)}, bf16[128,128]{1,0:T(8,128)(2,1)}, u32[]{:S(2)}) copy-start(bf16[128,128]{1,0:T(8,128)(2,1)} %constant.39.clone.table_ref) | copy-start | bytes 98308
  12.8 2.2 %copy-start.3 = (f32[1,128]{1,0:T(1,128)S(1)}, f32[1,128]{1,0:T(1,128)}, u32[]{:S(2)}) copy-start(f32[1,128]{1,0:T(1,128)} %constant.38.clone.raminv_ref) | copy-start | bytes 1540
  17.4 11.1 %collective-permute-start.4 = (bf16[2,64,32,128]{3,2,1,0:T(8,128)(2,1)S(1)}, bf16[2,64,32,128]{3,2,1,0:T(8,128)(2,1)S(1)}, u32[]{:S(2)}, u32[]{:S(2)}) collective-permute-start(bf16[2,64,32,128]{3,2,1,0:T(8,128)(2,1)S(1)} %prepare.5.refs_0_), channel_id=1, source_target_pairs={{2,0},{1,1},{4,2},{3,3},{6,4},{5,5},{8,6},{7,7},{10,8},{9,9},{12,1... | collective-permute-start | bytes 3145736 | tf_op jit(solution)/shard_map/ppermute | solution.py:307
  23.0 2.3 %copy-start = (bf16[128,144,128]{2,1,0:T(8,128)(2,1)S(1)}, bf16[128,144,128]{2,1,0:T(8,128)(2,1)}, u32[]{:S(2)}) copy-start(bf16[128,144,128]{2,1,0:T(8,128)(2,1)} %x_ref.9) | copy-start | bytes 14155780
  27.8 4.0 %collective-permute-start.5 = (bf16[2,64,32,128]{3,2,1,0:T(8,128)(2,1)S(1)}, bf16[2,64,32,128]{3,2,1,0:T(8,128)(2,1)S(1)}, u32[]{:S(2)}, u32[]{:S(2)}) collective-permute-start(bf16[2,64,32,128]{3,2,1,0:T(8,128)(2,1)S(1)} %prepare.6.refs_1_), channel_id=1, source_target_pairs={{2,0},{1,1},{4,2},{3,3},{6,4},{5,5},{8,6},{7,7},{10,8},{9,9},{12,1... | collective-permute-start | bytes 3145736 | tf_op jit(solution)/shard_map/ppermute | solution.py:307
  31.0 28.1 %collective-permute-start.6 = (bf16[2,64,32,128]{3,2,1,0:T(8,128)(2,1)S(1)}, bf16[2,64,32,128]{3,2,1,0:T(8,128)(2,1)S(1)}, u32[]{:S(2)}, u32[]{:S(2)}) collective-permute-start(bf16[2,64,32,128]{3,2,1,0:T(8,128)(2,1)S(1)} %prepare.7.refs_2_), channel_id=1, source_target_pairs={{2,0},{1,1},{4,2},{3,3},{6,4},{5,5},{8,6},{7,7},{10,8},{9,9},{12,1... | collective-permute-start | bytes 3145736 | tf_op jit(solution)/shard_map/ppermute | solution.py:307
  31.8 28.9 %collective-permute-start.11 = (bf16[16,128]{1,0:T(8,128)(2,1)S(1)}, bf16[16,128]{1,0:T(8,128)(2,1)S(1)}, u32[]{:S(2)}, u32[]{:S(2)}) collective-permute-start(bf16[16,128]{1,0:T(8,128)(2,1)S(1)} %slice_bitcast_fusion), channel_id=1, source_target_pairs={{0,1},{1,0},{2,3},{3,2},{4,5},{5,4},{6,7},{7,6},{8,9},{9,8},{10,11... | collective-permute-start | bytes 12296 | tf_op jit(solution)/shard_map/ppermute | solution.py:309
  50.7 19.2 %collective-permute-start.8 = (bf16[2,64,32,128]{3,2,1,0:T(8,128)(2,1)S(1)}, bf16[2,64,32,128]{3,2,1,0:T(8,128)(2,1)S(1)}, u32[]{:S(2)}, u32[]{:S(2)}) collective-permute-start(bf16[2,64,32,128]{3,2,1,0:T(8,128)(2,1)S(1)} %prepare.8.refs_3_), channel_id=1, source_target_pairs={{2,0},{1,1},{4,2},{3,3},{6,4},{5,5},{8,6},{7,7},{10,8},{9,9},{12,1... | collective-permute-start | bytes 3145736 | tf_op jit(solution)/shard_map/ppermute | solution.py:307
  51.4 19.2 %collective-permute-start.9 = (bf16[2,64,32,128]{3,2,1,0:T(8,128)(2,1)S(1)}, bf16[2,64,32,128]{3,2,1,0:T(8,128)(2,1)S(1)}, u32[]{:S(2)}, u32[]{:S(2)}) collective-permute-start(bf16[2,64,32,128]{3,2,1,0:T(8,128)(2,1)S(1)} %collective-permute-done.5.refs_6_), channel_id=1, source_target_pairs={{0,1},{1,0},{2,3},{3,2},{4,5},{5,4},{6,7},{7,6},{8,9},{9,8},{10,11... | collective-permute-start | bytes 3145736 | tf_op jit(solution)/shard_map/ppermute | solution.py:319
  60.7 38.0 %collective-permute-start.18 = (bf16[2,16,144,128]{3,2,1,0:T(8,128)(2,1)S(1)}, bf16[2,16,144,128]{3,2,1,0:T(8,128)(2,1)S(1)}, u32[]{:S(2)}, u32[]{:S(2)}) collective-permute-start(bf16[2,16,144,128]{3,2,1,0:T(8,128)(2,1)S(1)} %get-tuple-element.57), channel_id=1, source_target_pairs={{3,1},{5,3},{7,5},{9,7},{11,9},{13,11},{15,13},{17,15},{19,17},{21... | collective-permute-start | bytes 3538952 | tf_op jit(solution)/shard_map/ppermute | solution.py:314
  62.6 9.9 %collective-permute-start.7 = (bf16[2,64,32,128]{3,2,1,0:T(8,128)(2,1)S(1)}, bf16[2,64,32,128]{3,2,1,0:T(8,128)(2,1)S(1)}, u32[]{:S(2)}, u32[]{:S(2)}) collective-permute-start(bf16[2,64,32,128]{3,2,1,0:T(8,128)(2,1)S(1)} %collective-permute-done.4.refs_5_), channel_id=1, source_target_pairs={{0,1},{1,0},{2,3},{3,2},{4,5},{5,4},{6,7},{7,6},{8,9},{9,8},{10,11... | collective-permute-start | bytes 3145736 | tf_op jit(solution)/shard_map/ppermute | solution.py:319
  62.7 38.8 %collective-permute-start.17 = (bf16[2,16,144,128]{3,2,1,0:T(8,128)(2,1)S(1)}, bf16[2,16,144,128]{3,2,1,0:T(8,128)(2,1)S(1)}, u32[]{:S(2)}, u32[]{:S(2)}) collective-permute-start(bf16[2,16,144,128]{3,2,1,0:T(8,128)(2,1)S(1)} %get-tuple-element.56), channel_id=1, source_target_pairs={{3,1},{5,3},{7,5},{9,7},{11,9},{13,11},{15,13},{17,15},{19,17},{21... | collective-permute-start | bytes 3538952 | tf_op jit(solution)/shard_map/ppermute | solution.py:314
  69.9 4.6 %collective-permute-start.10 = (bf16[2,64,16,128]{3,2,1,0:T(8,128)(2,1)S(1)}, bf16[2,64,16,128]{3,2,1,0:T(8,128)(2,1)S(1)}, u32[]{:S(2)}, u32[]{:S(2)}) collective-permute-start(bf16[2,64,16,128]{3,2,1,0:T(8,128)(2,1)S(1)} %prepare.9.refs_4_), channel_id=1, source_target_pairs={{2,0},{1,1},{4,2},{3,3},{6,4},{5,5},{8,6},{7,7},{10,8},{9,9},{12,1... | collective-permute-start | bytes 1572872 | tf_op jit(solution)/shard_map/ppermute | solution.py:307
  70.6 43.5 %collective-permute-start.16 = (bf16[2,16,144,128]{3,2,1,0:T(8,128)(2,1)S(1)}, bf16[2,16,144,128]{3,2,1,0:T(8,128)(2,1)S(1)}, u32[]{:S(2)}, u32[]{:S(2)}) collective-permute-start(bf16[2,16,144,128]{3,2,1,0:T(8,128)(2,1)S(1)} %get-tuple-element.55), channel_id=1, source_target_pairs={{3,1},{5,3},{7,5},{9,7},{11,9},{13,11},{15,13},{17,15},{19,17},{21... | collective-permute-start | bytes 3538952 | tf_op jit(solution)/shard_map/ppermute | solution.py:314
  72.5 54.2 %collective-permute-start.12 = (bf16[2,16,144,128]{3,2,1,0:T(8,128)(2,1)S(1)}, bf16[2,16,144,128]{3,2,1,0:T(8,128)(2,1)S(1)}, u32[]{:S(2)}, u32[]{:S(2)}) collective-permute-start(bf16[2,16,144,128]{3,2,1,0:T(8,128)(2,1)S(1)} %get-tuple-element.52), channel_id=1, source_target_pairs={{3,1},{5,3},{7,5},{9,7},{11,9},{13,11},{15,13},{17,15},{19,17},{21... | collective-permute-start | bytes 3538952 | tf_op jit(solution)/shard_map/ppermute | solution.py:314
  74.5 41.6 %collective-permute-start.14 = (bf16[2,64,32,128]{3,2,1,0:T(8,128)(2,1)S(1)}, bf16[2,64,32,128]{3,2,1,0:T(8,128)(2,1)S(1)}, u32[]{:S(2)}, u32[]{:S(2)}) collective-permute-start(bf16[2,64,32,128]{3,2,1,0:T(8,128)(2,1)S(1)} %collective-permute-done.8.refs_8_), channel_id=1, source_target_pairs={{0,1},{1,0},{2,3},{3,2},{4,5},{5,4},{6,7},{7,6},{8,9},{9,8},{10,11... | collective-permute-start | bytes 3145736 | tf_op jit(solution)/shard_map/ppermute | solution.py:319
  98.7 17.4 %collective-permute-start.13 = (bf16[2,64,32,128]{3,2,1,0:T(8,128)(2,1)S(1)}, bf16[2,64,32,128]{3,2,1,0:T(8,128)(2,1)S(1)}, u32[]{:S(2)}, u32[]{:S(2)}) collective-permute-start(bf16[2,64,32,128]{3,2,1,0:T(8,128)(2,1)S(1)} %collective-permute-done.6.refs_7_), channel_id=1, source_target_pairs={{0,1},{1,0},{2,3},{3,2},{4,5},{5,4},{6,7},{7,6},{8,9},{9,8},{10,11... | collective-permute-start | bytes 3145736 | tf_op jit(solution)/shard_map/ppermute | solution.py:319
  101.4 14.6 %collective-permute-start.15 = (bf16[2,64,16,128]{3,2,1,0:T(8,128)(2,1)S(1)}, bf16[2,64,16,128]{3,2,1,0:T(8,128)(2,1)S(1)}, u32[]{:S(2)}, u32[]{:S(2)}) collective-permute-start(bf16[2,64,16,128]{3,2,1,0:T(8,128)(2,1)S(1)} %collective-permute-done.10.refs_9_), channel_id=1, source_target_pairs={{0,1},{1,0},{2,3},{3,2},{4,5},{5,4},{6,7},{7,6},{8,9},{9,8},{10,11... | collective-permute-start | bytes 1572872 | tf_op jit(solution)/shard_map/ppermute | solution.py:319

commit v6 on v5

--- a/solution.py
+++ b/solution.py
@@ -82,10 +82,8 @@
             re, im = spectra[:bins], spectra[bins:]
             power = re * re + im * im
             first = power.astype(jnp.bfloat16)
-            rest = power - first.astype(jnp.float32)
-            second = rest.astype(jnp.bfloat16)
-            third = (rest - second.astype(jnp.float32)).astype(jnp.bfloat16)
-            pieces = jnp.concatenate([first, second, third], axis=0)
+            second = (power - first.astype(jnp.float32)).astype(jnp.bfloat16)
+            pieces = jnp.concatenate([first, second], axis=0)
             band_sum = jnp.dot(band, pieces, preferred_element_type=jnp.float32)
             for n, w in enumerate(group):
                 part = slice(n * channels, (n + 1) * channels)
@@ -268,7 +266,7 @@
     table = (np.concatenate([np.cos(phase), -np.sin(phase)], axis=0) / math.sqrt(samples)).astype(ml_dtypes.bfloat16)
     same = bands[:, None] == bands[None, :]
     size = jnp.sum(same.astype(jnp.float32), axis=1, keepdims=True)
-    band = jnp.tile(same.astype(jnp.bfloat16), (1, 3))
+    band = jnp.tile(same.astype(jnp.bfloat16), (1, 2))
     bandinv = jnp.broadcast_to(1.0 / size, (bins, channels))
     return [jnp.asarray(ram), jnp.asarray(raminv), jnp.asarray(table), band, bandinv]
 

time: 129 us -> 129 us (level)
  transfers between devices with their start and end apart: 19 -> 19, of which waited for: 5 -> 5; matrix products, arithmetic and copies ran while one was open for 2% -> 2% of each run, Pallas kernels for 18% -> 17%
where the time goes in v6:
time: 129 us
  starting transfers between devices  75 us (58%)
  Pallas kernels  26.5 us (21%)
  waiting for transfers between devices  21.9 us (17%)
  local copies, waits for them, and re-layouts  4.51 us (3%)
    ppermute x5, starting transfers between devices, per_device(): other.append(lax.ppermute(held[n], 'blk', swap))  31.7 us
    ppermute x1, starting transfers between devices, per_device(): token = lax.ppermute(held[TOKEN][0, 0, :STEP], 'blk', swap)  16.6 us
    ppermute x4, waiting for transfers between devices, per_device(): far.append(lax.ppermute(mine, 'blk', second_pairs))  16.5 us
    ppermute x4, starting transfers between devices, per_device(): far.append(lax.ppermute(mine, 'blk', second_pairs))  12.9 us
    pallas_call x5, Pallas kernels, prepare(): pl.pallas_call(functools.partial(prepare_kernel, first, [start for _, sta...  10.9 us
    pallas_call x4, Pallas kernels, correlate_chunk(): pl.pallas_call(functools.partial(correlate_chunk_kernel, len(own), 1.0 /...  7.75 us
    pallas_call x1, Pallas kernels, correlate(): pl.pallas_call(functools.partial(correlate_kernel, len(own), 1.0 / math.s...  5.63 us
    ppermute x1, waiting for transfers between devices, per_device(): across_rest = lax.ppermute(outer_rest, 'blk', cross)  4.95 us
  transfers between devices with their start and end apart: 19, of which 5 were waited for; matrix products, arithmetic and copies ran while one was open for 2% of the time, Pallas kernels for 17%

profile of v6, /device:TPU:1, one launch (start us, length us, event | category | flops | bytes accessed | tf_op | source)
XLA Modules:
  0.0 128.8 jit_solution(696096927292321596)
XLA Ops:
  0.0 2.3 %borders.1 = (bf16[16,64,128]{2,1,0:T(8,128)(2,1)}, bf16[16,80,128]{2,1,0:T(8,128)(2,1)}, bf16[16,144,128]{2,1,0:T(8,128)(2,1)}) custom-call(bf16[128,144,128]{2,1,0:T(8,128)(2,1)} %x_ref.9), custom_call_target="tpu_custom_call" | custom-call | flops 1 | bytes 1 | tf_op jit(solution)/shard_map/borders/pallas_call | solution.py:116
  2.3 4.5 %collective-permute-start = (bf16[16,64,128]{2,1,0:T(8,128)(2,1)}, bf16[16,64,128]{2,1,0:T(8,128)(2,1)S(1)}, u32[]{:S(2)}, u32[]{:S(2)}) collective-permute-start(bf16[16,64,128]{2,1,0:T(8,128)(2,1)} %get-tuple-element.32), channel_id=1, source_target_pairs={{1,2},{3,4},{5,6},{7,8},{9,10},{11,12},{13,14},{15,16},{17,18},{19... | collective-permute-start | bytes 786440 | tf_op jit(solution)/shard_map/ppermute | solution.py:287
  6.8 1.3 %collective-permute-start.3 = (bf16[16,64,128]{2,1,0:T(8,128)(2,1)}, bf16[16,64,128]{2,1,0:T(8,128)(2,1)S(1)}, u32[]{:S(2)}, u32[]{:S(2)}) collective-permute-start(bf16[16,64,128]{2,1,0:T(8,128)(2,1)} %get-tuple-element.32), channel_id=1, source_target_pairs={{2,1},{4,3},{6,5},{8,7},{10,9},{12,11},{14,13},{16,15},{18,17},{20... | collective-permute-start | bytes 786440 | tf_op jit(solution)/shard_map/ppermute | solution.py:286
  8.1 0.1 collective-permute-start.2
  8.2 4.3 %collective-permute-start.1 = (bf16[16,80,128]{2,1,0:T(8,128)(2,1)}, bf16[16,80,128]{2,1,0:T(8,128)(2,1)S(1)}, u32[]{:S(2)}, u32[]{:S(2)}) collective-permute-start(bf16[16,80,128]{2,1,0:T(8,128)(2,1)} %get-tuple-element.33), channel_id=1, source_target_pairs={{1,2},{2,1},{3,4},{4,3},{5,6},{6,5},{7,8},{8,7},{9,10},{10,9},{11,... | collective-permute-start | bytes 983048 | tf_op jit(solution)/shard_map/ppermute | solution.py:289
  12.5 0.1 compare_convert_fusion.1
  12.6 0.2 fusion
  12.8 0.0 copy-start.1
  12.8 0.0 copy-start.2
  12.8 0.0 copy-start.3
  12.9 1.3 %slice.66.x_ref = bf16[128,32,128]{2,1,0:T(8,128)(2,1)S(1)} slice(bf16[128,144,128]{2,1,0:T(8,128)(2,1)} %x_ref.9), slice={[0:128], [0:32], [0:128]} | slice | bytes 2097152 | tf_op jit(solution)/shard_map/slice | solution.py:303
  14.2 0.1 tile.10.band_ref
  14.3 0.4 collective-permute-done.3.hi_odd
  14.8 0.1 broadcast_in_dim.4.inv_ref
  14.9 0.1 broadcast_in_dim.5.bandinv_ref
  15.0 2.4 %prepare.5.refs_0_ = bf16[2,64,32,128]{3,2,1,0:T(8,128)(2,1)S(1)} custom-call(bf16[128,32,128]{2,1,0:T(8,128)(2,1)S(1)} %slice.66.x_ref, bf16[16,64,128]{2,1,0:T(8,128)(2,1)S(1)} %collective-permute-done.lo_even, bf16[16,144,128]{2,1,0:T(8,128)(2,1)S(1)} %collective-permute-done.2.lo_odd.hi_even, ...), custom_call_target="tpu_custom_call" | custom-call | flops 1 | bytes 1 | tf_op jit(solution)/shard_map/prepare/pallas_call | solution.py:132
  17.3 0.7 collective-permute-start.4
  18.1 4.9 %collective-permute-done.1.lo_even.hi_odd = bf16[16,80,128]{2,1,0:T(8,128)(2,1)S(1)} collective-permute-done((bf16[16,80,128]{2,1,0:T(8,128)(2,1)}, bf16[16,80,128]{2,1,0:T(8,128)(2,1)S(1)}, u32[]{:S(2)}, u32[]{:S(2)}) %collective-permute-start.1) | collective-permute-done | bytes 327712 | tf_op jit(solution)/shard_map/ppermute | solution.py:289
  23.0 2.3 %copy-done = bf16[128,144,128]{2,1,0:T(8,128)(2,1)S(1)} copy-done((bf16[128,144,128]{2,1,0:T(8,128)(2,1)S(1)}, bf16[128,144,128]{2,1,0:T(8,128)(2,1)}, u32[]{:S(2)}) %copy-start) | copy-done | bytes 4718616
  25.4 2.4 %prepare.6.refs_1_ = bf16[2,64,32,128]{3,2,1,0:T(8,128)(2,1)S(1)} custom-call(bf16[128,144,128]{2,1,0:T(8,128)(2,1)S(1)} %copy-done, bf16[16,64,128]{2,1,0:T(8,128)(2,1)S(1)} %collective-permute-done.lo_even, bf16[16,144,128]{2,1,0:T(8,128)(2,1)S(1)} %collective-permute-done.2.lo_odd.hi_even, ...), custom_call_target="tpu_custom_call" | custom-call | flops 1 | bytes 1 | tf_op jit(solution)/shard_map/prepare/pallas_call | solution.py:132
  27.7 0.7 collective-permute-start.5
  28.5 2.4 %prepare.7.refs_2_ = bf16[2,64,32,128]{3,2,1,0:T(8,128)(2,1)S(1)} custom-call(bf16[128,144,128]{2,1,0:T(8,128)(2,1)S(1)} %copy-done, bf16[16,80,128]{2,1,0:T(8,128)(2,1)S(1)} %collective-permute-done.1.lo_even.hi_odd, bf16[16,144,128]{2,1,0:T(8,128)(2,1)S(1)} %collective-permute-done.2.lo_odd.hi_even, ...), custom_call_target="tpu_custom_call" | custom-call | flops 1 | bytes 1 | tf_op jit(solution)/shard_map/prepare/pallas_call | solution.py:132
  30.8 0.7 collective-permute-start.6
  31.6 0.1 slice_dynamic-update-slice_fusion.3
  31.7 16.6 %collective-permute-start.11 = (bf16[16,128]{1,0:T(8,128)(2,1)S(1)}, bf16[16,128]{1,0:T(8,128)(2,1)S(1)}, u32[]{:S(2)}, u32[]{:S(2)}) collective-permute-start(bf16[16,128]{1,0:T(8,128)(2,1)S(1)} %slice_bitcast_fusion), channel_id=1, source_target_pairs={{0,1},{1,0},{2,3},{3,2},{4,5},{5,4},{6,7},{7,6},{8,9},{9,8},{10,11... | collective-permute-start | bytes 12296 | tf_op jit(solution)/shard_map/ppermute | solution.py:307
  48.3 2.4 %prepare.8.refs_3_ = bf16[2,64,32,128]{3,2,1,0:T(8,128)(2,1)S(1)} custom-call(bf16[128,144,128]{2,1,0:T(8,128)(2,1)S(1)} %copy-done, bf16[16,80,128]{2,1,0:T(8,128)(2,1)S(1)} %collective-permute-done.1.lo_even.hi_odd, bf16[16,144,128]{2,1,0:T(8,128)(2,1)S(1)} %collective-permute-done.2.lo_odd.hi_even, ...), custom_call_target="tpu_custom_call" | custom-call | flops 1 | bytes 1 | tf_op jit(solution)/shard_map/prepare/pallas_call | solution.py:132
  50.6 0.7 collective-permute-start.8
  51.4 7.3 %collective-permute-start.9 = (bf16[2,64,32,128]{3,2,1,0:T(8,128)(2,1)S(1)}, bf16[2,64,32,128]{3,2,1,0:T(8,128)(2,1)S(1)}, u32[]{:S(2)}, u32[]{:S(2)}) collective-permute-start(bf16[2,64,32,128]{3,2,1,0:T(8,128)(2,1)S(1)} %collective-permute-done.5.refs_6_), channel_id=1, source_target_pairs={{0,1},{1,0},{2,3},{3,2},{4,5},{5,4},{6,7},{7,6},{8,9},{9,8},{10,11... | collective-permute-start | bytes 3145736 | tf_op jit(solution)/shard_map/ppermute | solution.py:317
  58.7 0.1 slice_dynamic-update-slice_fusion.2
  58.9 0.1 slice_dynamic-update-slice_fusion.1
  59.0 1.4 %prepare.9.refs_4_ = bf16[2,64,16,128]{3,2,1,0:T(8,128)(2,1)S(1)} custom-call(bf16[128,144,128]{2,1,0:T(8,128)(2,1)S(1)} %copy-done, bf16[16,80,128]{2,1,0:T(8,128)(2,1)S(1)} %collective-permute-done.1.lo_even.hi_odd, bf16[16,144,128]{2,1,0:T(8,128)(2,1)S(1)} %collective-permute-done.2.lo_odd.hi_even, ...), custom_call_target="tpu_custom_call" | custom-call | flops 1 | bytes 1 | tf_op jit(solution)/shard_map/prepare/pallas_call | solution.py:132
  60.4 0.1 slice_dynamic-update-slice_fusion
  60.6 0.1 slice_dynamic-update-slice_fusion.16
  60.6 1.9 %collective-permute-start.18 = (bf16[2,16,144,128]{3,2,1,0:T(8,128)(2,1)S(1)}, bf16[2,16,144,128]{3,2,1,0:T(8,128)(2,1)S(1)}, u32[]{:S(2)}, u32[]{:S(2)}) collective-permute-start(bf16[2,16,144,128]{3,2,1,0:T(8,128)(2,1)S(1)} %get-tuple-element.57), channel_id=1, source_target_pairs={{3,1},{5,3},{7,5},{9,7},{11,9},{13,11},{15,13},{17,15},{19,17},{21... | collective-permute-start | bytes 3538952 | tf_op jit(solution)/shard_map/ppermute | solution.py:312
  62.6 0.1 collective-permute-start.7
  62.7 7.2 %collective-permute-start.17 = (bf16[2,16,144,128]{3,2,1,0:T(8,128)(2,1)S(1)}, bf16[2,16,144,128]{3,2,1,0:T(8,128)(2,1)S(1)}, u32[]{:S(2)}, u32[]{:S(2)}) collective-permute-start(bf16[2,16,144,128]{3,2,1,0:T(8,128)(2,1)S(1)} %get-tuple-element.56), channel_id=1, source_target_pairs={{3,1},{5,3},{7,5},{9,7},{11,9},{13,11},{15,13},{17,15},{19,17},{21... | collective-permute-start | bytes 3538952 | tf_op jit(solution)/shard_map/ppermute | solution.py:312
  69.8 0.7 collective-permute-start.10
  70.6 1.9 %collective-permute-start.16 = (bf16[2,16,144,128]{3,2,1,0:T(8,128)(2,1)S(1)}, bf16[2,16,144,128]{3,2,1,0:T(8,128)(2,1)S(1)}, u32[]{:S(2)}, u32[]{:S(2)}) collective-permute-start(bf16[2,16,144,128]{3,2,1,0:T(8,128)(2,1)S(1)} %get-tuple-element.55), channel_id=1, source_target_pairs={{3,1},{5,3},{7,5},{9,7},{11,9},{13,11},{15,13},{17,15},{19,17},{21... | collective-permute-start | bytes 3538952 | tf_op jit(solution)/shard_map/ppermute | solution.py:312
  72.5 1.9 %collective-permute-start.12 = (bf16[2,16,144,128]{3,2,1,0:T(8,128)(2,1)S(1)}, bf16[2,16,144,128]{3,2,1,0:T(8,128)(2,1)S(1)}, u32[]{:S(2)}, u32[]{:S(2)}) collective-permute-start(bf16[2,16,144,128]{3,2,1,0:T(8,128)(2,1)S(1)} %get-tuple-element.52), channel_id=1, source_target_pairs={{3,1},{5,3},{7,5},{9,7},{11,9},{13,11},{15,13},{17,15},{19,17},{21... | collective-permute-start | bytes 3538952 | tf_op jit(solution)/shard_map/ppermute | solution.py:312
  74.4 24.3 %collective-permute-start.14 = (bf16[2,64,32,128]{3,2,1,0:T(8,128)(2,1)S(1)}, bf16[2,64,32,128]{3,2,1,0:T(8,128)(2,1)S(1)}, u32[]{:S(2)}, u32[]{:S(2)}) collective-permute-start(bf16[2,64,32,128]{3,2,1,0:T(8,128)(2,1)S(1)} %collective-permute-done.8.refs_8_), channel_id=1, source_target_pairs={{0,1},{1,0},{2,3},{3,2},{4,5},{5,4},{6,7},{7,6},{8,9},{9,8},{10,11... | collective-permute-start | bytes 3145736 | tf_op jit(solution)/shard_map/ppermute | solution.py:317
  98.7 2.7 %collective-permute-done.17.refs_10_ = bf16[2,16,144,128]{3,2,1,0:T(8,128)(2,1)S(1)} collective-permute-done((bf16[2,16,144,128]{3,2,1,0:T(8,128)(2,1)S(1)}, bf16[2,16,144,128]{3,2,1,0:T(8,128)(2,1)S(1)}, u32[]{:S(2)}, u32[]{:S(2)}) %collective-permute-start.17) | collective-permute-done | bytes 1179680 | tf_op jit(solution)/shard_map/ppermute | solution.py:312
  101.4 1.9 %correlate_chunk.4.refs_11_ = bf16[128,2,2,64,128]{4,3,2,1,0:T(8,128)(2,1)} custom-call(bf16[2,64,32,128]{3,2,1,0:T(8,128)(2,1)S(1)} %prepare.5.refs_0_, bf16[2,64,32,128]{3,2,1,0:T(8,128)(2,1)S(1)} %prepare.6.refs_1_, bf16[2,64,32,128]{3,2,1,0:T(8,128)(2,1)S(1)} %prepare.7.refs_2_, bf16[2,64,32,128]{3,2,1,0:T(8,128)(2,1)S(1)} %prepare.8.refs_3_, ...), custom_call_target="tpu_custom_call" | custom-call | flops 1 | bytes 1 | tf_op jit(solution)/shard_map/correlate_chunk/pallas_call | solution.py:228
  103.4 2.0 %correlate_chunk.5.refs_11_ = bf16[128,2,2,64,128]{4,3,2,1,0:T(8,128)(2,1)} custom-call(bf16[2,64,32,128]{3,2,1,0:T(8,128)(2,1)S(1)} %prepare.5.refs_0_, bf16[2,64,32,128]{3,2,1,0:T(8,128)(2,1)S(1)} %prepare.6.refs_1_, bf16[2,64,32,128]{3,2,1,0:T(8,128)(2,1)S(1)} %prepare.7.refs_2_, ...), custom_call_target="tpu_custom_call", output_to_operand_aliasing={{}: (11, {})} | custom-call | flops 1 | bytes 1 | tf_op jit(solution)/shard_map/correlate_chunk/pallas_call | solution.py:228
  105.3 8.7 %collective-permute-done.16.refs_10_ = bf16[2,16,144,128]{3,2,1,0:T(8,128)(2,1)S(1)} collective-permute-done((bf16[2,16,144,128]{3,2,1,0:T(8,128)(2,1)S(1)}, bf16[2,16,144,128]{3,2,1,0:T(8,128)(2,1)S(1)}, u32[]{:S(2)}, u32[]{:S(2)}) %collective-permute-start.16) | collective-permute-done | bytes 1179680 | tf_op jit(solution)/shard_map/ppermute | solution.py:312
  114.1 1.9 %correlate_chunk.6.refs_10_ = bf16[128,2,2,64,128]{4,3,2,1,0:T(8,128)(2,1)} custom-call(bf16[2,64,32,128]{3,2,1,0:T(8,128)(2,1)S(1)} %prepare.5.refs_0_, bf16[2,64,32,128]{3,2,1,0:T(8,128)(2,1)S(1)} %prepare.6.refs_1_, bf16[2,64,32,128]{3,2,1,0:T(8,128)(2,1)S(1)} %prepare.7.refs_2_, ...), custom_call_target="tpu_custom_call", output_to_operand_aliasing={{}: (11, {})} | custom-call | flops 1 | bytes 1 | tf_op jit(solution)/shard_map/correlate_chunk/pallas_call | solution.py:228
  116.0 5.6 %correlate.1.refs_11_ = bf16[128,2,2,64,128]{4,3,2,1,0:T(8,128)(2,1)} custom-call(bf16[2,64,32,128]{3,2,1,0:T(8,128)(2,1)S(1)} %prepare.5.refs_0_, bf16[2,64,32,128]{3,2,1,0:T(8,128)(2,1)S(1)} %prepare.6.refs_1_, bf16[2,64,32,128]{3,2,1,0:T(8,128)(2,1)S(1)} %prepare.7.refs_2_, ...), custom_call_target="tpu_custom_call", output_to_operand_aliasing={{}: (10, {})} | custom-call | flops 1 | bytes 1 | tf_op jit(solution)/shard_map/correlate/pallas_call | solution.py:182
  121.7 5.0 %collective-permute-done.12.refs_10_ = bf16[2,16,144,128]{3,2,1,0:T(8,128)(2,1)S(1)} collective-permute-done((bf16[2,16,144,128]{3,2,1,0:T(8,128)(2,1)S(1)}, bf16[2,16,144,128]{3,2,1,0:T(8,128)(2,1)S(1)}, u32[]{:S(2)}, u32[]{:S(2)}) %collective-permute-start.12) | collective-permute-done | bytes 1179680 | tf_op jit(solution)/shard_map/ppermute | solution.py:312
  126.7 1.9 %correlate_chunk.7 = bf16[128,2,2,64,128]{4,3,2,1,0:T(8,128)(2,1)} custom-call(bf16[2,64,32,128]{3,2,1,0:T(8,128)(2,1)S(1)} %prepare.5.refs_0_, bf16[2,64,32,128]{3,2,1,0:T(8,128)(2,1)S(1)} %prepare.6.refs_1_, bf16[2,64,32,128]{3,2,1,0:T(8,128)(2,1)S(1)} %prepare.7.refs_2_, ...), custom_call_target="tpu_custom_call", output_to_operand_aliasing={{}: (11, {})} | custom-call | flops 1 | bytes 1 | tf_op jit(solution)/shard_map/correlate_chunk/pallas_call | solution.py:228
  (30 shorter events, 0.1 us)
Async XLA Ops:
  0.0 12.8 %copy-start.4 = (pred[128,160]{1,0:T(32,128)(4,1)S(1)}, pred[128,160]{1,0:T(32,128)(4,1)}, u32[]{:S(2)}) copy-start(pred[128,160]{1,0:T(32,128)(4,1)} %constant.36.clone) | copy-start | bytes 61444
  0.0 12.5 %copy-start.5 = (s32[64]{0:T(128)S(1)}, s32[64]{0:T(128)}, u32[]{:S(2)}) copy-start(s32[64]{0:T(128)} %param.9) | copy-start | bytes 772
  2.3 12.0 %collective-permute-start = (bf16[16,64,128]{2,1,0:T(8,128)(2,1)}, bf16[16,64,128]{2,1,0:T(8,128)(2,1)S(1)}, u32[]{:S(2)}, u32[]{:S(2)}) collective-permute-start(bf16[16,64,128]{2,1,0:T(8,128)(2,1)} %get-tuple-element.32), channel_id=1, source_target_pairs={{1,2},{3,4},{5,6},{7,8},{9,10},{11,12},{13,14},{15,16},{17,18},{19... | collective-permute-start | bytes 786440 | tf_op jit(solution)/shard_map/ppermute | solution.py:287
  6.8 8.0 %collective-permute-start.3 = (bf16[16,64,128]{2,1,0:T(8,128)(2,1)}, bf16[16,64,128]{2,1,0:T(8,128)(2,1)S(1)}, u32[]{:S(2)}, u32[]{:S(2)}) collective-permute-start(bf16[16,64,128]{2,1,0:T(8,128)(2,1)} %get-tuple-element.32), channel_id=1, source_target_pairs={{2,1},{4,3},{6,5},{8,7},{10,9},{12,11},{14,13},{16,15},{18,17},{20... | collective-permute-start | bytes 786440 | tf_op jit(solution)/shard_map/ppermute | solution.py:286
  8.1 6.7 %collective-permute-start.2 = (bf16[16,144,128]{2,1,0:T(8,128)(2,1)}, bf16[16,144,128]{2,1,0:T(8,128)(2,1)S(1)}, u32[]{:S(2)}, u32[]{:S(2)}) collective-permute-start(bf16[16,144,128]{2,1,0:T(8,128)(2,1)} %get-tuple-element.34), channel_id=1, source_target_pairs={{0,1},{1,0},{2,3},{3,2},{4,5},{5,4},{6,7},{7,6},{8,9},{9,8},{10,11... | collective-permute-start | bytes 1769480 | tf_op jit(solution)/shard_map/ppermute | solution.py:288
  8.2 14.8 %collective-permute-start.1 = (bf16[16,80,128]{2,1,0:T(8,128)(2,1)}, bf16[16,80,128]{2,1,0:T(8,128)(2,1)S(1)}, u32[]{:S(2)}, u32[]{:S(2)}) collective-permute-start(bf16[16,80,128]{2,1,0:T(8,128)(2,1)} %get-tuple-element.33), channel_id=1, source_target_pairs={{1,2},{2,1},{3,4},{4,3},{5,6},{6,5},{7,8},{8,7},{9,10},{10,9},{11,... | collective-permute-start | bytes 983048 | tf_op jit(solution)/shard_map/ppermute | solution.py:289
  12.8 2.1 %copy-start.1 = (bf16[128,128]{1,0:T(8,128)(2,1)S(1)}, bf16[128,128]{1,0:T(8,128)(2,1)}, u32[]{:S(2)}) copy-start(bf16[128,128]{1,0:T(8,128)(2,1)} %constant.37.clone.ram_ref) | copy-start | bytes 98308
  12.8 2.1 %copy-start.2 = (bf16[128,128]{1,0:T(8,128)(2,1)S(1)}, bf16[128,128]{1,0:T(8,128)(2,1)}, u32[]{:S(2)}) copy-start(bf16[128,128]{1,0:T(8,128)(2,1)} %constant.39.clone.table_ref) | copy-start | bytes 98308
  12.8 2.1 %copy-start.3 = (f32[1,128]{1,0:T(1,128)S(1)}, f32[1,128]{1,0:T(1,128)}, u32[]{:S(2)}) copy-start(f32[1,128]{1,0:T(1,128)} %constant.38.clone.raminv_ref) | copy-start | bytes 1540
  17.3 11.1 %collective-permute-start.4 = (bf16[2,64,32,128]{3,2,1,0:T(8,128)(2,1)S(1)}, bf16[2,64,32,128]{3,2,1,0:T(8,128)(2,1)S(1)}, u32[]{:S(2)}, u32[]{:S(2)}) collective-permute-start(bf16[2,64,32,128]{3,2,1,0:T(8,128)(2,1)S(1)} %prepare.5.refs_0_), channel_id=1, source_target_pairs={{2,0},{1,1},{4,2},{3,3},{6,4},{5,5},{8,6},{7,7},{10,8},{9,9},{12,1... | collective-permute-start | bytes 3145736 | tf_op jit(solution)/shard_map/ppermute | solution.py:305
  23.0 2.3 %copy-start = (bf16[128,144,128]{2,1,0:T(8,128)(2,1)S(1)}, bf16[128,144,128]{2,1,0:T(8,128)(2,1)}, u32[]{:S(2)}) copy-start(bf16[128,144,128]{2,1,0:T(8,128)(2,1)} %x_ref.9) | copy-start | bytes 14155780
  27.7 3.9 %collective-permute-start.5 = (bf16[2,64,32,128]{3,2,1,0:T(8,128)(2,1)S(1)}, bf16[2,64,32,128]{3,2,1,0:T(8,128)(2,1)S(1)}, u32[]{:S(2)}, u32[]{:S(2)}) collective-permute-start(bf16[2,64,32,128]{3,2,1,0:T(8,128)(2,1)S(1)} %prepare.6.refs_1_), channel_id=1, source_target_pairs={{2,0},{1,1},{4,2},{3,3},{6,4},{5,5},{8,6},{7,7},{10,8},{9,9},{12,1... | collective-permute-start | bytes 3145736 | tf_op jit(solution)/shard_map/ppermute | solution.py:305
  30.8 28.2 %collective-permute-start.6 = (bf16[2,64,32,128]{3,2,1,0:T(8,128)(2,1)S(1)}, bf16[2,64,32,128]{3,2,1,0:T(8,128)(2,1)S(1)}, u32[]{:S(2)}, u32[]{:S(2)}) collective-permute-start(bf16[2,64,32,128]{3,2,1,0:T(8,128)(2,1)S(1)} %prepare.7.refs_2_), channel_id=1, source_target_pairs={{2,0},{1,1},{4,2},{3,3},{6,4},{5,5},{8,6},{7,7},{10,8},{9,9},{12,1... | collective-permute-start | bytes 3145736 | tf_op jit(solution)/shard_map/ppermute | solution.py:305
  31.7 29.0 %collective-permute-start.11 = (bf16[16,128]{1,0:T(8,128)(2,1)S(1)}, bf16[16,128]{1,0:T(8,128)(2,1)S(1)}, u32[]{:S(2)}, u32[]{:S(2)}) collective-permute-start(bf16[16,128]{1,0:T(8,128)(2,1)S(1)} %slice_bitcast_fusion), channel_id=1, source_target_pairs={{0,1},{1,0},{2,3},{3,2},{4,5},{5,4},{6,7},{7,6},{8,9},{9,8},{10,11... | collective-permute-start | bytes 12296 | tf_op jit(solution)/shard_map/ppermute | solution.py:307
  50.6 19.2 %collective-permute-start.8 = (bf16[2,64,32,128]{3,2,1,0:T(8,128)(2,1)S(1)}, bf16[2,64,32,128]{3,2,1,0:T(8,128)(2,1)S(1)}, u32[]{:S(2)}, u32[]{:S(2)}) collective-permute-start(bf16[2,64,32,128]{3,2,1,0:T(8,128)(2,1)S(1)} %prepare.8.refs_3_), channel_id=1, source_target_pairs={{2,0},{1,1},{4,2},{3,3},{6,4},{5,5},{8,6},{7,7},{10,8},{9,9},{12,1... | collective-permute-start | bytes 3145736 | tf_op jit(solution)/shard_map/ppermute | solution.py:305
  51.4 19.2 %collective-permute-start.9 = (bf16[2,64,32,128]{3,2,1,0:T(8,128)(2,1)S(1)}, bf16[2,64,32,128]{3,2,1,0:T(8,128)(2,1)S(1)}, u32[]{:S(2)}, u32[]{:S(2)}) collective-permute-start(bf16[2,64,32,128]{3,2,1,0:T(8,128)(2,1)S(1)} %collective-permute-done.5.refs_6_), channel_id=1, source_target_pairs={{0,1},{1,0},{2,3},{3,2},{4,5},{5,4},{6,7},{7,6},{8,9},{9,8},{10,11... | collective-permute-start | bytes 3145736 | tf_op jit(solution)/shard_map/ppermute | solution.py:317
  60.6 38.0 %collective-permute-start.18 = (bf16[2,16,144,128]{3,2,1,0:T(8,128)(2,1)S(1)}, bf16[2,16,144,128]{3,2,1,0:T(8,128)(2,1)S(1)}, u32[]{:S(2)}, u32[]{:S(2)}) collective-permute-start(bf16[2,16,144,128]{3,2,1,0:T(8,128)(2,1)S(1)} %get-tuple-element.57), channel_id=1, source_target_pairs={{3,1},{5,3},{7,5},{9,7},{11,9},{13,11},{15,13},{17,15},{19,17},{21... | collective-permute-start | bytes 3538952 | tf_op jit(solution)/shard_map/ppermute | solution.py:312
  62.6 9.9 %collective-permute-start.7 = (bf16[2,64,32,128]{3,2,1,0:T(8,128)(2,1)S(1)}, bf16[2,64,32,128]{3,2,1,0:T(8,128)(2,1)S(1)}, u32[]{:S(2)}, u32[]{:S(2)}) collective-permute-start(bf16[2,64,32,128]{3,2,1,0:T(8,128)(2,1)S(1)} %collective-permute-done.4.refs_5_), channel_id=1, source_target_pairs={{0,1},{1,0},{2,3},{3,2},{4,5},{5,4},{6,7},{7,6},{8,9},{9,8},{10,11... | collective-permute-start | bytes 3145736 | tf_op jit(solution)/shard_map/ppermute | solution.py:317
  62.7 38.8 %collective-permute-start.17 = (bf16[2,16,144,128]{3,2,1,0:T(8,128)(2,1)S(1)}, bf16[2,16,144,128]{3,2,1,0:T(8,128)(2,1)S(1)}, u32[]{:S(2)}, u32[]{:S(2)}) collective-permute-start(bf16[2,16,144,128]{3,2,1,0:T(8,128)(2,1)S(1)} %get-tuple-element.56), channel_id=1, source_target_pairs={{3,1},{5,3},{7,5},{9,7},{11,9},{13,11},{15,13},{17,15},{19,17},{21... | collective-permute-start | bytes 3538952 | tf_op jit(solution)/shard_map/ppermute | solution.py:312
  69.8 4.6 %collective-permute-start.10 = (bf16[2,64,16,128]{3,2,1,0:T(8,128)(2,1)S(1)}, bf16[2,64,16,128]{3,2,1,0:T(8,128)(2,1)S(1)}, u32[]{:S(2)}, u32[]{:S(2)}) collective-permute-start(bf16[2,64,16,128]{3,2,1,0:T(8,128)(2,1)S(1)} %prepare.9.refs_4_), channel_id=1, source_target_pairs={{2,0},{1,1},{4,2},{3,3},{6,4},{5,5},{8,6},{7,7},{10,8},{9,9},{12,1... | collective-permute-start | bytes 1572872 | tf_op jit(solution)/shard_map/ppermute | solution.py:305
  70.6 43.5 %collective-permute-start.16 = (bf16[2,16,144,128]{3,2,1,0:T(8,128)(2,1)S(1)}, bf16[2,16,144,128]{3,2,1,0:T(8,128)(2,1)S(1)}, u32[]{:S(2)}, u32[]{:S(2)}) collective-permute-start(bf16[2,16,144,128]{3,2,1,0:T(8,128)(2,1)S(1)} %get-tuple-element.55), channel_id=1, source_target_pairs={{3,1},{5,3},{7,5},{9,7},{11,9},{13,11},{15,13},{17,15},{19,17},{21... | collective-permute-start | bytes 3538952 | tf_op jit(solution)/shard_map/ppermute | solution.py:312
  72.5 54.2 %collective-permute-start.12 = (bf16[2,16,144,128]{3,2,1,0:T(8,128)(2,1)S(1)}, bf16[2,16,144,128]{3,2,1,0:T(8,128)(2,1)S(1)}, u32[]{:S(2)}, u32[]{:S(2)}) collective-permute-start(bf16[2,16,144,128]{3,2,1,0:T(8,128)(2,1)S(1)} %get-tuple-element.52), channel_id=1, source_target_pairs={{3,1},{5,3},{7,5},{9,7},{11,9},{13,11},{15,13},{17,15},{19,17},{21... | collective-permute-start | bytes 3538952 | tf_op jit(solution)/shard_map/ppermute | solution.py:312
  74.4 41.6 %collective-permute-start.14 = (bf16[2,64,32,128]{3,2,1,0:T(8,128)(2,1)S(1)}, bf16[2,64,32,128]{3,2,1,0:T(8,128)(2,1)S(1)}, u32[]{:S(2)}, u32[]{:S(2)}) collective-permute-start(bf16[2,64,32,128]{3,2,1,0:T(8,128)(2,1)S(1)} %collective-permute-done.8.refs_8_), channel_id=1, source_target_pairs={{0,1},{1,0},{2,3},{3,2},{4,5},{5,4},{6,7},{7,6},{8,9},{9,8},{10,11... | collective-permute-start | bytes 3145736 | tf_op jit(solution)/shard_map/ppermute | solution.py:317
  98.7 17.3 %collective-permute-start.13 = (bf16[2,64,32,128]{3,2,1,0:T(8,128)(2,1)S(1)}, bf16[2,64,32,128]{3,2,1,0:T(8,128)(2,1)S(1)}, u32[]{:S(2)}, u32[]{:S(2)}) collective-permute-start(bf16[2,64,32,128]{3,2,1,0:T(8,128)(2,1)S(1)} %collective-permute-done.6.refs_7_), channel_id=1, source_target_pairs={{0,1},{1,0},{2,3},{3,2},{4,5},{5,4},{6,7},{7,6},{8,9},{9,8},{10,11... | collective-permute-start | bytes 3145736 | tf_op jit(solution)/shard_map/ppermute | solution.py:317
  101.4 14.6 %collective-permute-start.15 = (bf16[2,64,16,128]{3,2,1,0:T(8,128)(2,1)S(1)}, bf16[2,64,16,128]{3,2,1,0:T(8,128)(2,1)S(1)}, u32[]{:S(2)}, u32[]{:S(2)}) collective-permute-start(bf16[2,64,16,128]{3,2,1,0:T(8,128)(2,1)S(1)} %collective-permute-done.10.refs_9_), channel_id=1, source_target_pairs={{0,1},{1,0},{2,3},{3,2},{4,5},{5,4},{6,7},{7,6},{8,9},{9,8},{10,11... | collective-permute-start | bytes 1572872 | tf_op jit(solution)/shard_map/ppermute | solution.py:317
